TPU v7x, 256 devices: a whole 4x4x8 slice. The times are simulated.
256 devices in a mesh: gz: 8 (over x, core), tile: 32 (over z, y).
Axes of the slice: x: 4, y: 4, z: 8, core: 2. Of those that a mesh axis runs over, the one named last changes fastest.
Arguments:
- patches: bfloat16 [8, 512, 25600], P('gz', 'tile'), may hold values from -450 to 450, as said below
- prior_patches: bfloat16 [512, 25600], P('tile'), may hold values from -450 to 450, as said below
- blocks: bfloat16 [8, 1024, 25600], P('gz', 'tile'), may hold values from -450 to 450, as said below
- dest: int32 [8, 1024, 1], P('gz', 'tile'), may hold values from 0 to 31; in each aligned block of 32 rows (0 to 31, 32 to 63, ..., all dimensions but the last counted through in order) at most 2 rows name the same one
- target: int32 [8, 1024], P('gz', 'tile'), may hold values from 0 to 15
- flows: float32 [8, 2, 256, 256], P('gz', None, 'tile'), may hold values from -8 to 8
- valid: int32 [8, 256, 256], P('gz', 'tile'), may hold values 0 or 1
- stiffness: float32 [8, 256, 256], P('gz', 'tile'), may hold values from 0.2 to 1
Outputs:
- corr_maps: bfloat16 [8, 1024, 25600], P('gz', 'tile')
- mesh_nodes: float32 [8, 2, 256, 256], P('gz', None, 'tile')
Inputs may be any that keep to these rules, and one draw needn't show every extreme that they name: `patches`: pixel intensities. `prior_patches`: pixel intensities. `blocks`: pixel intensities. `dest`: among the 32 blocks of one device, at most 2 name the same tile, and on every device some tile is named by exactly 2 of them.
All inputs are finite; a program needn't handle non-finite values. No bound on the sum of `valid` on one device may be relied on, other than what follows from the above.
Results may differ from a plain program's by a relative error of at most 0.015.
Values may be sent and summed in bfloat16 or wider, within the bound.
A program may use at most 128 MiB of HBM per device.

v0:
```python
import jax
import jax.numpy as jnp
from jax import lax
from jax.sharding import PartitionSpec as P

P_SIZE = 160
PIX = 25600
CAP = 2
ITERS = 64


def from_behind(value, axis, steps):
    count = lax.axis_size(axis)
    first, last = (max(0, -steps), min(count, count - steps))
    return lax.ppermute(value, axis, [(source, source + steps) for source in range(first, last)])


def with_halo(x, sides, width):
    for axis, dim in sides:
        devices, length = (lax.axis_size(axis), x.shape[dim])
        up = [(i, (i + 1) % devices) for i in range(devices - 1)]
        down = [(j, i) for i, j in up]
        last = lax.slice_in_dim(x, length - width, length, axis=dim)
        first = lax.slice_in_dim(x, 0, width, axis=dim)
        before = lax.ppermute(last, axis, up)
        after = lax.ppermute(first, axis, down)
        x = jnp.concatenate([before, x, after], axis=dim)
    return x


def dft_tables(edge_len):
    positions = jnp.arange(edge_len, dtype=jnp.int32)
    phase_idx = positions[:, None] * positions[None, :] % edge_len
    angles = phase_idx.astype(jnp.float32) * (2.0 * jnp.pi / edge_len)
    return (jnp.cos(angles).astype(jnp.bfloat16), jnp.sin(angles).astype(jnp.bfloat16))


def right_mul(pixels, matrix_t):
    return jnp.einsum("npq,qk->npk", pixels, matrix_t, preferred_element_type=jnp.float32)


def left_mul(matrix_t, pixels):
    return jnp.einsum("jp,npk->njk", matrix_t, pixels, preferred_element_type=jnp.float32)


def normalized(pixel_rows):
    values = pixel_rows.astype(jnp.float32)
    centred = values - jnp.mean(values, axis=-1, keepdims=True)
    spread = jnp.mean(centred * centred, axis=-1, keepdims=True)
    return (centred * lax.rsqrt(spread + 1e-05)).astype(jnp.bfloat16)


def spectrum(pixel_rows, cos_t, sin_t):
    edge_len = cos_t.shape[0]
    pixels = normalized(pixel_rows).reshape(pixel_rows.shape[0], edge_len, edge_len)
    first_re = right_mul(pixels, cos_t).astype(jnp.bfloat16)
    first_im = right_mul(pixels, sin_t).astype(jnp.bfloat16)
    spec_re = (left_mul(cos_t, first_re) - left_mul(sin_t, first_im)).astype(jnp.bfloat16)
    spec_im = (left_mul(sin_t, first_re) + left_mul(cos_t, first_im)).astype(jnp.bfloat16)
    return (spec_re, spec_im)


def correlate(spec_a, spec_b, cos_t, sin_t):
    edge_len = cos_t.shape[0]
    a_re = spec_a[0].astype(jnp.float32)
    a_im = spec_a[1].astype(jnp.float32)
    b_re = spec_b[0].astype(jnp.float32)
    b_im = spec_b[1].astype(jnp.float32)
    cross_re = (a_re * b_re + a_im * b_im).astype(jnp.bfloat16)
    cross_im = (a_im * b_re - a_re * b_im).astype(jnp.bfloat16)
    back_re = (right_mul(cross_re, cos_t) - right_mul(cross_im, sin_t)).astype(jnp.bfloat16)
    back_im = (right_mul(cross_re, sin_t) + right_mul(cross_im, cos_t)).astype(jnp.bfloat16)
    field_out = (left_mul(cos_t, back_re) - left_mul(sin_t, back_im)) * (1.0 / float(edge_len) ** 3)
    return field_out.astype(jnp.bfloat16).reshape(cross_re.shape[0], edge_len * edge_len)


def on_device(patches, prior_patches, blocks, dest, target, flows, valid, stiffness):
    cos_t, sin_t = dft_tables(P_SIZE)
    tile_count = lax.axis_size("tile")
    shifted = from_behind(patches, "gz", 1)
    earlier = jnp.where(lax.axis_index("gz") == 0, prior_patches[None], shifted)[0]
    owner_tile = dest[0, :, 0]
    wanted = target[0]
    own_blocks = blocks[0]
    block_count = own_blocks.shape[0]
    tile_ids = jnp.arange(tile_count, dtype=jnp.int32)
    slot_ids = jnp.arange(tile_count * CAP, dtype=jnp.int32)
    tile_hits = (owner_tile[:, None] == tile_ids[None, :]).astype(jnp.int32)
    slot_rank = jnp.sum((jnp.cumsum(tile_hits, axis=0) - tile_hits) * tile_hits, axis=1)
    slot_index = owner_tile * CAP + slot_rank
    slot_picks = slot_index[:, None] == slot_ids[None, :]
    requested = jnp.sum(jnp.where(slot_picks, wanted[:, None], 0), axis=0).reshape(tile_count, CAP)
    earlier_spec = spectrum(earlier, cos_t, sin_t)
    outgoing = jnp.einsum(
        "bs,bp->sp", slot_picks.astype(jnp.bfloat16), own_blocks, preferred_element_type=jnp.float32
    )
    outgoing = outgoing.astype(jnp.bfloat16).reshape(tile_count, CAP, PIX)
    arrived = lax.all_to_all(outgoing, "tile", split_axis=0, concat_axis=0, tiled=True)
    asked_rows = lax.all_to_all(requested, "tile", split_axis=0, concat_axis=0, tiled=True)
    slot_count = asked_rows.shape[1]
    flat_asked = asked_rows.reshape(-1)
    spec_a = (
        jnp.take(earlier_spec[0], flat_asked, axis=0),
        jnp.take(earlier_spec[1], flat_asked, axis=0),
    )
    spec_b = spectrum(arrived.reshape(tile_count * slot_count, PIX), cos_t, sin_t)
    result = correlate(spec_a, spec_b, cos_t, sin_t).reshape(tile_count, slot_count, PIX)
    returned = lax.all_to_all(result, "tile", split_axis=0, concat_axis=0, tiled=True)
    corr_maps = jnp.take(returned.reshape(tile_count * CAP, PIX), slot_index, axis=0)
    peak = jnp.max(corr_maps.astype(jnp.float32), axis=-1)
    confidence = peak / (1.0 + peak)
    node_cols = flows.shape[3]
    conf_cols = jnp.repeat(confidence, node_cols // block_count)
    has_prior = (lax.axis_index("gz") > 0).astype(jnp.float32)
    weight = stiffness * valid.astype(jnp.float32) * conf_cols[None, None, :] * has_prior
    weight_next, flow_next = from_behind((weight, flows), "gz", -1)

    def iteration(counter, nodes):
        padded = with_halo(nodes, (("gz", 0), ("tile", 2)), 1)
        padded = jnp.pad(padded, ((0, 0), (0, 0), (0, 0), (1, 1)))
        middle = padded[1:-1]
        laplace = (
            middle[:, :, 2:, 1:-1]
            + middle[:, :, :-2, 1:-1]
            + middle[:, :, 1:-1, 2:]
            + middle[:, :, 1:-1, :-2]
            - 4.0 * nodes
        )
        lower_nbr = padded[:-2, :, 1:-1, 1:-1]
        upper_nbr = padded[2:, :, 1:-1, 1:-1]
        pull_total = (
            laplace
            + weight[:, None] * (lower_nbr + flows - nodes)
            + weight_next[:, None] * (upper_nbr - flow_next - nodes)
        )
        return nodes + 0.15 * pull_total

    mesh_nodes = lax.fori_loop(0, ITERS, iteration, jnp.zeros_like(flows))
    return (corr_maps[None], mesh_nodes)


def solution(mesh):
    return jax.shard_map(
        on_device,
        mesh=mesh,
        in_specs=(
            P("gz", "tile", None),
            P("tile", None),
            P("gz", "tile", None),
            P("gz", "tile", None),
            P("gz", "tile"),
            P("gz", None, "tile", None),
            P("gz", "tile", None),
            P("gz", "tile", None),
        ),
        out_specs=(P("gz", "tile", None), P("gz", None, "tile", None)),
        check_vma=False,
    )
```

profile of v0, /device:TPU:132, one launch (start us, length us, event | category | flops | bytes accessed | tf_op | source)
XLA Modules:
  0.0 1485.6 jit_solution(8211841996373104940)
XLA Ops:
  4.5 10.0 all-to-all-start
  22.3 9.8 all-to-all-start.1
  35.4 10.4 collective-permute-done.4
  66.1 37.8 %all-to-all-done.1 = bf16[32,2,25600]{2,1,0:T(2,128)(2,1)} async-done(((bf16[32,2,25600]{2,1,0:T(2,128)(2,1)}), bf16[32,2,25600]{2,1,0:T(2,128)(2,1)}, u32[]{:S(2)}, u32[]{:S(2)}) %all-to-all-start.1) | async-done | bytes 3276832 | tf_op jit(solution)/shard_map/all_to_all | solution.py:98
  108.6 6.7 multiply_reduce_fusion
  115.5 9.8 reshape.181
  125.3 6.3 convolution_convert_fusion.1
  136.8 6.4 fusion.36
  148.1 19.9 %fusion.10 = (bf16[64,160,160]{1,2,0:T(8,128)(2,1)}, bf16[64,160,160]{1,2,0:T(8,128)(2,1)S(1)}) fusion(bf16[64,160,160]{2,1,0:T(8,128)(2,1)} %subtract_convert_fusion.1, bf16[64,160,160]{1,2,0:T(8,128)(2,1)} %gather_fusion.1, pred[64]{0:T(512)(128)(4,1)S(1)} %compare_and_fusion, bf16[64,160,160]{1,2,0:T(8,128)(2,1)} %gather_fusion.2, ...), kind=kOutput, calls=%fused_computation.36 | convolution fusion | flops 550758400 | bytes 26214464 | tf_op jit(solution)/shard_map/jp,npk->njk/dot_general | solution.py:43
  168.0 6.4 fusion.47
  174.4 6.3 fusion.32
  180.7 15.8 %fusion.11 = f32[64,160,160]{2,1,0:T(8,128)} fusion(f32[64,160,160]{2,1,0:T(8,128)} %fusion.47, bf16[64,160,160]{1,2,0:T(8,128)(2,1)} %get-tuple-element.120), kind=kOutput, calls=%fused_computation.44 | convolution fusion | flops 1052364800 | bytes 16384000 | tf_op jit(solution)/shard_map/jp,npk->njk/dot_general | solution.py:43
  196.5 17.3 %fusion.13 = bf16[64,160,160]{1,2,0:T(8,128)(2,1)} fusion(f32[64,160,160]{2,1,0:T(8,128)} %fusion.11, f32[64,160,160]{2,1,0:T(8,128)} %fusion.32, bf16[64,160,160]{1,2,0:T(8,128)(2,1)} %get-tuple-element.120), kind=kOutput, calls=%fused_computation.46 | convolution fusion | flops 1057280000 | bytes 19660800 | tf_op jit(solution)/shard_map/jp,npk->njk/dot_general | solution.py:43
  213.8 8.2 copy.58
  222.0 10.7 reshape_reshape.3
  232.6 9.6 all-to-all-start.2
  244.3 69.5 %all-to-all-done.2 = bf16[32,2,25600]{2,1,0:T(2,128)(2,1)} async-done(((bf16[32,2,25600]{2,1,0:T(2,128)(2,1)}), bf16[32,2,25600]{2,1,0:T(2,128)(2,1)}, u32[]{:S(2)}, u32[]{:S(2)}) %all-to-all-start.2) | async-done | bytes 3276832 | tf_op jit(solution)/shard_map/all_to_all | solution.py:108
  318.5 5.5 gather_fusion
  328.2 1156.6 %while.13 = (s32[]{:T(128)}, f32[1,2,8,256]{3,2,1,0:T(8,128)S(1)}, f32[1,8,256]{2,1,0:T(8,128)S(1)}, f32[1,2,8,256]{3,2,1,0:T(8,128)S(1)}, f32[1,8,256]{2,1,0:T(...) while((s32[]{:T(128)}, f32[1,2,8,256]{3,2,1,0:T(8,128)S(1)}, ...), condition=%wide.region_9.11_spmd.clone, body=%wide.region_8.10_spmd.clone.sunk | while | flops 282019 | bytes 557791 | solution.py:138
  343.2 6.9 collective-permute-done.3
  363.2 4.9 collective-permute-done.3
  381.2 4.9 collective-permute-done.3
  399.2 4.9 collective-permute-done.3
  417.2 4.9 collective-permute-done.3
  435.2 4.9 collective-permute-done.3
  453.2 4.9 collective-permute-done.3
  471.2 4.9 collective-permute-done.3
  489.2 4.9 collective-permute-done.3
  507.3 4.9 collective-permute-done.3
  525.3 4.9 collective-permute-done.3
  543.3 4.9 collective-permute-done.3
  561.3 4.9 collective-permute-done.3
  579.3 4.9 collective-permute-done.3
  597.3 4.9 collective-permute-done.3
  615.3 4.9 collective-permute-done.3
  633.3 4.9 collective-permute-done.3
  651.3 4.9 collective-permute-done.3
  669.3 4.9 collective-permute-done.3
  705.3 4.9 collective-permute-done.3
  741.3 4.9 collective-permute-done.3
  759.4 4.9 collective-permute-done.3
  795.4 4.9 collective-permute-done.3
  831.4 4.9 collective-permute-done.3
  867.4 4.9 collective-permute-done.3
  885.4 4.9 collective-permute-done.3
  921.4 4.9 collective-permute-done.3
  957.4 4.9 collective-permute-done.3
  993.5 4.9 collective-permute-done.3
  1011.5 4.9 collective-permute-done.3
  1047.5 4.9 collective-permute-done.3
  1083.5 4.9 collective-permute-done.3
  1101.5 4.9 collective-permute-done.3
  1137.5 4.9 collective-permute-done.3
  1173.5 4.9 collective-permute-done.3
  1209.5 4.9 collective-permute-done.3
  1227.5 4.9 collective-permute-done.3
  1263.6 4.9 collective-permute-done.3
  1299.6 4.9 collective-permute-done.3
  1335.6 4.9 collective-permute-done.3
  1353.6 4.9 collective-permute-done.3
  1389.6 4.9 collective-permute-done.3
  1425.6 4.9 collective-permute-done.3
  1443.6 4.9 collective-permute-done.3
  1479.7 4.9 collective-permute-done.3
  (800 shorter events, 991.7 us)
Async XLA Ops:
  4.5 17.8 %all-to-all-start = ((s32[32,1,2]{2,1,0:T(1,128)}), s32[32,1,2]{2,1,0:T(1,128)S(1)}, u32[]{:S(2)}, u32[]{:S(2)}) async-start(s32[32,1,2]{2,1,0:T(1,128)} %bitcast.2), calls=%async_computation | async-start | bytes 32768 | tf_op jit(solution)/shard_map/all_to_all | solution.py:99
  22.3 81.6 %all-to-all-start.1 = ((bf16[32,2,25600]{2,1,0:T(2,128)(2,1)}), bf16[32,2,25600]{2,1,0:T(2,128)(2,1)}, u32[]{:S(2)}, u32[]{:S(2)}) async-start(bf16[32,2,25600]{2,1,0:T(2,128)(2,1)} %reshape.178), calls=%async_computation.1 | async-start | bytes 6553600 | tf_op jit(solution)/shard_map/all_to_all | solution.py:98
  32.1 13.7 collective-permute-start.4
  232.6 81.1 %all-to-all-start.2 = ((bf16[32,2,25600]{2,1,0:T(2,128)(2,1)}), bf16[32,2,25600]{2,1,0:T(2,128)(2,1)}, u32[]{:S(2)}, u32[]{:S(2)}) async-start(bf16[32,2,25600]{2,1,0:T(2,128)(2,1)} %reshape_reshape.3), calls=%async_computation.2 | async-start | bytes 6553600 | tf_op jit(solution)/shard_map/all_to_all | solution.py:108
  242.3 85.9 %collective-permute-start.6 = (f32[1,2,8,256]{3,2,1,0:T(8,128)S(1)}, f32[1,2,8,256]{3,2,1,0:T(8,128)S(1)}, u32[]{:S(2)}, u32[]{:S(2)}) collective-permute-start(f32[1,2,8,256]{3,2,1,0:T(8,128)S(1)} %copy-done.7), channel_id=1, source_target_pairs={{32,0},{64,32},{96,64},{128,96},{160,128},{192,160},{224,192},{33,... | collective-permute-start | bytes 49160 | tf_op jit(solution)/shard_map/ppermute | solution.py:15
  341.2 8.8 collective-permute-start.3
  359.3 8.8 collective-permute-start.3
  377.3 8.8 collective-permute-start.3
  395.3 8.8 collective-permute-start.3
  413.3 8.8 collective-permute-start.3
  431.3 8.8 collective-permute-start.3
  449.3 8.8 collective-permute-start.3
  467.3 8.8 collective-permute-start.3
  485.3 8.8 collective-permute-start.3
  503.3 8.8 collective-permute-start.3
  521.3 8.8 collective-permute-start.3
  539.3 8.8 collective-permute-start.3
  557.3 8.8 collective-permute-start.3
  575.3 8.8 collective-permute-start.3
  593.3 8.8 collective-permute-start.3
  611.4 8.8 collective-permute-start.3
  629.4 8.8 collective-permute-start.3
  647.4 8.8 collective-permute-start.3
  665.4 8.8 collective-permute-start.3
  683.4 8.8 collective-permute-start.3
  701.4 8.8 collective-permute-start.3
  719.4 8.8 collective-permute-start.3
  737.4 8.8 collective-permute-start.3
  755.4 8.8 collective-permute-start.3
  791.4 8.8 collective-permute-start.3
  809.4 8.8 collective-permute-start.3
  827.4 8.8 collective-permute-start.3
  845.5 8.8 collective-permute-start.3
  863.5 8.8 collective-permute-start.3
  881.5 8.8 collective-permute-start.3
  917.5 8.8 collective-permute-start.3
  935.5 8.8 collective-permute-start.3
  953.5 8.8 collective-permute-start.3
  971.5 8.8 collective-permute-start.3
  989.5 8.8 collective-permute-start.3
  1007.5 8.8 collective-permute-start.3
  1025.5 8.8 collective-permute-start.3
  1043.5 8.8 collective-permute-start.3
  1061.5 8.8 collective-permute-start.3
  1079.5 8.8 collective-permute-start.3
  1097.6 8.8 collective-permute-start.3
  1133.6 8.8 collective-permute-start.3
  1151.6 8.8 collective-permute-start.3
  1169.6 8.8 collective-permute-start.3
  1187.6 8.8 collective-permute-start.3
  1205.6 8.8 collective-permute-start.3
  1223.6 8.8 collective-permute-start.3
  1259.6 8.8 collective-permute-start.3
  1277.6 8.8 collective-permute-start.3
  1295.6 8.8 collective-permute-start.3
  1313.6 8.8 collective-permute-start.3
  1331.7 8.8 collective-permute-start.3
  1349.7 8.8 collective-permute-start.3
  1367.7 8.8 collective-permute-start.3
  1385.7 8.8 collective-permute-start.3
  1403.7 8.8 collective-permute-start.3
  1421.7 8.8 collective-permute-start.3
  1439.7 8.8 collective-permute-start.3
  1475.7 8.8 collective-permute-start.3
  (211 other events, 2308.1 us)
where the time goes:
time: 1500 us; the launch traced here: 1490 us
  starting transfers between devices  687 us (46%)
  waiting for transfers between devices  603 us (40%)
  matrix products  101 us (7%)
  local copies, waits for them, and re-layouts  55.9 us (4%)
  other arithmetic  33.7 us (2%)
    ppermute x128, waiting for transfers between devices, with_halo(): before = lax.ppermute(last, axis, up)  485 us
    ppermute x128, starting transfers between devices, with_halo(): before = lax.ppermute(last, axis, up)  403 us
    ppermute x128, starting transfers between devices, with_halo(): after = lax.ppermute(first, axis, down)  250 us
    dot_general x10, matrix products, left_mul(): jnp.einsum('jp,npk->njk', matrix_t, pixels, preferred_element_type=jnp.fl...  72.7 us
    all_to_all x1, waiting for transfers between devices, on_device(): lax.all_to_all(result, 'tile', split_axis=0, concat_axis=0, tiled=True)  69.5 us
    all_to_all x1, waiting for transfers between devices, on_device(): lax.all_to_all(outgoing, 'tile', split_axis=0, concat_axis=0, tiled=True)  37.8 us
  transfers between devices with their start and end apart: 262, of which 131 were waited for; matrix products, arithmetic and copies ran while one was open for 3% of the time, Pallas kernels for 0%

commit v1 on v0

v1 whole, which is shorter than its diff:
```python
import functools

import jax
import jax.numpy as jnp
from jax import lax
from jax.experimental import pallas as pl
from jax.experimental.pallas import tpu as pltpu
from jax.sharding import PartitionSpec as P

P_SIZE = 160
PIX = 25600
CAP = 2
ITERS = 64
GROUP = 8


def from_behind(value, axis, steps):
    count = lax.axis_size(axis)
    first, last = (max(0, -steps), min(count, count - steps))
    return lax.ppermute(value, axis, [(source, source + steps) for source in range(first, last)])


def dft_tables(edge_len):
    positions = jnp.arange(edge_len, dtype=jnp.int32)
    phase_idx = positions[:, None] * positions[None, :] % edge_len
    angles = phase_idx.astype(jnp.float32) * (2.0 * jnp.pi / edge_len)
    return (jnp.cos(angles).astype(jnp.bfloat16), jnp.sin(angles).astype(jnp.bfloat16))


def right_mul(pixels, matrix_t):
    return jnp.einsum("npq,qk->npk", pixels, matrix_t, preferred_element_type=jnp.float32)


def left_mul(matrix_t, pixels):
    return jnp.einsum("jp,npk->njk", matrix_t, pixels, preferred_element_type=jnp.float32)


def normalized(pixel_rows):
    values = pixel_rows.astype(jnp.float32)
    centred = values - jnp.mean(values, axis=-1, keepdims=True)
    spread = jnp.mean(centred * centred, axis=-1, keepdims=True)
    return (centred * lax.rsqrt(spread + 1e-05)).astype(jnp.bfloat16)


def spectrum(pixel_rows, cos_t, sin_t):
    edge_len = cos_t.shape[0]
    pixels = normalized(pixel_rows).reshape(pixel_rows.shape[0], edge_len, edge_len)
    first_re = right_mul(pixels, cos_t).astype(jnp.bfloat16)
    first_im = right_mul(pixels, sin_t).astype(jnp.bfloat16)
    spec_re = (left_mul(cos_t, first_re) - left_mul(sin_t, first_im)).astype(jnp.bfloat16)
    spec_im = (left_mul(sin_t, first_re) + left_mul(cos_t, first_im)).astype(jnp.bfloat16)
    return (spec_re, spec_im)


def correlate(spec_a, spec_b, cos_t, sin_t):
    edge_len = cos_t.shape[0]
    a_re = spec_a[0].astype(jnp.float32)
    a_im = spec_a[1].astype(jnp.float32)
    b_re = spec_b[0].astype(jnp.float32)
    b_im = spec_b[1].astype(jnp.float32)
    cross_re = (a_re * b_re + a_im * b_im).astype(jnp.bfloat16)
    cross_im = (a_im * b_re - a_re * b_im).astype(jnp.bfloat16)
    back_re = (right_mul(cross_re, cos_t) - right_mul(cross_im, sin_t)).astype(jnp.bfloat16)
    back_im = (right_mul(cross_re, sin_t) + right_mul(cross_im, cos_t)).astype(jnp.bfloat16)
    field_out = (left_mul(cos_t, back_re) - left_mul(sin_t, back_im)) * (1.0 / float(edge_len) ** 3)
    return field_out.astype(jnp.bfloat16).reshape(cross_re.shape[0], edge_len * edge_len)


def relax_kernel(start_ref, spring_ref, flow_ref, conf_ref, out_ref, a_buf, w_buf, n_buf, c_buf, u_buf):
    start = start_ref[0]
    rows = a_buf.shape[0]
    total = spring_ref.shape[0]
    lane = lax.broadcasted_iota(jnp.int32, (1, 8, 128), 2)
    first_col, last_col = lane == 0, lane == 127
    section = lax.broadcasted_iota(jnp.int32, (8, 256), 0)
    u_buf[...] = jnp.zeros_like(u_buf)

    def prepare(i, carry):
        r = start + i
        inside = (r >= 0) & (r < total)

        @pl.when(inside)
        def _():
            conf = conf_ref[r // 8]
            w = 0.15 * spring_ref[r].astype(jnp.float32) * conf
            w = jnp.where(section == 0, 0.0, w)
            f = flow_ref[0, r].astype(jnp.float32)
            wf = w * f
            wn = pltpu.roll(w, 7, 0)
            c = wf - pltpu.roll(wf, 7, 0)
            w_buf[i] = w
            n_buf[i] = wn
            a_buf[i] = 0.4 - w - wn
            c_buf[i] = c
            u_buf[0, i + GROUP] = c

        @pl.when(jnp.logical_not(inside))
        def _():
            zero = jnp.zeros((8, 256), jnp.float32)
            w_buf[i] = zero
            n_buf[i] = zero
            a_buf[i] = zero
            c_buf[i] = zero

        return carry

    lax.fori_loop(0, rows, prepare, 0)

    def step(source, target, s):
        low = (s - 1) // GROUP
        high = (129 - s + GROUP - 1) // GROUP

        def group(g, carry):
            i = g * GROUP
            x = [u_buf[source, pl.ds(i + GROUP - 1, GROUP + 2), :, 128 * h : 128 * h + 128] for h in range(2)]
            mid = [v[1:-1] for v in x]
            rot_up = [pltpu.roll(v, 1, 2) for v in mid]
            rot_down = [pltpu.roll(v, 127, 2) for v in mid]
            left = [jnp.where(first_col, 0.0, rot_up[0]), jnp.where(first_col, rot_up[0], rot_up[1])]
            right = [jnp.where(last_col, rot_down[1], rot_down[0]), jnp.where(last_col, 0.0, rot_down[1])]
            for h in range(2):
                at = (pl.ds(i, GROUP), slice(None), slice(128 * h, 128 * h + 128))
                around = x[h][:-2] + x[h][2:] + left[h] + right[h]
                r = start + i
                row = lax.broadcasted_iota(jnp.int32, (GROUP, 1, 1), 0) + r
                share = jnp.where((row >= 0) & (row < total), 0.15, 0.0)
                new = a_buf[at] * mid[h] + c_buf[at] + share * around
                new = new + w_buf[at] * pltpu.roll(mid[h], 1, 1) + n_buf[at] * pltpu.roll(mid[h], 7, 1)
                u_buf[target, pl.ds(i + GROUP, GROUP), :, 128 * h : 128 * h + 128] = new
            return carry

        lax.fori_loop(low, high, group, 0)

    def pair(k, carry):
        step(0, 1, 2 * k + 2)
        step(1, 0, 2 * k + 3)
        return carry

    lax.fori_loop(0, (ITERS - 2) // 2, pair, 0)
    step(0, 1, ITERS)
    out_ref[...] = u_buf[1, pl.ds(63 + GROUP, 2)]


def relax(start, component, spring, flow, conf):
    rows = 2 * ITERS
    return pl.pallas_call(
        relax_kernel,
        out_shape=jax.ShapeDtypeStruct((2, 8, 256), jnp.float32),
        grid_spec=pltpu.PrefetchScalarGridSpec(
            num_scalar_prefetch=1,
            grid=(1,),
            in_specs=[
                pl.BlockSpec(spring.shape, lambda i, s: (0, 0, 0)),
                pl.BlockSpec((1,) + flow.shape[1:], lambda i, s: (s[1], 0, 0, 0)),
                pl.BlockSpec(conf.shape, lambda i, s: (0, 0, 0)),
            ],
            out_specs=pl.BlockSpec((2, 8, 256), lambda i, s: (0, 0, 0)),
            scratch_shapes=[pltpu.VMEM((rows, 8, 256), jnp.float32)] * 4
            + [pltpu.VMEM((2, rows + 2 * GROUP, 8, 256), jnp.float32)],
        ),
        compiler_params=pltpu.CompilerParams(vmem_limit_bytes=40 * 1024 * 1024),
    )(jnp.stack([start, component]).astype(jnp.int32), spring, flow, conf)


def on_device(patches, prior_patches, blocks, dest, target, flows, valid, stiffness):
    cos_t, sin_t = dft_tables(P_SIZE)
    tile_count = lax.axis_size("tile")
    gz_index = lax.axis_index("gz")
    tile_index = lax.axis_index("tile")

    spring = (stiffness * valid.astype(jnp.float32))[0].astype(jnp.bfloat16)
    both = jnp.stack([spring, flows[0, 0].astype(jnp.bfloat16), flows[0, 1].astype(jnp.bfloat16)])
    everywhere = lax.all_gather(both, ("tile", "gz"))
    node_rows = flows.shape[2]
    everywhere = everywhere.reshape(tile_count, 8, 3, node_rows, -1).transpose(2, 0, 3, 1, 4)
    everywhere = everywhere.reshape(3, tile_count * node_rows, 8, -1)

    shifted = from_behind(patches, "gz", 1)
    earlier = jnp.where(gz_index == 0, prior_patches[None], shifted)[0]
    owner_tile = dest[0, :, 0]
    wanted = target[0]
    own_blocks = blocks[0]
    block_count = own_blocks.shape[0]
    tile_ids = jnp.arange(tile_count, dtype=jnp.int32)
    slot_ids = jnp.arange(tile_count * CAP, dtype=jnp.int32)
    tile_hits = (owner_tile[:, None] == tile_ids[None, :]).astype(jnp.int32)
    slot_rank = jnp.sum((jnp.cumsum(tile_hits, axis=0) - tile_hits) * tile_hits, axis=1)
    slot_index = owner_tile * CAP + slot_rank
    slot_picks = slot_index[:, None] == slot_ids[None, :]
    requested = jnp.sum(jnp.where(slot_picks, wanted[:, None], 0), axis=0).reshape(tile_count, CAP)
    asked_rows = lax.all_to_all(requested, "tile", split_axis=0, concat_axis=0, tiled=True)
    outgoing = jnp.take(earlier, asked_rows.reshape(-1), axis=0).reshape(tile_count, CAP, PIX)
    arrived = lax.all_to_all(outgoing, "tile", split_axis=0, concat_axis=0, tiled=True)
    spec_b = spectrum(own_blocks, cos_t, sin_t)
    chosen = jnp.take(arrived.reshape(tile_count * CAP, PIX), slot_index, axis=0)
    spec_a = spectrum(chosen, cos_t, sin_t)
    corr_maps = correlate(spec_a, spec_b, cos_t, sin_t)
    peak = jnp.max(corr_maps.astype(jnp.float32), axis=-1)
    confidence = peak / (1.0 + peak)

    all_conf = lax.all_gather(confidence, ("tile", "gz")).reshape(tile_count, 8, block_count)
    node_cols = flows.shape[3]
    conf_cols = jnp.repeat(all_conf, node_cols // block_count, axis=2)
    start = tile_index * node_rows + 2 * (gz_index // 2) - (ITERS - 1)
    mine = relax(start, gz_index % 2, everywhere[0], everywhere[1:], conf_cols)
    swapped = lax.all_to_all(mine.transpose(1, 0, 2), "gz", split_axis=0, concat_axis=0, tiled=True)
    mesh_nodes = swapped.reshape(4, 2, 2, node_cols).transpose(1, 0, 2, 3).reshape(1, 2, node_rows, node_cols)
    return (corr_maps[None], mesh_nodes)


def solution(mesh):
    return jax.shard_map(
        on_device,
        mesh=mesh,
        in_specs=(
            P("gz", "tile", None),
            P("tile", None),
            P("gz", "tile", None),
            P("gz", "tile", None),
            P("gz", "tile"),
            P("gz", None, "tile", None),
            P("gz", "tile", None),
            P("gz", "tile", None),
        ),
        out_specs=(P("gz", "tile", None), P("gz", None, "tile", None)),
        check_vma=False,
    )
```

time: 1500 us -> 398 us (0.27)
  the two profiles are of different devices: /device:TPU:132 before, /device:TPU:33 now
where the time goes in v1:
time: 398 us; the launch traced here: 391 us
  waiting for transfers between devices  111 us (28%)
  Pallas kernels  66.4 us (17%)
  blocking collectives  55.6 us (14%)
  matrix products  55.2 us (14%)
  local copies, waits for them, and re-layouts  47 us (12%)
  starting transfers between devices  24 us (6%)
  other arithmetic  17.1 us (4%)
  between operations  14.6 us (4%)
    all_gather x1, waiting for transfers between devices, on_device(): everywhere = lax.all_gather(both, ('tile', 'gz'))  104 us
    pallas_call x1, Pallas kernels, relax(): pl.pallas_call(relax_kernel, out_shape=jax.ShapeDtypeStruct((2, 8, 256),...  66.4 us
    all_gather x1, blocking collectives, on_device(): lax.all_gather(confidence, ('tile', 'gz'))  55.6 us
    dot_general x10, matrix products, left_mul(): jnp.einsum('jp,npk->njk', matrix_t, pixels, preferred_element_type=jnp.fl...  38.7 us
    dot_general x6, matrix products, right_mul(): jnp.einsum('npq,qk->npk', pixels, matrix_t, preferred_element_type=jnp.fl...  16.5 us
    gather x2, local copies, waits for them, and re-layouts, on_device(): jnp.take(arrived.reshape(tile_count * CAP, PIX), slot_index, axis=0)  12 us
    all_to_all x1, starting transfers between devices, on_device(): lax.all_to_all(requested, 'tile', split_axis=0, concat_axis=0, tiled=True)  10.8 us
  transfers between devices with their start and end apart: 5, of which 2 were waited for; matrix products, arithmetic and copies ran while one was open for 10% of the time, Pallas kernels for 0%

profile of v1, /device:TPU:33, one launch (start us, length us, event | category | flops | bytes accessed | tf_op | source)
XLA Modules:
  0.0 390.6 jit_solution(12616193704492088253)
XLA Ops:
  7.2 3.7 collective-permute-start
  10.8 0.7 fusion.50
  11.6 0.1 reduce_window_sum.11
  11.6 0.8 select_reduce_fusion.1
  12.5 0.7 compare_and_fusion.1
  13.1 0.7 select_reduce_fusion
  13.9 0.7 all_to_all.12
  14.6 10.8 %all-to-all-start = ((s32[32,1,2]{2,1,0:T(1,128)}), s32[32,1,2]{2,1,0:T(1,128)S(1)}, u32[]{:S(2)}, u32[]{:S(2)}) async-start(s32[32,1,2]{2,1,0:T(1,128)} %bitcast.2), calls=%async_computation | async-start | bytes 32768 | tf_op jit(solution)/shard_map/all_to_all | solution.py:191
  25.4 0.7 multiply_convert_fusion.3
  26.1 0.7 convert.16
  26.9 6.2 %all-to-all-done = s32[32,1,2]{2,1,0:T(1,128)S(1)} async-done(((s32[32,1,2]{2,1,0:T(1,128)}), s32[32,1,2]{2,1,0:T(1,128)S(1)}, u32[]{:S(2)}, u32[]{:S(2)}) %all-to-all-start) | async-done | bytes 288 | tf_op jit(solution)/shard_map/all_to_all | solution.py:191
  33.0 0.5 broadcast.168
  33.6 0.7 reduce.7
  34.2 0.1 reshape.214
  34.4 0.1 copy.61
  34.4 0.1 copy.62
  34.6 1.2 fusion.16
  35.8 4.3 %gather_fusion = bf16[64,25600]{1,0:T(8,128)(2,1)} fusion(bf16[16,25600]{1,0:T(8,128)(2,1)S(1)} %fusion.16, s32[1024]{0:T(1024)S(1)} %pad_clamp_fusion.1), kind=kCustom, calls=%fused_computation | custom fusion | bytes 6553856 | tf_op jit(solution)/shard_map/jit(_take)/gather | solution.py:192
  40.2 3.3 gather.13
  43.5 4.6 %broadcast_select_fusion = bf16[32,2,25600]{2,1,0:T(2,128)(2,1)} fusion(bf16[32,2,25600]{2,1,0:T(2,128)(2,1)S(1)} %gather.13, pred[32,2]{1,0:T(8,128)(4,1)S(1)} %copy.62), kind=kLoop, calls=%fused_computation.2 | loop fusion | flops 1638400 | bytes 6553664 | tf_op jit(solution)/shard_map/jit(_take)/select_n | solution.py:192
  48.1 5.7 %all-to-all-start.1 = ((bf16[32,2,25600]{2,1,0:T(2,128)(2,1)}), bf16[32,2,25600]{2,1,0:T(2,128)(2,1)}, u32[]{:S(2)}, u32[]{:S(2)}) async-start(bf16[32,2,25600]{2,1,0:T(2,128)(2,1)} %broadcast_select_fusion), calls=%async_computation.1 | async-start | bytes 6553600 | tf_op jit(solution)/shard_map/all_to_all | solution.py:193
  53.8 0.0 all-gather.4.cloned.1.call-start
  53.9 0.6 pad_maximum_fusion
  54.5 0.1 all-gather.4.cloned.1.call-update
  54.6 5.0 %reshape.221 = f32[32,160,160]{2,1,0:T(8,128)} reshape(bf16[1,32,25600]{2,1,0:T(8,128)(2,1)S(1)} %copy-done) | data formatting | bytes 4915200 | tf_op jit(solution)/shard_map/convert_element_type | solution.py:39
  59.6 0.1 pad_add_fusion.start_ref
  59.7 0.3 convert_reduce_fusion.1
  60.0 0.8 fusion.7
  60.8 4.0 %convolution_convert_fusion.1 = bf16[32,160,160]{2,1,0:T(8,128)(2,1)S(1)} fusion(f32[32,160,160]{2,1,0:T(8,128)} %reshape.221, f32[32]{0:T(128)S(1)} %add_rsqrt_fusion, f32[32]{0:T(128)S(1)} %broadcast_multiply_fusion), kind=kOutput, calls=%fused_computation.35 | convolution fusion | flops 265676800 | bytes 4915456 | tf_op jit(solution)/shard_map/npq,qk->npk/dot_general | solution.py:31
  64.8 1.6 fusion.29
  66.4 1.6 fusion.44
  68.0 1.5 convolution_convert_fusion
  69.5 3.2 add_convert_fusion.1
  72.7 3.1 subtract_convert_fusion.1
  75.8 104.4 %all-gather.4.cloned.1.call-done = bf16[768,8,256]{2,1,0:T(8,128)(2,1)} async-done(((bf16[3,8,256]{2,1,0:T(8,128)(2,1)}), bf16[768,8,256]{2,1,0:T(8,128)(2,1)}) %all-gather.4.cloned.1.call-update) | async-done | bytes 3145744 | tf_op jit(solution)/shard_map/all_gather | solution.py:173
  180.2 3.0 copy.98
  183.2 0.1 slice.29
  183.3 0.1 slice.30
  183.4 4.9 %reshape.215 = bf16[64,25600]{1,0:T(8,128)(2,1)} reshape(bf16[32,2,25600]{2,1,0:T(2,128)(2,1)} %all-to-all-done.1) | data formatting | bytes 6553600 | tf_op jit(solution)/shard_map/reshape | solution.py:195
  188.3 6.5 %gather_fusion.1 = bf16[32,25600]{1,0:T(8,128)(2,1)} fusion(bf16[64,25600]{1,0:T(8,128)(2,1)} %reshape.215, s32[1024]{0:T(1024)S(1)} %pad_clamp_fusion), kind=kCustom, calls=%fused_computation.1 | custom fusion | bytes 3276928 | tf_op jit(solution)/shard_map/jit(_take)/gather | solution.py:195
  194.8 5.5 %gather.15 = bf16[32,160,160]{2,1,0:T(8,128)(2,1)} reshape(bf16[32,25600]{1,0:T(8,128)(2,1)} %gather_fusion.1) | data formatting | bytes 3276800 | tf_op jit(solution)/shard_map/jit(_take)/gather | solution.py:195
  200.4 2.1 convert_reduce_fusion
  202.5 2.1 fusion.5
  204.6 1.6 convolution_convert_fusion.3
  206.3 1.6 convolution_convert_fusion.2
  207.9 1.6 fusion.31
  209.5 1.6 fusion.47
  211.1 1.7 add_convert_fusion.2
  212.9 0.8 copy-done.2
  213.6 5.2 %fusion.10 = (bf16[32,160,160]{1,2,0:T(8,128)(2,1)}, bf16[32,160,160]{1,2,0:T(8,128)(2,1)S(1)}) fusion(bf16[32,160,160]{2,1,0:T(8,128)(2,1)S(1)} %copy-done.1, bf16[32,160,160]{2,1,0:T(8,128)(2,1)S(1)} %copy-done.2, bf16[32,160,160]{2,1,0:T(8,128)(2,1)S(1)} %add_convert_fusion.2, f32[32,160,160]{2,1,0:T(8,128)S(1)} %fusion.47, ...), kind=kOutput, calls=%fused_computation.30 | convolution fusion | flops 273868800 | bytes 13107200 | tf_op jit(solution)/shard_map/jp,npk->njk/dot_general | solution.py:35
  218.8 3.9 fusion.40
  222.7 3.9 %fusion.25 = f32[32,160,160]{2,1,0:T(8,128)} fusion(bf16[32,160,160]{1,2,0:T(8,128)(2,1)S(1)} %get-tuple-element.5), kind=kOutput, calls=%fused_computation.54 | convolution fusion | flops 262400000 | bytes 4915200 | tf_op jit(solution)/shard_map/npq,qk->npk/dot_general | solution.py:31
  226.6 9.2 %fusion.8 = f32[32,160,160]{2,1,0:T(8,128)} fusion(f32[32,160,160]{2,1,0:T(8,128)} %fusion.40, bf16[32,160,160]{1,2,0:T(8,128)(2,1)} %get-tuple-element.4), kind=kOutput, calls=%fused_computation.28 | convolution fusion | flops 526438400 | bytes 8192000 | tf_op jit(solution)/shard_map/jp,npk->njk/dot_general | solution.py:35
  235.9 9.9 %fusion.108 = (bf16[32]{0:T(256)(128)(2,1)S(1)}, bf16[32,160,160]{2,1,0:T(8,128)(2,1)}) fusion(f32[32,160,160]{2,1,0:T(8,128)} %fusion.8, f32[32,160,160]{2,1,0:T(8,128)} %fusion.25, bf16[32,160,160]{1,2,0:T(8,128)(2,1)} %get-tuple-element.4), kind=kOutput, calls=%fused_computation.136 | convolution fusion | flops 529715168 | bytes 9830464 | tf_op jit(solution)/shard_map/jp,npk->njk/dot_general | solution.py:35
  245.8 55.6 %all-gather.1 = f32[256,1,32]{2,1,0:T(1,128)S(1)} all-gather(f32[1,1,32]{2,1,0:T(1,128)S(1)} %fusion.51), channel_id=1, replica_groups=mesh['gz'=8,'tile'=32] {'tile','gz'}, dimensions={0}, use_global_device_ids=true | all-gather | bytes 32896 | tf_op jit(solution)/shard_map/all_gather | solution.py:201
  301.4 0.1 copy.79
  301.5 1.0 broadcast_bitcast_fusion
  302.5 1.6 copy.80.conf_ref
  304.1 66.4 %shard_map.95 = f32[2,8,256]{2,1,0:T(8,128)S(1)} custom-call(s32[2]{0:T(128)S(1)} %pad_add_fusion.start_ref, bf16[256,8,256]{2,1,0:T(8,128)(2,1)S(1)} %bitcast.101, bf16[2,256,8,256]{3,2,1,0:T(8,128)(2,1)S(1)} %bitcast.100, f32[32,8,256]{2,1,0:T(8,128)S(1)} %copy.80.conf_ref), custom_call_target="tpu_custom_call" | custom-call | tf_op jit(solution)/shard_map/pallas_call | solution.py:146
  370.4 0.6 copy.81
  371.1 3.8 all-to-all-start.2
  374.9 3.3 copy.77
  378.2 4.7 %broadcast_in_dim_reshape.3 = bf16[1,32,25600]{2,1,0:T(8,128)(2,1)} reshape(bf16[32,160,160]{2,1,0:T(8,128)(2,1)S(1)} %copy.77) | data formatting | bytes 3276800 | tf_op jit(solution)/shard_map/broadcast_in_dim;reshape | solution.py:208
  382.9 0.6 reshape.220
  (29 shorter events, 0.1 us)
Async XLA Ops:
  7.2 27.4 %collective-permute-start = (bf16[1,16,25600]{2,1,0:T(8,128)(2,1)}, bf16[1,16,25600]{2,1,0:T(8,128)(2,1)S(1)}, u32[]{:S(2)}, u32[]{:S(2)}) collective-permute-start(bf16[1,16,25600]{2,1,0:T(8,128)(2,1)} %param.8), channel_id=1, source_target_pairs={{0,32},{32,64},{64,96},{96,128},{128,160},{160,192},{192,224},{1,3... | collective-permute-start | bytes 2457608 | tf_op jit(solution)/shard_map/ppermute | solution.py:20
  14.6 18.4 %all-to-all-start = ((s32[32,1,2]{2,1,0:T(1,128)}), s32[32,1,2]{2,1,0:T(1,128)S(1)}, u32[]{:S(2)}, u32[]{:S(2)}) async-start(s32[32,1,2]{2,1,0:T(1,128)} %bitcast.2), calls=%async_computation | async-start | bytes 32768 | tf_op jit(solution)/shard_map/all_to_all | solution.py:191
  48.1 6.4 %copy-start = (bf16[1,32,25600]{2,1,0:T(8,128)(2,1)S(1)}, bf16[1,32,25600]{2,1,0:T(8,128)(2,1)}, u32[]{:S(2)}) copy-start(bf16[1,32,25600]{2,1,0:T(8,128)(2,1)} %param.10) | copy-start | bytes 4915204
  48.1 135.3 %all-to-all-start.1 = ((bf16[32,2,25600]{2,1,0:T(2,128)(2,1)}), bf16[32,2,25600]{2,1,0:T(2,128)(2,1)}, u32[]{:S(2)}, u32[]{:S(2)}) async-start(bf16[32,2,25600]{2,1,0:T(2,128)(2,1)} %broadcast_select_fusion), calls=%async_computation.1 | async-start | bytes 6553600 | tf_op jit(solution)/shard_map/all_to_all | solution.py:193
  53.8 126.4 %all-gather.4.cloned.1.call-start = ((), (), s32[]{:S(2)}) async-start(), calls=%async_computation.3 | async-start | bytes 3158016 | tf_op jit(solution)/shard_map/all_gather | solution.py:173
  54.6 5.1 %copy-start.4 = (s32[1,32,1]{1,2,0:T(1,128)S(1)}, s32[1,32,1]{1,2,0:T(1,128)}, u32[]{:S(2)}) copy-start(s32[1,32,1]{1,2,0:T(1,128)} %param.11) | copy-start | bytes 388
  64.8 3.2 slice-start
  66.4 1.6 slice-start.1
  200.4 4.2 %copy-start.3 = (bf16[32,160,160]{2,1,0:T(8,128)(2,1)S(1)}, bf16[32,160,160]{2,1,0:T(8,128)(2,1)}, u32[]{:S(2)}) copy-start(bf16[32,160,160]{2,1,0:T(8,128)(2,1)} %gather.15) | copy-start | bytes 4915204
  211.1 1.7 copy-start.1
  211.1 2.5 copy-start.2
  371.1 11.9 %all-to-all-start.2 = ((f32[8,2,256]{2,1,0:T(2,128)}), f32[8,2,256]{2,1,0:T(2,128)S(1)}, u32[]{:S(2)}, u32[]{:S(2)}) async-start(f32[8,2,256]{2,1,0:T(2,128)} %copy.81), calls=%async_computation.2 | async-start | bytes 32768 | tf_op jit(solution)/shard_map/all_to_all | solution.py:206
Sparse Core Ops, SparseCore 0:
  58.9 121.2 all-gather.3

commit v2 on v1

--- a/solution.py
+++ b/solution.py
@@ -66,45 +66,205 @@
     return field_out.astype(jnp.bfloat16).reshape(cross_re.shape[0], edge_len * edge_len)
 
 
-def relax_kernel(start_ref, spring_ref, flow_ref, conf_ref, out_ref, a_buf, w_buf, n_buf, c_buf, u_buf):
-    start = start_ref[0]
+MESH = pl.DeviceIdType.MESH
+GZ = 8
+REACH = 8
+
+
+def group_barrier(peers):
+    barrier = pltpu.get_barrier_semaphore()
+    for peer in peers:
+        pl.semaphore_signal(barrier, inc=1, device_id=peer, device_id_type=MESH)
+    pl.semaphore_wait(barrier, len(peers))
+
+
+def gz_peers():
+    gz, tile = lax.axis_index("gz"), lax.axis_index("tile")
+    return [(lax.rem(gz + d, GZ), tile) for d in range(1, GZ)]
+
+
+def tile_peers(tile_count):
+    gz, tile = lax.axis_index("gz"), lax.axis_index("tile")
+    offsets = [e for k in range(1, REACH + 1) for e in (k, -k)]
+    return offsets, [(gz, lax.rem(tile + e + tile_count, tile_count)) for e in offsets]
+
+
+def exchange_gz(source_of, held, send, recv):
+    gz = lax.axis_index("gz")
+    copies = []
+    for d, peer in enumerate(gz_peers()):
+        copies.append(
+            pltpu.make_async_remote_copy(
+                src_ref=source_of(peer[0]), dst_ref=held.at[gz], send_sem=send.at[d], recv_sem=recv.at[d],
+                device_id=peer, device_id_type=MESH,
+            )
+        )
+    for copy in copies:
+        copy.start()
+    return copies
+
+
+def exchange_tiles(tile_count, source, window, send, recv):
+    offsets, peers = tile_peers(tile_count)
+    copies = []
+    for n, (e, peer) in enumerate(zip(offsets, peers)):
+        copies.append(
+            pltpu.make_async_remote_copy(
+                src_ref=source, dst_ref=window.at[REACH - e], send_sem=send.at[n], recv_sem=recv.at[n],
+                device_id=peer, device_id_type=MESH,
+            )
+        )
+    for copy in copies:
+        copy.start()
+    return copies
+
+
+def gather_kernel(tile_count, own_ref, window_ref, held, local, send_a, recv_a, send_b, recv_b):
+    gz = lax.axis_index("gz")
+    group_barrier(gz_peers() + tile_peers(tile_count)[1])
+    copies = exchange_gz(lambda peer: own_ref.at[lax.rem(peer, 2)], held, send_a, recv_a)
+    mine = pltpu.make_async_copy(own_ref.at[lax.rem(gz, 2)], held.at[gz], local.at[0])
+    mine.start()
+    mine.wait()
+    for copy in copies:
+        copy.wait()
+    copies = exchange_tiles(tile_count, held, window_ref, send_b, recv_b)
+    mine = pltpu.make_async_copy(held, window_ref.at[REACH], local.at[1])
+    mine.start()
+    mine.wait()
+    for copy in copies:
+        copy.wait()
+
+
+def gather_springs(tile_count, own):
+    return pl.pallas_call(
+        functools.partial(gather_kernel, tile_count),
+        out_shape=jax.ShapeDtypeStruct((2 * REACH + 1, GZ) + own.shape[1:], own.dtype),
+        in_specs=[pl.BlockSpec(memory_space=pltpu.VMEM)],
+        out_specs=pl.BlockSpec(memory_space=pl.ANY),
+        scratch_shapes=[
+            pltpu.VMEM((GZ,) + own.shape[1:], own.dtype),
+            pltpu.SemaphoreType.DMA((2,)),
+            pltpu.SemaphoreType.DMA((GZ - 1,)),
+            pltpu.SemaphoreType.DMA((GZ - 1,)),
+            pltpu.SemaphoreType.DMA((2 * REACH,)),
+            pltpu.SemaphoreType.DMA((2 * REACH,)),
+        ],
+        compiler_params=pltpu.CompilerParams(collective_id=1, has_side_effects=True),
+        cost_estimate=pl.CostEstimate(flops=0, bytes_accessed=8 * 1024 * 1024, transcendentals=0),
+    )(own)
+
+
+def conf_kernel(tile_count, own_ref, window_ref, held, packed, send_a, recv_a, send_b, recv_b):
+    gz = lax.axis_index("gz")
+    group_barrier(gz_peers() + tile_peers(tile_count)[1])
+    copies = exchange_gz(lambda peer: own_ref, held, send_a, recv_a)
+    held[gz] = own_ref[...]
+    for copy in copies:
+        copy.wait()
+    for s in range(GZ):
+        packed[s : s + 1, :] = held[s, 0:1, :]
+    copies = exchange_tiles(tile_count, packed, window_ref, send_b, recv_b)
+    window_ref[REACH] = packed[...]
+    for copy in copies:
+        copy.wait()
+
+
+def gather_conf(tile_count, conf_cols):
+    own = jnp.broadcast_to(conf_cols[None, :], (8,) + conf_cols.shape)
+    return pl.pallas_call(
+        functools.partial(conf_kernel, tile_count),
+        out_shape=jax.ShapeDtypeStruct((2 * REACH + 1,) + own.shape, own.dtype),
+        in_specs=[pl.BlockSpec(memory_space=pltpu.VMEM)],
+        out_specs=pl.BlockSpec(memory_space=pltpu.VMEM),
+        scratch_shapes=[
+            pltpu.VMEM((GZ,) + own.shape, own.dtype),
+            pltpu.VMEM(own.shape, own.dtype),
+            pltpu.SemaphoreType.DMA((GZ - 1,)),
+            pltpu.SemaphoreType.DMA((GZ - 1,)),
+            pltpu.SemaphoreType.DMA((2 * REACH,)),
+            pltpu.SemaphoreType.DMA((2 * REACH,)),
+        ],
+        compiler_params=pltpu.CompilerParams(collective_id=2, has_side_effects=True),
+    )(own)
+
+
+def spread_kernel(own_ref, out_ref, source, held, send, recv):
+    gz = lax.axis_index("gz")
+    group_barrier(gz_peers())
+    for s in range(GZ):
+        for r in range(2):
+            source[s, r : r + 1, :] = own_ref[r, s : s + 1, :]
+    copies = exchange_gz(lambda peer: source.at[peer], held, send, recv)
+    held[gz] = source[gz]
+    for copy in copies:
+        copy.wait()
+    for g in range(GZ):
+        out_ref[g % 2, 2 * (g // 2) : 2 * (g // 2) + 2, :] = held[g, 0:2, :]
+
+
+def spread_result(own):
+    columns = own.shape[-1]
+    return pl.pallas_call(
+        spread_kernel,
+        out_shape=jax.ShapeDtypeStruct((2, 8, columns), own.dtype),
+        in_specs=[pl.BlockSpec(memory_space=pltpu.VMEM)],
+        out_specs=pl.BlockSpec(memory_space=pltpu.VMEM),
+        scratch_shapes=[
+            pltpu.VMEM((GZ, 8, columns), own.dtype),
+            pltpu.VMEM((GZ, 8, columns), own.dtype),
+            pltpu.SemaphoreType.DMA((GZ - 1,)),
+            pltpu.SemaphoreType.DMA((GZ - 1,)),
+        ],
+        compiler_params=pltpu.CompilerParams(collective_id=3, has_side_effects=True),
+    )(own)
+
+
+def relax_kernel(total, place_ref, window_ref, conf_ref, out_ref, s_buf, a_buf, w_buf, n_buf, c_buf, u_buf):
+    tile, part = place_ref[0], place_ref[1]
+    start = tile * 8 + 2 * part - (ITERS - 1)
     rows = a_buf.shape[0]
-    total = spring_ref.shape[0]
     lane = lax.broadcasted_iota(jnp.int32, (1, 8, 128), 2)
     first_col, last_col = lane == 0, lane == 127
     section = lax.broadcasted_iota(jnp.int32, (8, 256), 0)
     u_buf[...] = jnp.zeros_like(u_buf)
 
-    def prepare(i, carry):
-        r = start + i
-        inside = (r >= 0) & (r < total)
-
-        @pl.when(inside)
-        def _():
-            conf = conf_ref[r // 8]
-            w = 0.15 * spring_ref[r].astype(jnp.float32) * conf
-            w = jnp.where(section == 0, 0.0, w)
-            f = flow_ref[0, r].astype(jnp.float32)
-            wf = w * f
-            wn = pltpu.roll(w, 7, 0)
-            c = wf - pltpu.roll(wf, 7, 0)
-            w_buf[i] = w
-            n_buf[i] = wn
-            a_buf[i] = 0.4 - w - wn
-            c_buf[i] = c
-            u_buf[0, i + GROUP] = c
-
-        @pl.when(jnp.logical_not(inside))
-        def _():
-            zero = jnp.zeros((8, 256), jnp.float32)
-            w_buf[i] = zero
-            n_buf[i] = zero
-            a_buf[i] = zero
-            c_buf[i] = zero
+    def picked(j):
+        return jnp.concatenate([s_buf[h, pl.ds(j, 8, stride=16), :] for h in range(2)], axis=1)
+
+    def prepare(k, carry):
+        at = tile + k - REACH
+        inside = (at >= 0) & (at < total // 8)
+        conf = conf_ref[k]
+        nodes = window_ref[k].astype(jnp.float32).reshape(128, 256)
+        s_buf[0], s_buf[1] = nodes[:, :128], nodes[:, 128:]
+        for j in range(8):
+            i = 8 * k + j - 2 * part - 1
+
+            @pl.when((i >= 0) & (i < rows) & inside)
+            def _():
+                w = 0.15 * picked(j) * conf
+                w = jnp.where(section == 0, 0.0, w)
+                wf = w * picked(8 + j)
+                wn = pltpu.roll(w, 7, 0)
+                c = wf - pltpu.roll(wf, 7, 0)
+                w_buf[i] = w
+                n_buf[i] = wn
+                a_buf[i] = 0.4 - w - wn
+                c_buf[i] = c
+                u_buf[0, i + GROUP] = c
+
+            @pl.when((i >= 0) & (i < rows) & jnp.logical_not(inside))
+            def _():
+                zero = jnp.zeros((8, 256), jnp.float32)
+                w_buf[i] = zero
+                n_buf[i] = zero
+                a_buf[i] = zero
+                c_buf[i] = zero
 
         return carry
 
-    lax.fori_loop(0, rows, prepare, 0)
+    lax.fori_loop(0, 2 * REACH + 1, prepare, 0)
 
     def step(source, target, s):
         low = (s - 1) // GROUP
@@ -141,25 +301,25 @@
     out_ref[...] = u_buf[1, pl.ds(63 + GROUP, 2)]
 
 
-def relax(start, component, spring, flow, conf):
+def relax(place, total, window, conf):
     rows = 2 * ITERS
     return pl.pallas_call(
-        relax_kernel,
+        functools.partial(relax_kernel, total),
         out_shape=jax.ShapeDtypeStruct((2, 8, 256), jnp.float32),
         grid_spec=pltpu.PrefetchScalarGridSpec(
             num_scalar_prefetch=1,
             grid=(1,),
             in_specs=[
-                pl.BlockSpec(spring.shape, lambda i, s: (0, 0, 0)),
-                pl.BlockSpec((1,) + flow.shape[1:], lambda i, s: (s[1], 0, 0, 0)),
+                pl.BlockSpec(window.shape, lambda i, s: (0, 0, 0, 0)),
                 pl.BlockSpec(conf.shape, lambda i, s: (0, 0, 0)),
             ],
             out_specs=pl.BlockSpec((2, 8, 256), lambda i, s: (0, 0, 0)),
-            scratch_shapes=[pltpu.VMEM((rows, 8, 256), jnp.float32)] * 4
+            scratch_shapes=[pltpu.VMEM((2, 128, 128), jnp.float32)]
+            + [pltpu.VMEM((rows, 8, 256), jnp.float32)] * 4
             + [pltpu.VMEM((2, rows + 2 * GROUP, 8, 256), jnp.float32)],
         ),
         compiler_params=pltpu.CompilerParams(vmem_limit_bytes=40 * 1024 * 1024),
-    )(jnp.stack([start, component]).astype(jnp.int32), spring, flow, conf)
+    )(place, window, conf)
 
 
 def on_device(patches, prior_patches, blocks, dest, target, flows, valid, stiffness):
@@ -168,12 +328,10 @@
     gz_index = lax.axis_index("gz")
     tile_index = lax.axis_index("tile")
 
-    spring = (stiffness * valid.astype(jnp.float32))[0].astype(jnp.bfloat16)
-    both = jnp.stack([spring, flows[0, 0].astype(jnp.bfloat16), flows[0, 1].astype(jnp.bfloat16)])
-    everywhere = lax.all_gather(both, ("tile", "gz"))
-    node_rows = flows.shape[2]
-    everywhere = everywhere.reshape(tile_count, 8, 3, node_rows, -1).transpose(2, 0, 3, 1, 4)
-    everywhere = everywhere.reshape(3, tile_count * node_rows, 8, -1)
+    node_rows, node_cols = flows.shape[2:]
+    spring = (stiffness * valid.astype(jnp.float32))[0]
+    own_nodes = jnp.stack([jnp.concatenate([spring, flows[0, c]]) for c in range(2)]).astype(jnp.bfloat16)
+    window = gather_springs(tile_count, own_nodes)
 
     shifted = from_behind(patches, "gz", 1)
     earlier = jnp.where(gz_index == 0, prior_patches[None], shifted)[0]
@@ -198,13 +356,10 @@
     peak = jnp.max(corr_maps.astype(jnp.float32), axis=-1)
     confidence = peak / (1.0 + peak)
 
-    all_conf = lax.all_gather(confidence, ("tile", "gz")).reshape(tile_count, 8, block_count)
-    node_cols = flows.shape[3]
-    conf_cols = jnp.repeat(all_conf, node_cols // block_count, axis=2)
-    start = tile_index * node_rows + 2 * (gz_index // 2) - (ITERS - 1)
-    mine = relax(start, gz_index % 2, everywhere[0], everywhere[1:], conf_cols)
-    swapped = lax.all_to_all(mine.transpose(1, 0, 2), "gz", split_axis=0, concat_axis=0, tiled=True)
-    mesh_nodes = swapped.reshape(4, 2, 2, node_cols).transpose(1, 0, 2, 3).reshape(1, 2, node_rows, node_cols)
+    conf_window = gather_conf(tile_count, jnp.repeat(confidence, node_cols // block_count))
+    place = jnp.stack([tile_index, gz_index // 2]).astype(jnp.int32)
+    mine = relax(place, tile_count * node_rows, window, conf_window)
+    mesh_nodes = spread_result(mine)[None]
     return (corr_maps[None], mesh_nodes)
 
 

time: 398 us -> 321 us (0.81)
  the two profiles are of different devices: /device:TPU:33 before, /device:TPU:1 now
where the time goes in v2:
time: 321 us; the launch traced here: 315 us
  Pallas kernels  177 us (55%)
  matrix products  52.6 us (16%)
  local copies, waits for them, and re-layouts  41.5 us (13%)
  starting transfers between devices  21.2 us (7%)
  other arithmetic  13 us (4%)
  waiting for transfers between devices  8.5 us (3%)
    pallas_call x1, Pallas kernels, gather_springs(): pl.pallas_call(functools.partial(gather_kernel, tile_count), out_shape=ja...  81.6 us
    pallas_call x1, Pallas kernels, relax(): pl.pallas_call(functools.partial(relax_kernel, total), out_shape=jax.Shap...  65.8 us
    dot_general x10, matrix products, left_mul(): jnp.einsum('jp,npk->njk', matrix_t, pixels, preferred_element_type=jnp.fl...  36 us
    pallas_call x1, Pallas kernels, gather_conf(): pl.pallas_call(functools.partial(conf_kernel, tile_count), out_shape=jax....  22.2 us
    dot_general x6, matrix products, right_mul(): jnp.einsum('npq,qk->npk', pixels, matrix_t, preferred_element_type=jnp.fl...  16.6 us
    all_to_all x1, starting transfers between devices, on_device(): lax.all_to_all(requested, 'tile', split_axis=0, concat_axis=0, tiled=True)  11.2 us
    all_to_all x1, waiting for transfers between devices, on_device(): lax.all_to_all(requested, 'tile', split_axis=0, concat_axis=0, tiled=True)  8.5 us
    gather x2, local copies, waits for them, and re-layouts, on_device(): jnp.take(arrived.reshape(tile_count * CAP, PIX), slot_index, axis=0)  8.44 us
  transfers between devices with their start and end apart: 3, of which 1 were waited for; matrix products, arithmetic and copies ran while one was open for 8% of the time, Pallas kernels for 26%

profile of v2, /device:TPU:1, one launch (start us, length us, event | category | flops | bytes accessed | tf_op | source)
XLA Modules:
  0.0 315.4 jit_solution(16940306829096403052)
XLA Ops:
  0.6 4.5 %collective-permute-start = (bf16[1,16,25600]{2,1,0:T(8,128)(2,1)}, bf16[1,16,25600]{2,1,0:T(8,128)(2,1)S(1)}, u32[]{:S(2)}, u32[]{:S(2)}) collective-permute-start(bf16[1,16,25600]{2,1,0:T(8,128)(2,1)} %param.8), channel_id=1, source_target_pairs={{0,32},{32,64},{64,96},{96,128},{128,160},{160,192},{192,224},{1,3... | collective-permute-start | bytes 2457608 | tf_op jit(solution)/shard_map/ppermute | solution.py:20
  5.1 0.7 fusion.50
  5.9 0.1 reduce_window_sum.11
  5.9 0.8 select_reduce_fusion.1
  6.8 0.7 compare_and_fusion.1
  7.4 0.7 select_reduce_fusion
  8.2 0.7 all_to_all.9
  8.9 11.2 %all-to-all-start = ((s32[32,1,2]{2,1,0:T(1,128)}), s32[32,1,2]{2,1,0:T(1,128)S(1)}, u32[]{:S(2)}, u32[]{:S(2)}) async-start(s32[32,1,2]{2,1,0:T(1,128)} %bitcast.2), calls=%async_computation | async-start | bytes 32768 | tf_op jit(solution)/shard_map/all_to_all | solution.py:349
  20.1 8.5 %all-to-all-done = s32[32,1,2]{2,1,0:T(1,128)S(1)} async-done(((s32[32,1,2]{2,1,0:T(1,128)}), s32[32,1,2]{2,1,0:T(1,128)S(1)}, u32[]{:S(2)}, u32[]{:S(2)}) %all-to-all-start) | async-done | bytes 288 | tf_op jit(solution)/shard_map/all_to_all | solution.py:349
  28.6 0.5 broadcast.160
  29.1 0.7 reduce.7
  29.8 0.1 reshape.159
  29.9 0.1 copy.50
  30.0 0.1 copy.51
  30.2 1.2 fusion.16
  31.4 4.3 %gather_fusion = bf16[64,25600]{1,0:T(8,128)(2,1)} fusion(bf16[16,25600]{1,0:T(8,128)(2,1)S(1)} %fusion.16, s32[1024]{0:T(1024)S(1)} %pad_clamp_fusion.1), kind=kCustom, calls=%fused_computation | custom fusion | bytes 6553856 | tf_op jit(solution)/shard_map/jit(_take)/gather | solution.py:350
  35.7 3.3 %gather.13 = bf16[32,2,25600]{2,1,0:T(2,128)(2,1)S(1)} reshape(bf16[64,25600]{1,0:T(8,128)(2,1)} %gather_fusion) | data formatting | bytes 6553600 | tf_op jit(solution)/shard_map/jit(_take)/gather | solution.py:350
  39.0 4.7 %broadcast_select_fusion = bf16[32,2,25600]{2,1,0:T(2,128)(2,1)} fusion(bf16[32,2,25600]{2,1,0:T(2,128)(2,1)S(1)} %gather.13, pred[32,2]{1,0:T(8,128)(4,1)S(1)} %copy.51), kind=kLoop, calls=%fused_computation.2 | loop fusion | flops 1638400 | bytes 6553664 | tf_op jit(solution)/shard_map/jit(_take)/select_n | solution.py:350
  43.7 5.5 %all-to-all-start.1 = ((bf16[32,2,25600]{2,1,0:T(2,128)(2,1)}), bf16[32,2,25600]{2,1,0:T(2,128)(2,1)}, u32[]{:S(2)}, u32[]{:S(2)}) async-start(bf16[32,2,25600]{2,1,0:T(2,128)(2,1)} %broadcast_select_fusion), calls=%async_computation.1 | async-start | bytes 6553600 | tf_op jit(solution)/shard_map/all_to_all | solution.py:351
  49.2 0.0 copy-start.8
  49.3 0.0 copy-start.9
  49.3 0.0 copy-start.10
  49.3 0.0 copy-start.11
  49.3 4.4 %reshape.161 = f32[32,160,160]{2,1,0:T(8,128)} reshape(bf16[1,32,25600]{2,1,0:T(8,128)(2,1)S(1)} %copy-done.4) | data formatting | bytes 4915200 | tf_op jit(solution)/shard_map/convert_element_type | solution.py:39
  53.8 0.6 pad_maximum_fusion.own_ref
  54.4 81.6 %shard_map.95.window_ref = bf16[17,8,16,256]{3,2,1,0:T(8,128)(2,1)} custom-call(bf16[2,16,256]{2,1,0:T(8,128)(2,1)} %pad_maximum_fusion.own_ref), custom_call_target="tpu_custom_call" | custom-call | bytes 8388608 | tf_op jit(solution)/shard_map/pallas_call | solution.py:140
  136.0 0.1 pad_add_fusion.place_ref
  136.1 0.3 convert_reduce_fusion.1
  136.5 0.8 fusion.7
  137.3 4.0 %convolution_convert_fusion.1 = bf16[32,160,160]{2,1,0:T(8,128)(2,1)S(1)} fusion(f32[32,160,160]{2,1,0:T(8,128)} %reshape.161, f32[32]{0:T(128)S(1)} %add_rsqrt_fusion, f32[32]{0:T(128)S(1)} %broadcast_multiply_fusion), kind=kOutput, calls=%fused_computation.34 | convolution fusion | flops 265676800 | bytes 4915456 | tf_op jit(solution)/shard_map/npq,qk->npk/dot_general | solution.py:31
  141.2 1.6 fusion.29
  142.9 1.6 fusion.44
  144.5 1.5 convolution_convert_fusion
  146.0 3.1 add_convert_fusion.1
  149.1 3.1 subtract_convert_fusion.1
  152.2 3.5 %reshape.160 = bf16[64,25600]{1,0:T(8,128)(2,1)S(1)} reshape(bf16[32,2,25600]{2,1,0:T(2,128)(2,1)} %all-to-all-done.1) | data formatting | bytes 6553600 | tf_op jit(solution)/shard_map/reshape | solution.py:353
  155.7 2.8 gather_fusion.1
  158.5 5.7 %gather.15 = bf16[32,160,160]{2,1,0:T(8,128)(2,1)} reshape(bf16[32,25600]{1,0:T(8,128)(2,1)} %gather_fusion.1) | data formatting | bytes 3276800 | tf_op jit(solution)/shard_map/jit(_take)/gather | solution.py:353
  164.2 0.7 convert_reduce_fusion
  164.8 0.8 fusion.5
  165.6 0.3 copy-done.7
  165.9 1.6 convolution_convert_fusion.3
  167.5 1.6 convolution_convert_fusion.2
  169.2 1.6 fusion.31
  170.8 1.6 fusion.47
  172.4 1.7 add_convert_fusion.2
  174.1 0.0 copy-done.5
  174.1 0.8 copy-done.6
  174.9 3.9 %fusion.10 = (bf16[32,160,160]{1,2,0:T(8,128)(2,1)S(1)}, bf16[32,160,160]{1,2,0:T(8,128)(2,1)S(1)}) fusion(bf16[32,160,160]{2,1,0:T(8,128)(2,1)S(1)} %copy-done.5, bf16[32,160,160]{2,1,0:T(8,128)(2,1)S(1)} %copy-done.6, bf16[32,160,160]{2,1,0:T(8,128)(2,1)S(1)} %add_convert_fusion.2, f32[32,160,160]{2,1,0:T(8,128)S(1)} %fusion.47, ...), kind=kOutput, calls=%fused_computation.29 | convolution fusion | flops 273868800 | bytes 13107200 | tf_op jit(solution)/shard_map/jp,npk->njk/dot_general | solution.py:35
  178.8 4.0 %fusion.40 = f32[32,160,160]{2,1,0:T(8,128)} fusion(bf16[32,160,160]{1,2,0:T(8,128)(2,1)S(1)} %get-tuple-element.5), kind=kOutput, calls=%fused_computation.55 | convolution fusion | flops 262400000 | bytes 4915200 | tf_op jit(solution)/shard_map/npq,qk->npk/dot_general | solution.py:31
  182.8 4.0 %fusion.25 = f32[32,160,160]{2,1,0:T(8,128)} fusion(bf16[32,160,160]{1,2,0:T(8,128)(2,1)S(1)} %get-tuple-element.5), kind=kOutput, calls=%fused_computation.52 | convolution fusion | flops 262400000 | bytes 4915200 | tf_op jit(solution)/shard_map/npq,qk->npk/dot_general | solution.py:31
  186.8 8.4 %fusion.8 = f32[32,160,160]{2,1,0:T(8,128)} fusion(f32[32,160,160]{2,1,0:T(8,128)} %fusion.40, bf16[32,160,160]{1,2,0:T(8,128)(2,1)S(1)} %get-tuple-element.4), kind=kOutput, calls=%fused_computation.27 | convolution fusion | flops 526438400 | bytes 8192000 | tf_op jit(solution)/shard_map/jp,npk->njk/dot_general | solution.py:35
  195.2 9.3 %fusion.110 = (bf16[32]{0:T(256)(128)(2,1)S(1)}, bf16[32,160,160]{2,1,0:T(8,128)(2,1)}) fusion(f32[32,160,160]{2,1,0:T(8,128)} %fusion.8, f32[32,160,160]{2,1,0:T(8,128)} %fusion.25, bf16[32,160,160]{1,2,0:T(8,128)(2,1)S(1)} %get-tuple-element.4), kind=kOutput, calls=%fused_computation.138 | convolution fusion | flops 529715168 | bytes 9830464 | tf_op jit(solution)/shard_map/jp,npk->njk/dot_general | solution.py:35
  204.5 4.8 %copy.66 = bf16[32,160,160]{2,1,0:T(8,128)(2,1)} copy(bf16[32,160,160]{1,2,0:T(8,128)(2,1)} %bitcast.91) | data formatting | bytes 3276800 | tf_op jit(solution)/shard_map/convert_element_type | solution.py:66
  209.3 6.5 %broadcast_in_dim_reshape.4 = bf16[1,32,25600]{2,1,0:T(8,128)(2,1)} reshape(bf16[32,160,160]{2,1,0:T(8,128)(2,1)} %copy.66) | data formatting | bytes 3276800 | tf_op jit(solution)/shard_map/broadcast_in_dim;reshape | solution.py:363
  215.8 0.1 broadcast_in_dim.73
  215.9 0.1 broadcast_in_dim.74
  216.0 0.6 broadcast_in_dim.75.own_ref
  216.6 22.2 %shard_map.96.conf_ref = f32[17,8,256]{2,1,0:T(8,128)} custom-call(f32[8,256]{1,0:T(8,128)} %broadcast_in_dim.75.own_ref), custom_call_target="tpu_custom_call" | custom-call | tf_op jit(solution)/shard_map/pallas_call | solution.py:175
  238.8 0.9 copy-done.1
  239.7 65.8 %shard_map.97.own_ref = f32[2,8,256]{2,1,0:T(8,128)S(1)} custom-call(s32[2]{0:T(128)S(1)} %pad_add_fusion.place_ref, bf16[17,8,16,256]{3,2,1,0:T(8,128)(2,1)S(1)} %copy-done, f32[17,8,256]{2,1,0:T(8,128)S(1)} %copy-done.1), custom_call_target="tpu_custom_call" | custom-call | tf_op jit(solution)/shard_map/pallas_call | solution.py:306
  305.5 0.6 copy-done.2
  306.1 7.6 %shard_map.98 = f32[2,8,256]{2,1,0:T(8,128)} custom-call(f32[2,8,256]{2,1,0:T(8,128)} %copy-done.2), custom_call_target="tpu_custom_call" | custom-call | tf_op jit(solution)/shard_map/pallas_call | solution.py:208
  313.8 1.3 copy.82
  (36 shorter events, 0.1 us)
Async XLA Ops:
  0.6 29.5 %collective-permute-start = (bf16[1,16,25600]{2,1,0:T(8,128)(2,1)}, bf16[1,16,25600]{2,1,0:T(8,128)(2,1)S(1)}, u32[]{:S(2)}, u32[]{:S(2)}) collective-permute-start(bf16[1,16,25600]{2,1,0:T(8,128)(2,1)} %param.8), channel_id=1, source_target_pairs={{0,32},{32,64},{64,96},{96,128},{128,160},{160,192},{192,224},{1,3... | collective-permute-start | bytes 2457608 | tf_op jit(solution)/shard_map/ppermute | solution.py:20
  8.9 19.7 %all-to-all-start = ((s32[32,1,2]{2,1,0:T(1,128)}), s32[32,1,2]{2,1,0:T(1,128)S(1)}, u32[]{:S(2)}, u32[]{:S(2)}) async-start(s32[32,1,2]{2,1,0:T(1,128)} %bitcast.2), calls=%async_computation | async-start | bytes 32768 | tf_op jit(solution)/shard_map/all_to_all | solution.py:349
  43.7 5.5 %copy-start.4 = (bf16[1,32,25600]{2,1,0:T(8,128)(2,1)S(1)}, bf16[1,32,25600]{2,1,0:T(8,128)(2,1)}, u32[]{:S(2)}) copy-start(bf16[1,32,25600]{2,1,0:T(8,128)(2,1)} %param.10) | copy-start | bytes 4915204
  43.7 108.5 %all-to-all-start.1 = ((bf16[32,2,25600]{2,1,0:T(2,128)(2,1)}), bf16[32,2,25600]{2,1,0:T(2,128)(2,1)}, u32[]{:S(2)}, u32[]{:S(2)}) async-start(bf16[32,2,25600]{2,1,0:T(2,128)(2,1)} %broadcast_select_fusion), calls=%async_computation.1 | async-start | bytes 6553600 | tf_op jit(solution)/shard_map/all_to_all | solution.py:351
  49.2 4.5 %copy-start.8 = (f32[1,2,8,256]{3,2,1,0:T(8,128)S(1)}, f32[1,2,8,256]{3,2,1,0:T(8,128)}, u32[]{:S(2)}) copy-start(f32[1,2,8,256]{3,2,1,0:T(8,128)} %param.13) | copy-start | bytes 49156
  49.3 4.5 %copy-start.9 = (f32[1,8,256]{2,1,0:T(8,128)S(1)}, f32[1,8,256]{2,1,0:T(8,128)}, u32[]{:S(2)}) copy-start(f32[1,8,256]{2,1,0:T(8,128)} %param.15) | copy-start | bytes 24580
  49.3 4.5 %copy-start.10 = (s32[1,8,256]{2,1,0:T(8,128)S(1)}, s32[1,8,256]{2,1,0:T(8,128)}, u32[]{:S(2)}) copy-start(s32[1,8,256]{2,1,0:T(8,128)} %param.14) | copy-start | bytes 24580
  49.3 86.8 %copy-start.11 = (s32[1,32,1]{1,2,0:T(1,128)S(1)}, s32[1,32,1]{1,2,0:T(1,128)}, u32[]{:S(2)}) copy-start(s32[1,32,1]{1,2,0:T(1,128)} %param.11) | copy-start | bytes 388
  141.2 3.2 %slice-start = ((s8[5242880]{0:T(1024)(128)(4,1)}), s8[4194304]{0:T(1024)(128)(4,1)S(1)}, s32[]{:S(2)}) async-start(s8[5242880]{0:T(1024)(128)(4,1)} %bitcast.89), calls=%async_computation.2 | async-start | bytes 8388608
  142.9 1.6 slice-start.1
  158.5 5.7 %copy-start.3 = (bf16[32,25600]{1,0:T(8,128)(2,1)S(1)}, bf16[32,25600]{1,0:T(8,128)(2,1)}, u32[]{:S(2)}) copy-start(bf16[32,25600]{1,0:T(8,128)(2,1)} %gather_fusion.1) | copy-start | bytes 4915204
  164.2 1.7 copy-start.7
  172.4 1.7 copy-start.5
  172.4 2.5 copy-start.6
  209.3 29.5 %copy-start = (bf16[17,8,16,256]{3,2,1,0:T(8,128)(2,1)S(1)}, bf16[17,8,16,256]{3,2,1,0:T(8,128)(2,1)}, u32[]{:S(2)}) copy-start(bf16[17,8,16,256]{3,2,1,0:T(8,128)(2,1)} %shard_map.95.window_ref) | copy-start | bytes 3342340
  238.8 0.9 copy-start.1
  305.5 0.6 copy-start.2

commit v3 on v2

--- a/solution.py
+++ b/solution.py
@@ -2,6 +2,8 @@
 
 import jax
 import jax.numpy as jnp
+import ml_dtypes
+import numpy as np
 from jax import lax
 from jax.experimental import pallas as pl
 from jax.experimental.pallas import tpu as pltpu
@@ -20,50 +22,238 @@
     return lax.ppermute(value, axis, [(source, source + steps) for source in range(first, last)])
 
 
-def dft_tables(edge_len):
-    positions = jnp.arange(edge_len, dtype=jnp.int32)
-    phase_idx = positions[:, None] * positions[None, :] % edge_len
-    angles = phase_idx.astype(jnp.float32) * (2.0 * jnp.pi / edge_len)
-    return (jnp.cos(angles).astype(jnp.bfloat16), jnp.sin(angles).astype(jnp.bfloat16))
-
-
-def right_mul(pixels, matrix_t):
-    return jnp.einsum("npq,qk->npk", pixels, matrix_t, preferred_element_type=jnp.float32)
-
-
-def left_mul(matrix_t, pixels):
-    return jnp.einsum("jp,npk->njk", matrix_t, pixels, preferred_element_type=jnp.float32)
-
-
-def normalized(pixel_rows):
-    values = pixel_rows.astype(jnp.float32)
-    centred = values - jnp.mean(values, axis=-1, keepdims=True)
-    spread = jnp.mean(centred * centred, axis=-1, keepdims=True)
-    return (centred * lax.rsqrt(spread + 1e-05)).astype(jnp.bfloat16)
-
-
-def spectrum(pixel_rows, cos_t, sin_t):
-    edge_len = cos_t.shape[0]
-    pixels = normalized(pixel_rows).reshape(pixel_rows.shape[0], edge_len, edge_len)
-    first_re = right_mul(pixels, cos_t).astype(jnp.bfloat16)
-    first_im = right_mul(pixels, sin_t).astype(jnp.bfloat16)
-    spec_re = (left_mul(cos_t, first_re) - left_mul(sin_t, first_im)).astype(jnp.bfloat16)
-    spec_im = (left_mul(sin_t, first_re) + left_mul(cos_t, first_im)).astype(jnp.bfloat16)
-    return (spec_re, spec_im)
-
-
-def correlate(spec_a, spec_b, cos_t, sin_t):
-    edge_len = cos_t.shape[0]
-    a_re = spec_a[0].astype(jnp.float32)
-    a_im = spec_a[1].astype(jnp.float32)
-    b_re = spec_b[0].astype(jnp.float32)
-    b_im = spec_b[1].astype(jnp.float32)
-    cross_re = (a_re * b_re + a_im * b_im).astype(jnp.bfloat16)
-    cross_im = (a_im * b_re - a_re * b_im).astype(jnp.bfloat16)
-    back_re = (right_mul(cross_re, cos_t) - right_mul(cross_im, sin_t)).astype(jnp.bfloat16)
-    back_im = (right_mul(cross_re, sin_t) + right_mul(cross_im, cos_t)).astype(jnp.bfloat16)
-    field_out = (left_mul(cos_t, back_re) - left_mul(sin_t, back_im)) * (1.0 / float(edge_len) ** 3)
-    return field_out.astype(jnp.bfloat16).reshape(cross_re.shape[0], edge_len * edge_len)
+LANES = 128
+HALF = 64
+WIRE = 208
+BATCH = 16
+
+
+def tables():
+    size = P_SIZE
+    line = np.arange(size)
+    angles = (np.outer(line, line) % size).astype(np.float32) * np.float32(2.0 * np.pi / size)
+    rounded = lambda x: x.astype(ml_dtypes.bfloat16).astype(np.float32)
+    cos_t, sin_t = rounded(np.cos(angles)), rounded(np.sin(angles))
+    lane = np.arange(2 * LANES)
+    column = HALF * (lane // LANES) + lane % HALF
+    used = column <= size // 2
+    column = np.where(used, column, 0)
+    real = lane % LANES < HALF
+    c, s = cos_t[:, column] * used, sin_t[:, column] * used
+    first = np.zeros((2 * LANES, 4 * LANES), np.float32)
+    first[:size, : 2 * LANES] = np.where(real, c, s)
+    first[:size, 2 * LANES :] = np.where(real, -s, c)
+    second = np.concatenate([cos_t, sin_t], axis=1)
+    third = np.concatenate([cos_t, sin_t], axis=0)
+    twice = np.where((column == 0) | (column == size // 2), 1.0, 2.0)
+    fourth = np.zeros((4 * LANES, 2 * LANES), np.float32)
+    fourth[: 2 * LANES, :size] = (np.where(real, c, -s) * twice).T
+    fourth[2 * LANES :, :size] = (np.where(real, -s, -c) * twice).T
+    return [jnp.asarray(x, jnp.bfloat16) for x in (first, second, third, fourth)]
+
+
+def to_images(rows_ref, low_buf, high_buf):
+    parts = PIX // 640
+    chunk = lambda m: rows_ref[:, pl.ds(pl.multiple_of(640 * m, LANES), 640)].astype(jnp.float32)
+    fold = lambda x: sum(x[:, LANES * k : LANES * k + LANES] for k in range(5))
+    zero = jnp.zeros((BATCH, LANES), jnp.float32)
+    sums = lax.fori_loop(0, parts, lambda m, t: t + fold(chunk(m)), zero)
+    mean = jnp.sum(sums, axis=1, keepdims=True) * (1.0 / PIX)
+
+    def square(m, t):
+        x = chunk(m) - mean
+        return t + fold(x * x)
+
+    sums = lax.fori_loop(0, parts, square, zero)
+    scale = lax.rsqrt(jnp.sum(sums, axis=1, keepdims=True) * (1.0 / PIX) + 1e-05)
+    lane = lax.broadcasted_iota(jnp.int32, (BATCH, LANES), 1)
+
+    def place(m, carry):
+        x = (chunk(m) - mean) * scale
+        t = [x[:, LANES * k : LANES * k + LANES] for k in range(5)]
+        low = [
+            t[0],
+            pltpu.roll(jnp.where(lane < 32, t[2], t[1]), 96, 1),
+            pltpu.roll(jnp.where(lane < 64, t[3], t[2]), 64, 1),
+            pltpu.roll(jnp.where(lane < 96, t[4], t[3]), 32, 1),
+        ]
+        high = [t[1], pltpu.roll(t[2], 96, 1), pltpu.roll(t[3], 64, 1), pltpu.roll(t[4], 32, 1)]
+        for k in range(4):
+            at = pl.ds(4 * m + k, BATCH, stride=P_SIZE)
+            low_buf[at, :] = low[k]
+            high_buf[at, :] = high[k]
+        return carry
+
+    lax.fori_loop(0, parts, place, 0)
+
+
+def image_spectrum(n, low_buf, high_buf, first_ref, second_ref):
+    at = pl.ds(pl.multiple_of(P_SIZE * n, 8), P_SIZE)
+    image = jnp.concatenate([low_buf[at, :], high_buf[at, :]], axis=1).astype(jnp.bfloat16)
+    first = jnp.dot(image, first_ref[...], preferred_element_type=jnp.float32).astype(jnp.bfloat16)
+    both = jnp.concatenate([first[:, : 2 * LANES], first[:, 2 * LANES :]], axis=0)
+    return jnp.dot(second_ref[...], both, preferred_element_type=jnp.float32)
+
+
+def block_kernel(rows_ref, first_ref, second_ref, out_ref, low_buf, high_buf):
+    to_images(rows_ref, low_buf, high_buf)
+    low_half = lax.broadcasted_iota(jnp.int32, (P_SIZE, LANES), 1) < HALF
+
+    def image(n, carry):
+        spec = image_spectrum(n, low_buf, high_buf, first_ref, second_ref)
+        for h in range(2):
+            x = spec[:, LANES * h : LANES * h + LANES]
+            swapped = pltpu.roll(x, HALF, 1)
+            out_ref[n, :, LANES * h : LANES * h + LANES] = jnp.where(low_half, x, swapped).astype(jnp.bfloat16)
+            at = slice(LANES * (2 + h), LANES * (3 + h))
+            out_ref[n, :, at] = jnp.where(low_half, swapped, -x).astype(jnp.bfloat16)
+        return carry
+
+    lax.fori_loop(0, BATCH, image, 0)
+
+
+def block_spectra(rows, first, second):
+    count = rows.shape[0]
+    fixed = lambda x: pl.BlockSpec(x.shape, lambda i: (0, 0))
+    return pl.pallas_call(
+        block_kernel,
+        out_shape=jax.ShapeDtypeStruct((count, P_SIZE, 4 * LANES), jnp.bfloat16),
+        grid=(count // BATCH,),
+        in_specs=[pl.BlockSpec((BATCH, PIX), lambda i: (i, 0)), fixed(first), fixed(second)],
+        out_specs=pl.BlockSpec((BATCH, P_SIZE, 4 * LANES), lambda i: (i, 0, 0)),
+        scratch_shapes=[pltpu.VMEM((BATCH * P_SIZE, LANES), jnp.float32)] * 2,
+        compiler_params=pltpu.CompilerParams(vmem_limit_bytes=40 * 1024 * 1024),
+        cost_estimate=pl.CostEstimate(flops=20_000_000_000, bytes_accessed=8_000_000, transcendentals=0),
+    )(rows, first, second)
+
+
+def patch_kernel(asked_ref, rows_ref, first_ref, second_ref, out_ref, low_buf, high_buf, wire_buf, sems):
+    to_images(rows_ref, low_buf, high_buf)
+    lane = lax.broadcasted_iota(jnp.int32, (8, LANES), 1) % HALF
+
+    def image(n, carry):
+        spec = image_spectrum(n, low_buf, high_buf, first_ref, second_ref)
+        rest = [spec[8 * i : 8 * i + 8, LANES:] for i in range(20)]
+        pieces = [spec[:, :LANES]]
+        for i in range(5):
+            pieces.append(sum(pltpu.roll(jnp.where(lane < 16, rest[5 * b + i], 0.0), 16 * b, 1) for b in range(4)))
+        pieces.append(sum(pltpu.roll(jnp.where(lane == 16, rest[i], 0.0), (i + 112) % LANES, 1) for i in range(20)))
+        wire_buf[n] = jnp.concatenate(pieces, axis=0).astype(jnp.bfloat16)
+        return carry
+
+    lax.fori_loop(0, BATCH, image, 0)
+    copy = lambda s: pltpu.make_async_copy(wire_buf.at[asked_ref[s]], out_ref.at[s], sems.at[s])
+    slots = out_ref.shape[0]
+
+    def begin(s, carry):
+        copy(s).start()
+        return carry
+
+    def finish(s, carry):
+        copy(s).wait()
+        return carry
+
+    lax.fori_loop(0, slots, begin, 0)
+    lax.fori_loop(0, slots, finish, 0)
+
+
+def patch_spectra(asked, rows, first, second):
+    slots = asked.shape[0]
+    fixed = lambda x: pl.BlockSpec(x.shape, lambda i, s: (0, 0))
+    return pl.pallas_call(
+        patch_kernel,
+        out_shape=jax.ShapeDtypeStruct((slots, WIRE, LANES), jnp.bfloat16),
+        grid_spec=pltpu.PrefetchScalarGridSpec(
+            num_scalar_prefetch=1,
+            grid=(1,),
+            in_specs=[fixed(rows), fixed(first), fixed(second)],
+            out_specs=pl.BlockSpec(memory_space=pl.ANY),
+            scratch_shapes=[pltpu.VMEM((BATCH * P_SIZE, LANES), jnp.float32)] * 2
+            + [pltpu.VMEM((BATCH, WIRE, LANES), jnp.bfloat16), pltpu.SemaphoreType.DMA((slots,))],
+        ),
+        compiler_params=pltpu.CompilerParams(vmem_limit_bytes=40 * 1024 * 1024),
+        cost_estimate=pl.CostEstimate(flops=10_000_000_000, bytes_accessed=8_000_000, transcendentals=0),
+    )(asked, rows, first, second)
+
+
+def match_kernel(slot_ref, wire_ref, block_ref, third_ref, fourth_ref, map_ref, peak_ref, low_buf, high_buf):
+    step = pl.program_id(0)
+    lane8 = lax.broadcasted_iota(jnp.int32, (8, LANES), 1) % HALF == 16
+
+    def image(n, carry):
+        wire = wire_ref[slot_ref[BATCH * step + n]].astype(jnp.float32)
+        last = wire[200:208]
+        rest = []
+        for i in range(20):
+            part = wire[160 + 8 * (i % 5) : 168 + 8 * (i % 5)]
+            part = pltpu.roll(part, (LANES - 16 * (i // 5)) % LANES, 1)
+            rest.append(jnp.where(lane8, pltpu.roll(last, (16 - i) % LANES, 1), part))
+        cross = []
+        for h, a in enumerate((wire[:P_SIZE], jnp.concatenate(rest, axis=0))):
+            straight = block_ref[n, :, LANES * h : LANES * h + LANES].astype(jnp.float32)
+            swapped = block_ref[n, :, LANES * (2 + h) : LANES * (3 + h)].astype(jnp.float32)
+            cross.append((a * straight + pltpu.roll(a, HALF, 1) * swapped).astype(jnp.bfloat16))
+        back = jnp.dot(third_ref[...], jnp.concatenate(cross, axis=1), preferred_element_type=jnp.float32)
+        back = back.astype(jnp.bfloat16)
+        back = jnp.concatenate([back[:P_SIZE], back[P_SIZE:]], axis=1)
+        field = jnp.dot(back, fourth_ref[...], preferred_element_type=jnp.float32) * (1.0 / float(P_SIZE) ** 3)
+        at = pl.ds(pl.multiple_of(P_SIZE * n, 8), P_SIZE)
+        low_buf[at, :] = field[:, :LANES]
+        high_buf[at, :] = field[:, LANES:]
+        return carry
+
+    lax.fori_loop(0, BATCH, image, 0)
+    lane = lax.broadcasted_iota(jnp.int32, (BATCH, LANES), 1)
+
+    def place(m, top):
+        load = lambda buf, k: buf[pl.ds(4 * m + k, BATCH, stride=P_SIZE), :]
+        low = [load(low_buf, 0)] + [pltpu.roll(load(low_buf, k), 32 * k, 1) for k in range(1, 4)]
+        high = [load(high_buf, 0)] + [pltpu.roll(load(high_buf, k), 32 * k, 1) for k in range(1, 4)]
+        tiles = [
+            low[0],
+            jnp.where(lane < 32, high[0], low[1]),
+            jnp.where(lane < 32, low[1], jnp.where(lane < 64, high[1], low[2])),
+            jnp.where(lane < 64, low[2], jnp.where(lane < 96, high[2], low[3])),
+            jnp.where(lane < 96, low[3], high[3]),
+        ]
+        rows = jnp.concatenate(tiles, axis=1).astype(jnp.bfloat16)
+        map_ref[:, pl.ds(pl.multiple_of(640 * m, LANES), 640)] = rows
+        for tile in tiles:
+            top = jnp.maximum(top, tile)
+        return top
+
+    top = lax.fori_loop(0, P_SIZE // 4, place, jnp.full((BATCH, LANES), -jnp.inf, jnp.float32))
+    top = jnp.max(top, axis=1, keepdims=True).astype(jnp.bfloat16).astype(jnp.float32)
+    peak_ref[...] = jnp.broadcast_to(top, (BATCH, LANES))
+
+
+def match(slot_index, wire, block_spec, third, fourth):
+    count = block_spec.shape[0]
+    fixed = lambda x: pl.BlockSpec(x.shape, lambda i, s: (0,) * x.ndim)
+    return pl.pallas_call(
+        match_kernel,
+        out_shape=(
+            jax.ShapeDtypeStruct((count, PIX), jnp.bfloat16),
+            jax.ShapeDtypeStruct((count, LANES), jnp.float32),
+        ),
+        grid_spec=pltpu.PrefetchScalarGridSpec(
+            num_scalar_prefetch=1,
+            grid=(count // BATCH,),
+            in_specs=[
+                fixed(wire),
+                pl.BlockSpec((BATCH, P_SIZE, 4 * LANES), lambda i, s: (i, 0, 0)),
+                fixed(third),
+                fixed(fourth),
+            ],
+            out_specs=[
+                pl.BlockSpec((BATCH, PIX), lambda i, s: (i, 0)),
+                pl.BlockSpec((BATCH, LANES), lambda i, s: (i, 0)),
+            ],
+            scratch_shapes=[pltpu.VMEM((BATCH * P_SIZE, LANES), jnp.float32)] * 2,
+        ),
+        compiler_params=pltpu.CompilerParams(vmem_limit_bytes=48 * 1024 * 1024),
+        cost_estimate=pl.CostEstimate(flops=20_000_000_000, bytes_accessed=10_000_000, transcendentals=0),
+    )(slot_index, wire, block_spec, third, fourth)
 
 
 MESH = pl.DeviceIdType.MESH
@@ -155,8 +345,14 @@
     )(own)
 
 
-def conf_kernel(tile_count, own_ref, window_ref, held, packed, send_a, recv_a, send_b, recv_b):
+def conf_kernel(tile_count, peak_ref, window_ref, own_ref, held, packed, send_a, recv_a, send_b, recv_b):
     gz = lax.axis_index("gz")
+    count, columns = peak_ref.shape[0], own_ref.shape[1]
+    peak = jnp.concatenate([peak_ref[...]] * (columns // LANES), axis=1)
+    block = lax.broadcasted_iota(jnp.int32, (count, columns), 1) // (columns // count)
+    mine = block == lax.broadcasted_iota(jnp.int32, (count, columns), 0)
+    confidence = jnp.sum(jnp.where(mine, peak / (1.0 + peak), 0.0), axis=0, keepdims=True)
+    own_ref[...] = jnp.broadcast_to(confidence, own_ref.shape)
     group_barrier(gz_peers() + tile_peers(tile_count)[1])
     copies = exchange_gz(lambda peer: own_ref, held, send_a, recv_a)
     held[gz] = own_ref[...]
@@ -170,14 +366,15 @@
         copy.wait()
 
 
-def gather_conf(tile_count, conf_cols):
-    own = jnp.broadcast_to(conf_cols[None, :], (8,) + conf_cols.shape)
+def gather_conf(tile_count, peaks, columns):
+    own = jax.ShapeDtypeStruct((8, columns), jnp.float32)
     return pl.pallas_call(
         functools.partial(conf_kernel, tile_count),
         out_shape=jax.ShapeDtypeStruct((2 * REACH + 1,) + own.shape, own.dtype),
         in_specs=[pl.BlockSpec(memory_space=pltpu.VMEM)],
         out_specs=pl.BlockSpec(memory_space=pltpu.VMEM),
         scratch_shapes=[
+            pltpu.VMEM(own.shape, own.dtype),
             pltpu.VMEM((GZ,) + own.shape, own.dtype),
             pltpu.VMEM(own.shape, own.dtype),
             pltpu.SemaphoreType.DMA((GZ - 1,)),
@@ -186,7 +383,7 @@
             pltpu.SemaphoreType.DMA((2 * REACH,)),
         ],
         compiler_params=pltpu.CompilerParams(collective_id=2, has_side_effects=True),
-    )(own)
+    )(peaks)
 
 
 def spread_kernel(own_ref, out_ref, source, held, send, recv):
@@ -323,7 +520,7 @@
 
 
 def on_device(patches, prior_patches, blocks, dest, target, flows, valid, stiffness):
-    cos_t, sin_t = dft_tables(P_SIZE)
+    first, second, third, fourth = tables()
     tile_count = lax.axis_size("tile")
     gz_index = lax.axis_index("gz")
     tile_index = lax.axis_index("tile")
@@ -347,16 +544,13 @@
     slot_picks = slot_index[:, None] == slot_ids[None, :]
     requested = jnp.sum(jnp.where(slot_picks, wanted[:, None], 0), axis=0).reshape(tile_count, CAP)
     asked_rows = lax.all_to_all(requested, "tile", split_axis=0, concat_axis=0, tiled=True)
-    outgoing = jnp.take(earlier, asked_rows.reshape(-1), axis=0).reshape(tile_count, CAP, PIX)
+    outgoing = patch_spectra(asked_rows.reshape(-1), earlier, first, second)
+    outgoing = outgoing.reshape(tile_count, CAP * WIRE, LANES)
     arrived = lax.all_to_all(outgoing, "tile", split_axis=0, concat_axis=0, tiled=True)
-    spec_b = spectrum(own_blocks, cos_t, sin_t)
-    chosen = jnp.take(arrived.reshape(tile_count * CAP, PIX), slot_index, axis=0)
-    spec_a = spectrum(chosen, cos_t, sin_t)
-    corr_maps = correlate(spec_a, spec_b, cos_t, sin_t)
-    peak = jnp.max(corr_maps.astype(jnp.float32), axis=-1)
-    confidence = peak / (1.0 + peak)
-
-    conf_window = gather_conf(tile_count, jnp.repeat(confidence, node_cols // block_count))
+    block_spec = block_spectra(own_blocks, first, second)
+    corr_maps, peaks = match(slot_index, arrived.reshape(tile_count * CAP, WIRE, LANES), block_spec, third, fourth)
+
+    conf_window = gather_conf(tile_count, peaks, node_cols)
     place = jnp.stack([tile_index, gz_index // 2]).astype(jnp.int32)
     mine = relax(place, tile_count * node_rows, window, conf_window)
     mesh_nodes = spread_result(mine)[None]

time: 321 us -> 313 us (0.975)
  the two profiles are of different devices: /device:TPU:1 before, /device:TPU:33 now
where the time goes in v3:
time: 313 us; the launch traced here: 310 us
  Pallas kernels  257 us (82%)
  starting transfers between devices  19.5 us (6%)
  local copies, waits for them, and re-layouts  18.7 us (6%)
  waiting for transfers between devices  7.63 us (2%)
  other arithmetic  6.41 us (2%)
    pallas_call x1, Pallas kernels, gather_springs(): pl.pallas_call(functools.partial(gather_kernel, tile_count), out_shape=ja...  93.7 us
    pallas_call x1, Pallas kernels, relax(): pl.pallas_call(functools.partial(relax_kernel, total), out_shape=jax.Shap...  66.1 us
    pallas_call x1, Pallas kernels, match(): pl.pallas_call(match_kernel, out_shape=(jax.ShapeDtypeStruct((count, PIX)...  27 us
    pallas_call x1, Pallas kernels, block_spectra(): pl.pallas_call(block_kernel, out_shape=jax.ShapeDtypeStruct((count, P_SIZ...  26.8 us
    pallas_call x1, Pallas kernels, patch_spectra(): pl.pallas_call(patch_kernel, out_shape=jax.ShapeDtypeStruct((slots, WIRE,...  19.9 us
    unnamed x33, local copies, waits for them, and re-layouts  17.4 us
    pallas_call x1, Pallas kernels, gather_conf(): pl.pallas_call(functools.partial(conf_kernel, tile_count), out_shape=jax....  15.9 us
    all_to_all x1, starting transfers between devices, on_device(): lax.all_to_all(requested, 'tile', split_axis=0, concat_axis=0, tiled=True)  10.8 us
  transfers between devices with their start and end apart: 3, of which 1 were waited for; matrix products, arithmetic and copies ran while one was open for 2% of the time, Pallas kernels for 39%

profile of v3, /device:TPU:33, one launch (start us, length us, event | category | flops | bytes accessed | tf_op | source)
XLA Modules:
  0.0 310.5 jit_solution(4027353672427509645)
XLA Ops:
  0.6 3.7 %collective-permute-start = (bf16[1,16,25600]{2,1,0:T(8,128)(2,1)}, bf16[1,16,25600]{2,1,0:T(8,128)(2,1)S(1)}, u32[]{:S(2)}, u32[]{:S(2)}) collective-permute-start(bf16[1,16,25600]{2,1,0:T(8,128)(2,1)} %param.12), channel_id=1, source_target_pairs={{0,32},{32,64},{64,96},{96,128},{128,160},{160,192},{192,224},{1,3... | collective-permute-start | bytes 2457608 | tf_op jit(solution)/shard_map/ppermute | solution.py:22
  4.3 0.7 fusion.1
  5.0 0.1 reduce_window_sum.11
  5.1 0.8 select_reduce_fusion.1
  5.9 0.7 multiply_add_fusion.slot_ref
  6.6 0.7 select_reduce_fusion
  7.3 0.7 all_to_all.9
  8.1 10.8 %all-to-all-start = ((s32[32,1,2]{2,1,0:T(1,128)}), s32[32,1,2]{2,1,0:T(1,128)S(1)}, u32[]{:S(2)}, u32[]{:S(2)}) async-start(s32[32,1,2]{2,1,0:T(1,128)} %bitcast.2), calls=%async_computation | async-start | bytes 32768 | tf_op jit(solution)/shard_map/all_to_all | solution.py:546
  18.9 7.6 %all-to-all-done = s32[32,1,2]{2,1,0:T(1,128)S(1)} async-done(((s32[32,1,2]{2,1,0:T(1,128)}), s32[32,1,2]{2,1,0:T(1,128)S(1)}, u32[]{:S(2)}, u32[]{:S(2)}) %all-to-all-start) | async-done | bytes 288 | tf_op jit(solution)/shard_map/all_to_all | solution.py:546
  26.5 0.5 broadcast.13
  27.0 0.7 reduce.3
  27.7 0.1 reshape.28.asked_ref
  27.8 0.0 collective-permute-done
  27.8 1.3 fusion.rows_ref
  29.1 0.0 copy-start.9
  29.1 0.9 copy-done.9
  30.1 0.0 copy-start.12
  30.1 0.9 copy-done.12
  31.0 19.9 %shard_map.131 = bf16[64,208,128]{2,1,0:T(8,128)(2,1)S(1)} custom-call(s32[64]{0:T(128)S(1)} %reshape.28.asked_ref, bf16[16,25600]{1,0:T(8,128)(2,1)S(1)} %fusion.rows_ref, bf16[256,512]{1,0:T(8,128)(2,1)S(1)} %copy-done.9, bf16[160,320]{1,0:T(8,128)(2,1)S(1)} %copy-done.12), custom_call_target="tpu_custom_call" | custom-call | flops 10000000000 | bytes 8000000 | tf_op jit(solution)/shard_map/pallas_call | solution.py:163
  50.8 0.0 copy-start.3
  50.8 1.8 copy-done.3
  52.6 0.0 copy-start.15
  52.6 0.0 copy-start.13
  52.6 5.0 %all-to-all-start.1 = ((bf16[32,416,128]{2,1,0:T(8,128)(2,1)}), bf16[32,416,128]{2,1,0:T(8,128)(2,1)S(1)}, u32[]{:S(2)}, u32[]{:S(2)}) async-start(bf16[32,416,128]{2,1,0:T(8,128)(2,1)} %bitcast.28), calls=%async_computation.1 | async-start | bytes 6815744 | tf_op jit(solution)/shard_map/all_to_all | solution.py:549
  57.6 0.0 copy-done.15
  57.7 0.7 fusion.4
  58.4 0.6 pad_maximum_fusion.own_ref
  59.0 93.7 %shard_map.134.window_ref = bf16[17,8,16,256]{3,2,1,0:T(8,128)(2,1)} custom-call(bf16[2,16,256]{2,1,0:T(8,128)(2,1)} %pad_maximum_fusion.own_ref), custom_call_target="tpu_custom_call" | custom-call | bytes 8388608 | tf_op jit(solution)/shard_map/pallas_call | solution.py:330
  152.7 0.1 pad_add_fusion.place_ref
  152.8 0.0 copy-done.13
  152.8 0.0 copy-start.7
  152.8 1.4 copy-done.7
  154.2 0.0 copy-start.10
  154.2 0.9 copy-done.10
  155.2 26.8 %shard_map.132.block_ref = bf16[32,160,512]{2,1,0:T(8,128)(2,1)S(1)} custom-call(bf16[32,25600]{1,0:T(8,128)(2,1)S(1)} %bitcast.29, bf16[256,512]{1,0:T(8,128)(2,1)S(1)} %copy-done.10, bf16[160,320]{1,0:T(8,128)(2,1)S(1)} %copy-done.13), custom_call_target="tpu_custom_call" | custom-call | flops 20000000000 | bytes 8000000 | tf_op jit(solution)/shard_map/pallas_call | solution.py:118
  182.0 0.0 copy-start.14
  182.0 2.3 copy-done.14
  184.3 0.0 all-to-all-done.1
  184.3 0.0 copy-start.1
  184.3 1.8 copy-done.1
  186.1 0.0 copy-start.2
  186.1 2.0 copy-done.2
  188.0 0.0 copy-start.8
  188.0 0.9 copy-done.8
  189.0 0.0 copy-start.11
  189.0 0.9 copy-done.11
  189.9 0.0 copy-start
  189.9 27.0 %shard_map.133 = (bf16[32,25600]{1,0:T(8,128)(2,1)}, f32[32,128]{1,0:T(8,128)S(1)}) custom-call(s32[32]{0:T(128)S(1)} %multiply_add_fusion.slot_ref, bf16[64,208,128]{2,1,0:T(8,128)(2,1)S(1)} %bitcast.27, bf16[32,160,512]{2,1,0:T(8,128)(2,1)} %copy-done.14, bf16[320,160]{1,0:T(8,128)(2,1)S(1)} %copy-done.11, bf16[512,256]{1,0:T(8,128)(2,1)S(1)} %copy-done.8), custom_call_target="tpu_custom_call" | custom-call | flops 20000000000 | bytes 10000000 | tf_op jit(solution)/shard_map/pallas_call | solution.py:233
  216.9 0.0 copy-start.6
  216.9 0.6 copy-done.6
  217.5 15.9 %shard_map.135.conf_ref = f32[17,8,256]{2,1,0:T(8,128)} custom-call(f32[32,128]{1,0:T(8,128)} %copy-done.6), custom_call_target="tpu_custom_call" | custom-call | tf_op jit(solution)/shard_map/pallas_call | solution.py:371
  233.4 0.0 copy-done
  233.4 0.0 copy-start.4
  233.4 0.9 copy-done.4
  234.3 66.1 %shard_map.136.own_ref = f32[2,8,256]{2,1,0:T(8,128)S(1)} custom-call(s32[2]{0:T(128)S(1)} %pad_add_fusion.place_ref, bf16[17,8,16,256]{3,2,1,0:T(8,128)(2,1)S(1)} %copy-done, f32[17,8,256]{2,1,0:T(8,128)S(1)} %copy-done.4), custom_call_target="tpu_custom_call" | custom-call | tf_op jit(solution)/shard_map/pallas_call | solution.py:503
  300.4 0.0 copy-start.5
  300.4 0.6 copy-done.5
  301.0 8.1 %shard_map.137 = f32[2,8,256]{2,1,0:T(8,128)} custom-call(f32[2,8,256]{2,1,0:T(8,128)} %copy-done.5), custom_call_target="tpu_custom_call" | custom-call | tf_op jit(solution)/shard_map/pallas_call | solution.py:405
  309.2 1.3 copy.17
  (3 shorter events, 0.0 us)
Async XLA Ops:
  0.6 27.2 %collective-permute-start = (bf16[1,16,25600]{2,1,0:T(8,128)(2,1)}, bf16[1,16,25600]{2,1,0:T(8,128)(2,1)S(1)}, u32[]{:S(2)}, u32[]{:S(2)}) collective-permute-start(bf16[1,16,25600]{2,1,0:T(8,128)(2,1)} %param.12), channel_id=1, source_target_pairs={{0,32},{32,64},{64,96},{96,128},{128,160},{160,192},{192,224},{1,3... | collective-permute-start | bytes 2457608 | tf_op jit(solution)/shard_map/ppermute | solution.py:22
  8.1 18.4 %all-to-all-start = ((s32[32,1,2]{2,1,0:T(1,128)}), s32[32,1,2]{2,1,0:T(1,128)S(1)}, u32[]{:S(2)}, u32[]{:S(2)}) async-start(s32[32,1,2]{2,1,0:T(1,128)} %bitcast.2), calls=%async_computation | async-start | bytes 32768 | tf_op jit(solution)/shard_map/all_to_all | solution.py:546
  29.1 1.0 copy-start.9
  30.1 0.9 copy-start.12
  50.8 1.8 copy-start.3
  52.6 5.0 %copy-start.15 = (f32[1,2,8,256]{3,2,1,0:T(8,128)S(1)}, f32[1,2,8,256]{3,2,1,0:T(8,128)}, u32[]{:S(2)}) copy-start(f32[1,2,8,256]{3,2,1,0:T(8,128)} %param.17) | copy-start | bytes 49156
  52.6 100.2 %copy-start.13 = (bf16[160,320]{1,0:T(8,128)(2,1)S(1)}, bf16[160,320]{1,0:T(8,128)(2,1)}, u32[]{:S(2)}) copy-start(bf16[160,320]{1,0:T(8,128)(2,1)} %constant.39.clone.second_ref) | copy-start | bytes 307204
  52.6 131.6 %all-to-all-start.1 = ((bf16[32,416,128]{2,1,0:T(8,128)(2,1)}), bf16[32,416,128]{2,1,0:T(8,128)(2,1)S(1)}, u32[]{:S(2)}, u32[]{:S(2)}) async-start(bf16[32,416,128]{2,1,0:T(8,128)(2,1)} %bitcast.28), calls=%async_computation.1 | async-start | bytes 6815744 | tf_op jit(solution)/shard_map/all_to_all | solution.py:549
  152.8 1.4 copy-start.7
  154.2 0.9 copy-start.10
  182.0 2.3 copy-start.14
  184.3 1.8 copy-start.1
  186.1 2.0 copy-start.2
  188.0 0.9 copy-start.8
  189.0 0.9 copy-start.11
  189.9 43.5 %copy-start = (bf16[17,8,16,256]{3,2,1,0:T(8,128)(2,1)S(1)}, bf16[17,8,16,256]{3,2,1,0:T(8,128)(2,1)}, u32[]{:S(2)}) copy-start(bf16[17,8,16,256]{3,2,1,0:T(8,128)(2,1)} %shard_map.134.window_ref) | copy-start | bytes 3342340
  216.9 0.6 copy-start.6
  233.4 0.9 copy-start.4
  300.4 0.6 copy-start.5

commit v4 on v3

--- a/solution.py
+++ b/solution.py
@@ -13,7 +13,8 @@
 PIX = 25600
 CAP = 2
 ITERS = 64
-GROUP = 8
+GROUP = 4
+UNROLL = 8
 
 
 def from_behind(value, axis, steps):
@@ -109,7 +110,7 @@
             out_ref[n, :, at] = jnp.where(low_half, swapped, -x).astype(jnp.bfloat16)
         return carry
 
-    lax.fori_loop(0, BATCH, image, 0)
+    lax.fori_loop(0, BATCH, image, 0, unroll=UNROLL)
 
 
 def block_spectra(rows, first, second):
@@ -141,7 +142,7 @@
         wire_buf[n] = jnp.concatenate(pieces, axis=0).astype(jnp.bfloat16)
         return carry
 
-    lax.fori_loop(0, BATCH, image, 0)
+    lax.fori_loop(0, BATCH, image, 0, unroll=UNROLL)
     copy = lambda s: pltpu.make_async_copy(wire_buf.at[asked_ref[s]], out_ref.at[s], sems.at[s])
     slots = out_ref.shape[0]
 
@@ -202,7 +203,7 @@
         high_buf[at, :] = field[:, LANES:]
         return carry
 
-    lax.fori_loop(0, BATCH, image, 0)
+    lax.fori_loop(0, BATCH, image, 0, unroll=UNROLL)
     lane = lax.broadcasted_iota(jnp.int32, (BATCH, LANES), 1)
 
     def place(m, top):
@@ -309,47 +310,68 @@
     return copies
 
 
-def gather_kernel(tile_count, own_ref, window_ref, held, local, send_a, recv_a, send_b, recv_b):
-    gz = lax.axis_index("gz")
-    group_barrier(gz_peers() + tile_peers(tile_count)[1])
+def ask_kernel(tile_count, request_ref, own_ref, asked_ref, window_ref, held, local, send_r, recv_r, send_a, recv_a, send_b, recv_b):
+    gz, tile = lax.axis_index("gz"), lax.axis_index("tile")
+    others = [(gz, lax.rem(tile + d, tile_count)) for d in range(1, tile_count)]
+    group_barrier(gz_peers() + others)
     copies = exchange_gz(lambda peer: own_ref.at[lax.rem(peer, 2)], held, send_a, recv_a)
     mine = pltpu.make_async_copy(own_ref.at[lax.rem(gz, 2)], held.at[gz], local.at[0])
     mine.start()
+    requests = []
+    for d, peer in enumerate(others):
+        requests.append(
+            pltpu.make_async_remote_copy(
+                src_ref=request_ref.at[peer[1]], dst_ref=asked_ref.at[tile], send_sem=send_r.at[d],
+                recv_sem=recv_r.at[d], device_id=peer, device_id_type=MESH,
+            )
+        )
+        requests[-1].start()
+    asked_ref[tile] = request_ref[tile]
     mine.wait()
     for copy in copies:
         copy.wait()
     copies = exchange_tiles(tile_count, held, window_ref, send_b, recv_b)
     mine = pltpu.make_async_copy(held, window_ref.at[REACH], local.at[1])
     mine.start()
+    for copy in requests:
+        copy.wait()
     mine.wait()
     for copy in copies:
         copy.wait()
 
 
-def gather_springs(tile_count, own):
-    return pl.pallas_call(
-        functools.partial(gather_kernel, tile_count),
-        out_shape=jax.ShapeDtypeStruct((2 * REACH + 1, GZ) + own.shape[1:], own.dtype),
-        in_specs=[pl.BlockSpec(memory_space=pltpu.VMEM)],
-        out_specs=pl.BlockSpec(memory_space=pl.ANY),
+def ask_and_gather(request, own):
+    tile_count = request.shape[0]
+    dma = lambda count: pltpu.SemaphoreType.DMA((count,))
+    return pl.pallas_call(
+        functools.partial(ask_kernel, tile_count),
+        out_shape=(
+            jax.ShapeDtypeStruct(request.shape, request.dtype),
+            jax.ShapeDtypeStruct((2 * REACH + 1, GZ) + own.shape[1:], own.dtype),
+        ),
+        in_specs=[pl.BlockSpec(memory_space=pltpu.VMEM)] * 2,
+        out_specs=(pl.BlockSpec(memory_space=pltpu.VMEM), pl.BlockSpec(memory_space=pl.ANY)),
         scratch_shapes=[
             pltpu.VMEM((GZ,) + own.shape[1:], own.dtype),
-            pltpu.SemaphoreType.DMA((2,)),
-            pltpu.SemaphoreType.DMA((GZ - 1,)),
-            pltpu.SemaphoreType.DMA((GZ - 1,)),
-            pltpu.SemaphoreType.DMA((2 * REACH,)),
-            pltpu.SemaphoreType.DMA((2 * REACH,)),
+            dma(2),
+            dma(tile_count - 1),
+            dma(tile_count - 1),
+            dma(GZ - 1),
+            dma(GZ - 1),
+            dma(2 * REACH),
+            dma(2 * REACH),
         ],
         compiler_params=pltpu.CompilerParams(collective_id=1, has_side_effects=True),
-        cost_estimate=pl.CostEstimate(flops=0, bytes_accessed=8 * 1024 * 1024, transcendentals=0),
-    )(own)
+        cost_estimate=pl.CostEstimate(flops=0, bytes_accessed=32 * 1024 * 1024, transcendentals=0),
+    )(request, own)
 
 
 def conf_kernel(tile_count, peak_ref, window_ref, own_ref, held, packed, send_a, recv_a, send_b, recv_b):
     gz = lax.axis_index("gz")
     count, columns = peak_ref.shape[0], own_ref.shape[1]
     peak = jnp.concatenate([peak_ref[...]] * (columns // LANES), axis=1)
-    block = lax.broadcasted_iota(jnp.int32, (count, columns), 1) // (columns // count)
+    half = columns // 2
+    block = lax.rem(lax.broadcasted_iota(jnp.int32, (count, columns), 1), half) // (half // count)
     mine = block == lax.broadcasted_iota(jnp.int32, (count, columns), 0)
     confidence = jnp.sum(jnp.where(mine, peak / (1.0 + peak), 0.0), axis=0, keepdims=True)
     own_ref[...] = jnp.broadcast_to(confidence, own_ref.shape)
@@ -396,8 +418,19 @@
     held[gz] = source[gz]
     for copy in copies:
         copy.wait()
-    for g in range(GZ):
-        out_ref[g % 2, 2 * (g // 2) : 2 * (g // 2) + 2, :] = held[g, 0:2, :]
+    columns = own_ref.shape[2]
+    order = lax.broadcasted_iota(jnp.int32, (columns, columns), 1)
+    order = order // 2 + lax.rem(order, 2) * (columns // 2)
+    spot = lax.broadcasted_iota(jnp.int32, (columns, columns), 0) == order
+    pick = jnp.where(spot, 1.0, 0.0).astype(jnp.bfloat16)
+    rest = jnp.concatenate([held[2 * h + c, 0:2, :] for c in range(2) for h in range(4)], axis=0)
+    total = jnp.zeros_like(rest)
+    for _ in range(3):
+        part = rest.astype(jnp.bfloat16)
+        rest = rest - part.astype(jnp.float32)
+        total = total + jnp.dot(part, pick, preferred_element_type=jnp.float32)
+    out_ref[0] = total[:8]
+    out_ref[1] = total[8:]
 
 
 def spread_result(own):
@@ -417,76 +450,60 @@
     )(own)
 
 
-def relax_kernel(total, place_ref, window_ref, conf_ref, out_ref, s_buf, a_buf, w_buf, n_buf, c_buf, u_buf):
+FRONT = 32
+SPAN = 8 * (2 * REACH + 1)
+
+
+def relax_kernel(total, place_ref, window_ref, conf_ref, out_ref, s_buf, w_buf, f_buf, u_buf):
     tile, part = place_ref[0], place_ref[1]
-    start = tile * 8 + 2 * part - (ITERS - 1)
-    rows = a_buf.shape[0]
+    first_slot = jnp.maximum(REACH - tile, 0)
+    last_slot = jnp.minimum(REACH + total // 8 - tile, 2 * REACH + 1)
     lane = lax.broadcasted_iota(jnp.int32, (1, 8, 128), 2)
-    first_col, last_col = lane == 0, lane == 127
+    first_lane, last_lane = lane == 0, lane == 127
     section = lax.broadcasted_iota(jnp.int32, (8, 256), 0)
-    u_buf[...] = jnp.zeros_like(u_buf)
+    for buf in (w_buf, f_buf, u_buf):
+        buf[...] = jnp.zeros_like(buf)
 
     def picked(j):
         return jnp.concatenate([s_buf[h, pl.ds(j, 8, stride=16), :] for h in range(2)], axis=1)
 
     def prepare(k, carry):
-        at = tile + k - REACH
-        inside = (at >= 0) & (at < total // 8)
-        conf = conf_ref[k]
+        conf = jnp.where(section == 0, 0.0, 0.15 * conf_ref[k])
         nodes = window_ref[k].astype(jnp.float32).reshape(128, 256)
         s_buf[0], s_buf[1] = nodes[:, :128], nodes[:, 128:]
         for j in range(8):
-            i = 8 * k + j - 2 * part - 1
-
-            @pl.when((i >= 0) & (i < rows) & inside)
-            def _():
-                w = 0.15 * picked(j) * conf
-                w = jnp.where(section == 0, 0.0, w)
-                wf = w * picked(8 + j)
-                wn = pltpu.roll(w, 7, 0)
-                c = wf - pltpu.roll(wf, 7, 0)
-                w_buf[i] = w
-                n_buf[i] = wn
-                a_buf[i] = 0.4 - w - wn
-                c_buf[i] = c
-                u_buf[0, i + GROUP] = c
-
-            @pl.when((i >= 0) & (i < rows) & jnp.logical_not(inside))
-            def _():
-                zero = jnp.zeros((8, 256), jnp.float32)
-                w_buf[i] = zero
-                n_buf[i] = zero
-                a_buf[i] = zero
-                c_buf[i] = zero
-
-        return carry
-
-    lax.fori_loop(0, 2 * REACH + 1, prepare, 0)
+            i = FRONT + 8 * k + j
+            w = picked(j) * conf
+            wf = w * picked(8 + j)
+            w_buf[i] = w
+            f_buf[i] = wf
+            u_buf[0, i] = wf - pltpu.roll(wf, 7, 0)
+        return carry
+
+    lax.fori_loop(first_slot, last_slot, prepare, 0)
 
     def step(source, target, s):
-        low = (s - 1) // GROUP
-        high = (129 - s + GROUP - 1) // GROUP
+        low = jnp.maximum((2 * part + s) // 8, first_slot)
+        high = jnp.minimum((130 + 2 * part - s + 7) // 8, last_slot)
+        count = (high - low + GROUP - 1) // GROUP
+        low = jnp.where(tile < REACH, low, high - count * GROUP)
 
         def group(g, carry):
-            i = g * GROUP
-            x = [u_buf[source, pl.ds(i + GROUP - 1, GROUP + 2), :, 128 * h : 128 * h + 128] for h in range(2)]
-            mid = [v[1:-1] for v in x]
-            rot_up = [pltpu.roll(v, 1, 2) for v in mid]
-            rot_down = [pltpu.roll(v, 127, 2) for v in mid]
-            left = [jnp.where(first_col, 0.0, rot_up[0]), jnp.where(first_col, rot_up[0], rot_up[1])]
-            right = [jnp.where(last_col, rot_down[1], rot_down[0]), jnp.where(last_col, 0.0, rot_down[1])]
-            for h in range(2):
-                at = (pl.ds(i, GROUP), slice(None), slice(128 * h, 128 * h + 128))
-                around = x[h][:-2] + x[h][2:] + left[h] + right[h]
-                r = start + i
-                row = lax.broadcasted_iota(jnp.int32, (GROUP, 1, 1), 0) + r
-                share = jnp.where((row >= 0) & (row < total), 0.15, 0.0)
-                new = a_buf[at] * mid[h] + c_buf[at] + share * around
-                new = new + w_buf[at] * pltpu.roll(mid[h], 1, 1) + n_buf[at] * pltpu.roll(mid[h], 7, 1)
-                u_buf[target, pl.ds(i + GROUP, GROUP), :, 128 * h : 128 * h + 128] = new
+            i = FRONT + 8 * low + 8 * GROUP * g
+            rows = 8 * GROUP
+            even, odd = [u_buf[source, pl.ds(i - 1, rows + 2), :, 128 * h : 128 * h + 128] for h in range(2)]
+            to_left = jnp.where(first_lane, 0.0, pltpu.roll(odd[1:-1], 1, 2))
+            to_right = jnp.where(last_lane, 0.0, pltpu.roll(even[1:-1], 127, 2))
+            for h, (x, beside, other) in enumerate(((even, odd[1:-1], to_left), (odd, even[1:-1], to_right))):
+                at = (pl.ds(i, rows), slice(None), slice(128 * h, 128 * h + 128))
+                mid = x[1:-1]
+                around = (x[:-2] + x[2:]) + (beside + other)
+                force = w_buf[at] * (pltpu.roll(mid, 1, 1) - mid) + f_buf[at]
+                new = (0.4 * mid + 0.15 * around) + (force - pltpu.roll(force, 7, 1))
+                u_buf[target, pl.ds(i, rows), :, 128 * h : 128 * h + 128] = new
             return carry
 
-        lax.fori_loop(low, high, group, 0)
+        lax.fori_loop(0, count, group, 0)
 
     def pair(k, carry):
         step(0, 1, 2 * k + 2)
@@ -495,11 +512,11 @@
 
     lax.fori_loop(0, (ITERS - 2) // 2, pair, 0)
     step(0, 1, ITERS)
-    out_ref[...] = u_buf[1, pl.ds(63 + GROUP, 2)]
+    out_ref[...] = u_buf[1, pl.ds(FRONT + 8 * REACH + 2 * part, 2)]
 
 
 def relax(place, total, window, conf):
-    rows = 2 * ITERS
+    rows = SPAN + 2 * FRONT
     return pl.pallas_call(
         functools.partial(relax_kernel, total),
         out_shape=jax.ShapeDtypeStruct((2, 8, 256), jnp.float32),
@@ -512,8 +529,8 @@
             ],
             out_specs=pl.BlockSpec((2, 8, 256), lambda i, s: (0, 0, 0)),
             scratch_shapes=[pltpu.VMEM((2, 128, 128), jnp.float32)]
-            + [pltpu.VMEM((rows, 8, 256), jnp.float32)] * 4
-            + [pltpu.VMEM((2, rows + 2 * GROUP, 8, 256), jnp.float32)],
+            + [pltpu.VMEM((rows, 8, 256), jnp.float32)] * 2
+            + [pltpu.VMEM((2, rows, 8, 256), jnp.float32)],
         ),
         compiler_params=pltpu.CompilerParams(vmem_limit_bytes=40 * 1024 * 1024),
     )(place, window, conf)
@@ -527,23 +544,23 @@
 
     node_rows, node_cols = flows.shape[2:]
     spring = (stiffness * valid.astype(jnp.float32))[0]
-    own_nodes = jnp.stack([jnp.concatenate([spring, flows[0, c]]) for c in range(2)]).astype(jnp.bfloat16)
-    window = gather_springs(tile_count, own_nodes)
+    own_nodes = jnp.stack([jnp.concatenate([spring, flows[0, c]]) for c in range(2)])
+    own_nodes = jnp.concatenate([own_nodes[..., 0::2], own_nodes[..., 1::2]], axis=-1).astype(jnp.bfloat16)
 
     shifted = from_behind(patches, "gz", 1)
     earlier = jnp.where(gz_index == 0, prior_patches[None], shifted)[0]
     owner_tile = dest[0, :, 0]
     wanted = target[0]
     own_blocks = blocks[0]
-    block_count = own_blocks.shape[0]
-    tile_ids = jnp.arange(tile_count, dtype=jnp.int32)
+    block_ids = jnp.arange(own_blocks.shape[0], dtype=jnp.int32)
     slot_ids = jnp.arange(tile_count * CAP, dtype=jnp.int32)
-    tile_hits = (owner_tile[:, None] == tile_ids[None, :]).astype(jnp.int32)
-    slot_rank = jnp.sum((jnp.cumsum(tile_hits, axis=0) - tile_hits) * tile_hits, axis=1)
-    slot_index = owner_tile * CAP + slot_rank
+    before = (owner_tile[:, None] == owner_tile[None, :]) & (block_ids[None, :] < block_ids[:, None])
+    slot_index = owner_tile * CAP + jnp.sum(before.astype(jnp.int32), axis=1)
     slot_picks = slot_index[:, None] == slot_ids[None, :]
-    requested = jnp.sum(jnp.where(slot_picks, wanted[:, None], 0), axis=0).reshape(tile_count, CAP)
-    asked_rows = lax.all_to_all(requested, "tile", split_axis=0, concat_axis=0, tiled=True)
+    requested = jnp.sum(jnp.where(slot_picks, wanted[:, None], 0), axis=0).reshape(tile_count, 1, CAP)
+    request = jnp.pad(requested, ((0, 0), (0, 7), (0, LANES - CAP)))
+    asked, window = ask_and_gather(request, own_nodes)
+    asked_rows = asked[:, 0, :CAP]
     outgoing = patch_spectra(asked_rows.reshape(-1), earlier, first, second)
     outgoing = outgoing.reshape(tile_count, CAP * WIRE, LANES)
     arrived = lax.all_to_all(outgoing, "tile", split_axis=0, concat_axis=0, tiled=True)

time: 313 us -> 224 us (0.72)
  Pallas kernels: 257 us -> 133 us
  waiting for transfers between devices: 7.63 us -> 55.2 us
  starting transfers between devices: 19.5 us -> 11 us
    pallas_call x1, Pallas kernels: 93.7 us -> 35.4 us  [ask_and_gather(): pl.pallas_call(functools.partial(ask_kernel, tile_count), out_shape=(jax....]
    all_to_all x1, waiting for transfers between devices: 0.01 us -> 55.2 us  [on_device(): lax.all_to_all(outgoing, 'tile', split_axis=0, concat_axis=0, tiled=True)]
    pallas_call x1, Pallas kernels: 66.1 us -> 25.3 us  [relax(): pl.pallas_call(functools.partial(relax_kernel, total), out_shape=jax.Shap...]
    pallas_call x1, Pallas kernels: 26.8 us -> 15.6 us  [block_spectra(): pl.pallas_call(block_kernel, out_shape=jax.ShapeDtypeStruct((count, P_SIZ...]
    pallas_call x1, Pallas kernels: 27 us -> 16.1 us  [match(): pl.pallas_call(match_kernel, out_shape=(jax.ShapeDtypeStruct((count, PIX)...]
    all_to_all x1 -> x0, starting transfers between devices: 10.8 us -> none  [on_device(): lax.all_to_all(requested, 'tile', split_axis=0, concat_axis=0, tiled=True)]
    all_to_all x1 -> x0, waiting for transfers between devices: 7.62 us -> none  [on_device(): lax.all_to_all(requested, 'tile', split_axis=0, concat_axis=0, tiled=True)]
    pallas_call x1, Pallas kernels: 19.9 us -> 14.2 us  [patch_spectra(): pl.pallas_call(patch_kernel, out_shape=jax.ShapeDtypeStruct((slots, WIRE,...]
  transfers between devices with their start and end apart: 3 -> 2, of which waited for: 1 -> 1; matrix products, arithmetic and copies ran while one was open for 2% -> 3% of each run, Pallas kernels for 39% -> 23%
where the time goes in v4:
time: 224 us; the launch traced here: 223 us
  Pallas kernels  133 us (59%)
  waiting for transfers between devices  55.2 us (25%)
  local copies, waits for them, and re-layouts  18.1 us (8%)
  starting transfers between devices  11 us (5%)
  other arithmetic  4.97 us (2%)
    all_to_all x1, waiting for transfers between devices, on_device(): lax.all_to_all(outgoing, 'tile', split_axis=0, concat_axis=0, tiled=True)  55.2 us
    pallas_call x1, Pallas kernels, ask_and_gather(): pl.pallas_call(functools.partial(ask_kernel, tile_count), out_shape=(jax....  35.4 us
    pallas_call x1, Pallas kernels, relax(): pl.pallas_call(functools.partial(relax_kernel, total), out_shape=jax.Shap...  25.3 us
    pallas_call x1, Pallas kernels, gather_conf(): pl.pallas_call(functools.partial(conf_kernel, tile_count), out_shape=jax....  16.8 us
    pallas_call x1, Pallas kernels, match(): pl.pallas_call(match_kernel, out_shape=(jax.ShapeDtypeStruct((count, PIX)...  16.1 us
    pallas_call x1, Pallas kernels, block_spectra(): pl.pallas_call(block_kernel, out_shape=jax.ShapeDtypeStruct((count, P_SIZ...  15.6 us
    unnamed x27, local copies, waits for them, and re-layouts  14.8 us
    pallas_call x1, Pallas kernels, patch_spectra(): pl.pallas_call(patch_kernel, out_shape=jax.ShapeDtypeStruct((slots, WIRE,...  14.2 us
  transfers between devices with their start and end apart: 2, of which 1 were waited for; matrix products, arithmetic and copies ran while one was open for 3% of the time, Pallas kernels for 23%

profile of v4, /device:TPU:33, one launch (start us, length us, event | category | flops | bytes accessed | tf_op | source)
XLA Modules:
  0.0 222.6 jit_solution(10329406419204687075)
XLA Ops:
  0.6 3.7 %collective-permute-start = (bf16[1,16,25600]{2,1,0:T(8,128)(2,1)}, bf16[1,16,25600]{2,1,0:T(8,128)(2,1)S(1)}, u32[]{:S(2)}, u32[]{:S(2)}) collective-permute-start(bf16[1,16,25600]{2,1,0:T(8,128)(2,1)} %param.12), channel_id=1, source_target_pairs={{0,32},{32,64},{64,96},{96,128},{128,160},{160,192},{192,224},{1,3... | collective-permute-start | bytes 2457608 | tf_op jit(solution)/shard_map/ppermute | solution.py:23
  4.3 0.7 slice_bitcast_fusion.1
  5.0 0.7 multiply_bitcast_fusion
  5.8 0.3 slice.20
  6.1 0.4 slice.19
  6.5 0.9 convert_reduce_fusion
  7.4 0.7 multiply_add_fusion.slot_ref
  8.0 0.7 select_reduce_fusion
  8.8 0.1 reshape.24
  8.9 0.7 pad.4.request_ref
  9.6 0.6 pad_maximum_fusion.2.own_ref
  10.2 35.4 %shard_map.131 = (s32[32,8,128]{2,1,0:T(8,128)}, bf16[17,8,16,256]{3,2,1,0:T(8,128)(2,1)}) custom-call(s32[32,8,128]{2,1,0:T(8,128)} %pad.4.request_ref, bf16[2,16,256]{2,1,0:T(8,128)(2,1)} %pad_maximum_fusion.2.own_ref), custom_call_target="tpu_custom_call" | custom-call | bytes 33554432 | tf_op jit(solution)/shard_map/pallas_call | solution.py:346
  45.6 0.9 slice_reduce_fusion
  46.5 0.1 reshape_squeeze.3.asked_ref
  46.6 0.0 collective-permute-done
  46.6 1.2 fusion.rows_ref
  47.9 0.0 copy-start.7
  47.9 0.9 copy-done.7
  48.8 0.0 copy-start.10
  48.8 0.9 copy-done.10
  49.7 14.2 %shard_map.132 = bf16[64,208,128]{2,1,0:T(8,128)(2,1)S(1)} custom-call(s32[64]{0:T(128)S(1)} %reshape_squeeze.3.asked_ref, bf16[16,25600]{1,0:T(8,128)(2,1)S(1)} %fusion.rows_ref, bf16[256,512]{1,0:T(8,128)(2,1)S(1)} %copy-done.7, bf16[160,320]{1,0:T(8,128)(2,1)S(1)} %copy-done.10), custom_call_target="tpu_custom_call" | custom-call | flops 10000000000 | bytes 8000000 | tf_op jit(solution)/shard_map/pallas_call | solution.py:164
  64.0 0.0 copy-start
  64.0 1.8 copy-done
  65.8 0.0 copy-start.11
  65.8 7.3 %all-to-all-start = ((bf16[32,416,128]{2,1,0:T(8,128)(2,1)}), bf16[32,416,128]{2,1,0:T(8,128)(2,1)S(1)}, u32[]{:S(2)}, u32[]{:S(2)}) async-start(bf16[32,416,128]{2,1,0:T(8,128)(2,1)} %bitcast.28), calls=%async_computation | async-start | bytes 6815744 | tf_op jit(solution)/shard_map/all_to_all | solution.py:566
  73.1 0.1 pad_add_fusion.place_ref
  73.2 0.0 copy-done.11
  73.2 0.0 copy-start.5
  73.2 1.4 copy-done.5
  74.7 0.0 copy-start.8
  74.7 0.9 copy-done.8
  75.6 15.6 %shard_map.133.block_ref = bf16[32,160,512]{2,1,0:T(8,128)(2,1)S(1)} custom-call(bf16[32,25600]{1,0:T(8,128)(2,1)S(1)} %bitcast.29, bf16[256,512]{1,0:T(8,128)(2,1)S(1)} %copy-done.8, bf16[160,320]{1,0:T(8,128)(2,1)S(1)} %copy-done.11), custom_call_target="tpu_custom_call" | custom-call | flops 20000000000 | bytes 8000000 | tf_op jit(solution)/shard_map/pallas_call | solution.py:119
  91.2 0.0 copy-start.12
  91.2 2.3 %copy-done.12 = bf16[32,160,512]{2,1,0:T(8,128)(2,1)} copy-done((bf16[32,160,512]{2,1,0:T(8,128)(2,1)}, bf16[32,160,512]{2,1,0:T(8,128)(2,1)S(1)}, u32[]{:S(2)}) %copy-start.12) | copy-done | bytes 5242904
  93.5 55.2 %all-to-all-done = bf16[32,416,128]{2,1,0:T(8,128)(2,1)S(1)} async-done(((bf16[32,416,128]{2,1,0:T(8,128)(2,1)}), bf16[32,416,128]{2,1,0:T(8,128)(2,1)S(1)}, u32[]{:S(2)}, u32[]{:S(2)}) %all-to-all-start) | async-done | bytes 3407904 | tf_op jit(solution)/shard_map/all_to_all | solution.py:566
  148.7 0.0 copy-start.6
  148.7 0.9 copy-done.6
  149.7 0.0 copy-start.9
  149.7 0.9 copy-done.9
  150.6 16.1 %shard_map.134 = (bf16[32,25600]{1,0:T(8,128)(2,1)}, f32[32,128]{1,0:T(8,128)S(1)}) custom-call(s32[32]{0:T(128)S(1)} %multiply_add_fusion.slot_ref, bf16[64,208,128]{2,1,0:T(8,128)(2,1)S(1)} %bitcast.27, bf16[32,160,512]{2,1,0:T(8,128)(2,1)} %copy-done.12, bf16[320,160]{1,0:T(8,128)(2,1)S(1)} %copy-done.9, bf16[512,256]{1,0:T(8,128)(2,1)S(1)} %copy-done.6), custom_call_target="tpu_custom_call" | custom-call | flops 20000000000 | bytes 10000000 | tf_op jit(solution)/shard_map/pallas_call | solution.py:234
  166.7 0.0 copy-start.4
  166.7 0.6 copy-done.4
  167.3 16.8 %shard_map.135.conf_ref = f32[17,8,256]{2,1,0:T(8,128)} custom-call(f32[32,128]{1,0:T(8,128)} %copy-done.4), custom_call_target="tpu_custom_call" | custom-call | tf_op jit(solution)/shard_map/pallas_call | solution.py:393
  184.1 0.0 copy-start.1
  184.1 1.2 copy-done.1
  185.3 0.0 copy-start.2
  185.3 0.9 copy-done.2
  186.2 25.3 %shard_map.136.own_ref = f32[2,8,256]{2,1,0:T(8,128)S(1)} custom-call(s32[2]{0:T(128)S(1)} %pad_add_fusion.place_ref, bf16[17,8,16,256]{3,2,1,0:T(8,128)(2,1)S(1)} %copy-done.1, f32[17,8,256]{2,1,0:T(8,128)S(1)} %copy-done.2), custom_call_target="tpu_custom_call" | custom-call | tf_op jit(solution)/shard_map/pallas_call | solution.py:520
  211.5 0.0 copy-start.3
  211.5 0.6 copy-done.3
  212.1 9.2 %shard_map.137 = f32[2,8,256]{2,1,0:T(8,128)} custom-call(f32[2,8,256]{2,1,0:T(8,128)} %copy-done.3), custom_call_target="tpu_custom_call" | custom-call | tf_op jit(solution)/shard_map/pallas_call | solution.py:438
  221.3 1.3 copy.18
  (2 shorter events, 0.0 us)
Async XLA Ops:
  0.6 46.0 %collective-permute-start = (bf16[1,16,25600]{2,1,0:T(8,128)(2,1)}, bf16[1,16,25600]{2,1,0:T(8,128)(2,1)S(1)}, u32[]{:S(2)}, u32[]{:S(2)}) collective-permute-start(bf16[1,16,25600]{2,1,0:T(8,128)(2,1)} %param.12), channel_id=1, source_target_pairs={{0,32},{32,64},{64,96},{96,128},{128,160},{160,192},{192,224},{1,3... | collective-permute-start | bytes 2457608 | tf_op jit(solution)/shard_map/ppermute | solution.py:23
  47.9 1.0 copy-start.7
  48.8 0.9 copy-start.10
  64.0 1.8 copy-start
  65.8 7.4 %copy-start.11 = (bf16[160,320]{1,0:T(8,128)(2,1)S(1)}, bf16[160,320]{1,0:T(8,128)(2,1)}, u32[]{:S(2)}) copy-start(bf16[160,320]{1,0:T(8,128)(2,1)} %constant.35.clone.second_ref) | copy-start | bytes 307204
  65.8 83.0 %all-to-all-start = ((bf16[32,416,128]{2,1,0:T(8,128)(2,1)}), bf16[32,416,128]{2,1,0:T(8,128)(2,1)S(1)}, u32[]{:S(2)}, u32[]{:S(2)}) async-start(bf16[32,416,128]{2,1,0:T(8,128)(2,1)} %bitcast.28), calls=%async_computation | async-start | bytes 6815744 | tf_op jit(solution)/shard_map/all_to_all | solution.py:566
  73.2 1.4 copy-start.5
  74.7 0.9 copy-start.8
  91.2 2.3 %copy-start.12 = (bf16[32,160,512]{2,1,0:T(8,128)(2,1)}, bf16[32,160,512]{2,1,0:T(8,128)(2,1)S(1)}, u32[]{:S(2)}) copy-start(bf16[32,160,512]{2,1,0:T(8,128)(2,1)S(1)} %shard_map.133.block_ref) | copy-start | bytes 15728644
  148.7 1.0 copy-start.6
  149.7 0.9 copy-start.9
  166.7 0.6 copy-start.4
  184.1 1.2 copy-start.1
  185.3 0.9 copy-start.2
  211.5 0.6 copy-start.3

commit v5 on v4

--- a/solution.py
+++ b/solution.py
@@ -15,12 +15,6 @@
 ITERS = 64
 GROUP = 4
 UNROLL = 8
-
-
-def from_behind(value, axis, steps):
-    count = lax.axis_size(axis)
-    first, last = (max(0, -steps), min(count, count - steps))
-    return lax.ppermute(value, axis, [(source, source + steps) for source in range(first, last)])
 
 
 LANES = 128
@@ -96,8 +90,7 @@
     return jnp.dot(second_ref[...], both, preferred_element_type=jnp.float32)
 
 
-def block_kernel(rows_ref, first_ref, second_ref, out_ref, low_buf, high_buf):
-    to_images(rows_ref, low_buf, high_buf)
+def block_batch(low_buf, high_buf, first_ref, second_ref, out_ref):
     low_half = lax.broadcasted_iota(jnp.int32, (P_SIZE, LANES), 1) < HALF
 
     def image(n, carry):
@@ -113,23 +106,7 @@
     lax.fori_loop(0, BATCH, image, 0, unroll=UNROLL)
 
 
-def block_spectra(rows, first, second):
-    count = rows.shape[0]
-    fixed = lambda x: pl.BlockSpec(x.shape, lambda i: (0, 0))
-    return pl.pallas_call(
-        block_kernel,
-        out_shape=jax.ShapeDtypeStruct((count, P_SIZE, 4 * LANES), jnp.bfloat16),
-        grid=(count // BATCH,),
-        in_specs=[pl.BlockSpec((BATCH, PIX), lambda i: (i, 0)), fixed(first), fixed(second)],
-        out_specs=pl.BlockSpec((BATCH, P_SIZE, 4 * LANES), lambda i: (i, 0, 0)),
-        scratch_shapes=[pltpu.VMEM((BATCH * P_SIZE, LANES), jnp.float32)] * 2,
-        compiler_params=pltpu.CompilerParams(vmem_limit_bytes=40 * 1024 * 1024),
-        cost_estimate=pl.CostEstimate(flops=20_000_000_000, bytes_accessed=8_000_000, transcendentals=0),
-    )(rows, first, second)
-
-
-def patch_kernel(asked_ref, rows_ref, first_ref, second_ref, out_ref, low_buf, high_buf, wire_buf, sems):
-    to_images(rows_ref, low_buf, high_buf)
+def patch_batch(low_buf, high_buf, first_ref, second_ref, wire_buf):
     lane = lax.broadcasted_iota(jnp.int32, (8, LANES), 1) % HALF
 
     def image(n, carry):
@@ -143,38 +120,6 @@
         return carry
 
     lax.fori_loop(0, BATCH, image, 0, unroll=UNROLL)
-    copy = lambda s: pltpu.make_async_copy(wire_buf.at[asked_ref[s]], out_ref.at[s], sems.at[s])
-    slots = out_ref.shape[0]
-
-    def begin(s, carry):
-        copy(s).start()
-        return carry
-
-    def finish(s, carry):
-        copy(s).wait()
-        return carry
-
-    lax.fori_loop(0, slots, begin, 0)
-    lax.fori_loop(0, slots, finish, 0)
-
-
-def patch_spectra(asked, rows, first, second):
-    slots = asked.shape[0]
-    fixed = lambda x: pl.BlockSpec(x.shape, lambda i, s: (0, 0))
-    return pl.pallas_call(
-        patch_kernel,
-        out_shape=jax.ShapeDtypeStruct((slots, WIRE, LANES), jnp.bfloat16),
-        grid_spec=pltpu.PrefetchScalarGridSpec(
-            num_scalar_prefetch=1,
-            grid=(1,),
-            in_specs=[fixed(rows), fixed(first), fixed(second)],
-            out_specs=pl.BlockSpec(memory_space=pl.ANY),
-            scratch_shapes=[pltpu.VMEM((BATCH * P_SIZE, LANES), jnp.float32)] * 2
-            + [pltpu.VMEM((BATCH, WIRE, LANES), jnp.bfloat16), pltpu.SemaphoreType.DMA((slots,))],
-        ),
-        compiler_params=pltpu.CompilerParams(vmem_limit_bytes=40 * 1024 * 1024),
-        cost_estimate=pl.CostEstimate(flops=10_000_000_000, bytes_accessed=8_000_000, transcendentals=0),
-    )(asked, rows, first, second)
 
 
 def match_kernel(slot_ref, wire_ref, block_ref, third_ref, fourth_ref, map_ref, peak_ref, low_buf, high_buf):
@@ -310,60 +255,204 @@
     return copies
 
 
-def ask_kernel(tile_count, request_ref, own_ref, asked_ref, window_ref, held, local, send_r, recv_r, send_a, recv_a, send_b, recv_b):
+def request_rows(owner_col, owner_row, wanted_row, tile_count):
+    count = owner_col.shape[0]
+    earlier = lax.broadcasted_iota(jnp.int32, (count, count), 0) < lax.broadcasted_iota(jnp.int32, (count, count), 1)
+    rank = jnp.sum(jnp.where(earlier & (owner_col == owner_row), 1, 0), axis=0, keepdims=True)
+    hit = owner_row == lax.broadcasted_iota(jnp.int32, (tile_count, count), 0)
+    lane = lax.broadcasted_iota(jnp.int32, (tile_count, LANES), 1)
+    rows = jnp.zeros((tile_count, LANES), jnp.int32)
+    for c in range(CAP):
+        asked = jnp.sum(jnp.where(hit & (rank == c), wanted_row, 0), axis=1, keepdims=True)
+        rows = jnp.where(lane == c, asked, rows)
+    return rows
+
+
+def trade_kernel(
+    tile_count, patch_ref, prior_ref, block_ref, col_ref, row_ref, want_ref, flow_ref, valid_ref, stiff_ref, first_ref,
+    second_ref, arrived_ref, spec_ref, window_ref, rows_buf, block_buf, low_buf, high_buf, wire_buf, send_buf, spec_buf,
+    own_buf, held, ask_buf, heard_buf, list_buf, told_buf, told_smem, local, send_r, recv_r, send_a, recv_a, send_b,
+    recv_b, send_f, recv_f, send_p, recv_p,
+):
     gz, tile = lax.axis_index("gz"), lax.axis_index("tile")
-    others = [(gz, lax.rem(tile + d, tile_count)) for d in range(1, tile_count)]
-    group_barrier(gz_peers() + others)
-    copies = exchange_gz(lambda peer: own_ref.at[lax.rem(peer, 2)], held, send_a, recv_a)
-    mine = pltpu.make_async_copy(own_ref.at[lax.rem(gz, 2)], held.at[gz], local.at[0])
+    after, before = lax.rem(gz + 1, GZ), lax.rem(gz + GZ - 1, GZ)
+    barrier = pltpu.get_barrier_semaphore()
+
+    def greet(peer):
+        pl.semaphore_signal(barrier, inc=1, device_id=peer, device_id_type=MESH)
+
+    def greet_tiles(d, carry):
+        peer = lax.rem(tile + d, tile_count)
+        greet((after, peer))
+        greet((before, peer))
+
+        @pl.when(d > 0)
+        def _():
+            greet((gz, peer))
+
+        return carry
+
+    lax.fori_loop(0, tile_count, greet_tiles, 0)
+    for d in range(2, GZ - 1):
+        greet((lax.rem(gz + d, GZ), tile))
+
+    from_prior = pltpu.make_async_copy(prior_ref, rows_buf, local.at[0])
+    from_patches = pltpu.make_async_copy(patch_ref.at[0], rows_buf, local.at[0])
+    load_blocks = pltpu.make_async_copy(block_ref.at[0], block_buf, local.at[1])
+
+    @pl.when(gz == GZ - 1)
+    def _():
+        from_prior.start()
+
+    @pl.when(gz != GZ - 1)
+    def _():
+        from_patches.start()
+
+    load_blocks.start()
+
+    rows = request_rows(col_ref[...], row_ref[...], want_ref[...], tile_count)
+    for j in range(8):
+        ask_buf[pl.ds(j, tile_count, stride=8), :] = rows
+    columns = stiff_ref.shape[2]
+    lane = lax.broadcasted_iota(jnp.int32, (columns, columns), 1)
+    order = 2 * lax.rem(lane, columns // 2) + lane // (columns // 2)
+    pick = jnp.where(lax.broadcasted_iota(jnp.int32, (columns, columns), 0) == order, 1.0, 0.0).astype(jnp.bfloat16)
+    spring = stiff_ref[0] * valid_ref[0].astype(jnp.float32)
+    for c in range(2):
+        nodes = jnp.concatenate([spring, flow_ref[0, c]], axis=0).astype(jnp.bfloat16)
+        own_buf[c] = jnp.dot(nodes, pick, preferred_element_type=jnp.float32).astype(jnp.bfloat16)
+
+    pl.semaphore_wait(barrier, 3 * tile_count - 1 + GZ - 3)
+
+    springs = exchange_gz(lambda peer: own_buf.at[lax.rem(peer, 2)], held, send_a, recv_a)
+    mine = pltpu.make_async_copy(own_buf.at[lax.rem(gz, 2)], held.at[gz], local.at[2])
     mine.start()
-    requests = []
-    for d, peer in enumerate(others):
-        requests.append(
-            pltpu.make_async_remote_copy(
-                src_ref=request_ref.at[peer[1]], dst_ref=asked_ref.at[tile], send_sem=send_r.at[d],
-                recv_sem=recv_r.at[d], device_id=peer, device_id_type=MESH,
-            )
+
+    def request(d):
+        peer = lax.rem(tile + d, tile_count)
+        part = lambda t: pl.ds(pl.multiple_of(8 * t, 8), 8)
+        return pltpu.make_async_remote_copy(
+            src_ref=ask_buf.at[part(peer)], dst_ref=heard_buf.at[part(tile)], send_sem=send_r.at[d],
+            recv_sem=recv_r.at[d], device_id=(gz, peer), device_id_type=MESH,
         )
-        requests[-1].start()
-    asked_ref[tile] = request_ref[tile]
+
+    def each(first, last, act):
+        def body(d, carry):
+            act(d)
+            return carry
+
+        lax.fori_loop(first, last, body, 0)
+
+    each(1, tile_count, lambda d: request(d).start())
+    own_part = pl.ds(pl.multiple_of(8 * tile, 8), 8)
+    heard_buf[own_part, :] = ask_buf[own_part, :]
+
+    @pl.when(gz == GZ - 1)
+    def _():
+        from_prior.wait()
+
+    @pl.when(gz != GZ - 1)
+    def _():
+        from_patches.wait()
+
+    to_images(rows_buf, low_buf, high_buf)
+
     mine.wait()
-    for copy in copies:
+    for copy in springs:
         copy.wait()
-    copies = exchange_tiles(tile_count, held, window_ref, send_b, recv_b)
-    mine = pltpu.make_async_copy(held, window_ref.at[REACH], local.at[1])
+    springs = exchange_tiles(tile_count, held, window_ref, send_b, recv_b)
+    mine = pltpu.make_async_copy(held, window_ref.at[REACH], local.at[2])
     mine.start()
-    for copy in requests:
+    each(1, tile_count, lambda d: request(d).wait())
+    list_buf[...] = heard_buf[pl.ds(0, tile_count, stride=8), :]
+    forward = pltpu.make_async_remote_copy(
+        src_ref=list_buf, dst_ref=told_buf, send_sem=send_f.at[0], recv_sem=recv_f.at[0], device_id=(before, tile),
+        device_id_type=MESH,
+    )
+    forward.start()
+    patch_batch(low_buf, high_buf, first_ref, second_ref, wire_buf)
+    forward.wait()
+    told = pltpu.make_async_copy(told_buf, told_smem, local.at[3])
+    told.start()
+    told.wait()
+
+    def parcel(d):
+        peer = lax.rem(tile + d, tile_count)
+        return pltpu.make_async_remote_copy(
+            src_ref=send_buf.at[peer], dst_ref=arrived_ref.at[tile], send_sem=send_p.at[d], recv_sem=recv_p.at[d],
+            device_id=(after, peer), device_id_type=MESH,
+        )
+
+    def post(d):
+        peer = lax.rem(tile + d, tile_count)
+        for c in range(CAP):
+            send_buf[peer, WIRE * c : WIRE * c + WIRE, :] = wire_buf[told_smem[peer, c]]
+        parcel(d).start()
+
+    each(0, tile_count, post)
+
+    load_blocks.wait()
+    stores = []
+    for half in range(2):
+        to_images(block_buf.at[pl.ds(BATCH * half, BATCH)], low_buf, high_buf)
+        block_batch(low_buf, high_buf, first_ref, second_ref, spec_buf.at[pl.ds(BATCH * half, BATCH)])
+        part = pl.ds(BATCH * half, BATCH)
+        stores.append(pltpu.make_async_copy(spec_buf.at[part], spec_ref.at[part], local.at[4 + half]))
+        stores[-1].start()
+
+    mine.wait()
+    for copy in springs + stores:
         copy.wait()
-    mine.wait()
-    for copy in copies:
-        copy.wait()
-
-
-def ask_and_gather(request, own):
-    tile_count = request.shape[0]
-    dma = lambda count: pltpu.SemaphoreType.DMA((count,))
+    each(0, tile_count, lambda d: parcel(d).wait())
+
+
+def trade(tile_count, patches, prior, blocks, col, row, want, flows, valid, stiffness, first, second):
+    count = blocks.shape[1]
+    columns = flows.shape[3]
+    dma = lambda number: pltpu.SemaphoreType.DMA((number,))
+    vmem, anywhere = pl.BlockSpec(memory_space=pltpu.VMEM), pl.BlockSpec(memory_space=pl.ANY)
+    f32, bf16 = jnp.float32, jnp.bfloat16
     return pl.pallas_call(
-        functools.partial(ask_kernel, tile_count),
+        functools.partial(trade_kernel, tile_count),
         out_shape=(
-            jax.ShapeDtypeStruct(request.shape, request.dtype),
-            jax.ShapeDtypeStruct((2 * REACH + 1, GZ) + own.shape[1:], own.dtype),
+            jax.ShapeDtypeStruct((tile_count, CAP * WIRE, LANES), bf16),
+            jax.ShapeDtypeStruct((count, P_SIZE, 4 * LANES), bf16),
+            jax.ShapeDtypeStruct((2 * REACH + 1, GZ, 16, columns), bf16),
         ),
-        in_specs=[pl.BlockSpec(memory_space=pltpu.VMEM)] * 2,
-        out_specs=(pl.BlockSpec(memory_space=pltpu.VMEM), pl.BlockSpec(memory_space=pl.ANY)),
+        in_specs=[anywhere] * 3 + [vmem] * 8,
+        out_specs=(anywhere,) * 3,
         scratch_shapes=[
-            pltpu.VMEM((GZ,) + own.shape[1:], own.dtype),
-            dma(2),
-            dma(tile_count - 1),
-            dma(tile_count - 1),
+            pltpu.VMEM((BATCH, PIX), bf16),
+            pltpu.VMEM((count, PIX), bf16),
+            pltpu.VMEM((BATCH * P_SIZE, LANES), f32),
+            pltpu.VMEM((BATCH * P_SIZE, LANES), f32),
+            pltpu.VMEM((BATCH, WIRE, LANES), bf16),
+            pltpu.VMEM((tile_count, CAP * WIRE, LANES), bf16),
+            pltpu.VMEM((count, P_SIZE, 4 * LANES), bf16),
+            pltpu.VMEM((2, 16, columns), bf16),
+            pltpu.VMEM((GZ, 16, columns), bf16),
+            pltpu.VMEM((8 * tile_count, LANES), jnp.int32),
+            pltpu.VMEM((8 * tile_count, LANES), jnp.int32),
+            pltpu.VMEM((tile_count, LANES), jnp.int32),
+            pltpu.VMEM((tile_count, LANES), jnp.int32),
+            pltpu.SMEM((tile_count, LANES), jnp.int32),
+            dma(6),
+            dma(tile_count),
+            dma(tile_count),
             dma(GZ - 1),
             dma(GZ - 1),
             dma(2 * REACH),
             dma(2 * REACH),
+            dma(1),
+            dma(1),
+            dma(tile_count),
+            dma(tile_count),
         ],
-        compiler_params=pltpu.CompilerParams(collective_id=1, has_side_effects=True),
-        cost_estimate=pl.CostEstimate(flops=0, bytes_accessed=32 * 1024 * 1024, transcendentals=0),
-    )(request, own)
+        compiler_params=pltpu.CompilerParams(
+            collective_id=1, has_side_effects=True, vmem_limit_bytes=60 * 1024 * 1024
+        ),
+        cost_estimate=pl.CostEstimate(flops=30_000_000_000, bytes_accessed=32_000_000, transcendentals=0),
+    )(patches, prior, blocks, col, row, want, flows, valid, stiffness, first, second)
 
 
 def conf_kernel(tile_count, peak_ref, window_ref, own_ref, held, packed, send_a, recv_a, send_b, recv_b):
@@ -543,28 +632,13 @@
     tile_index = lax.axis_index("tile")
 
     node_rows, node_cols = flows.shape[2:]
-    spring = (stiffness * valid.astype(jnp.float32))[0]
-    own_nodes = jnp.stack([jnp.concatenate([spring, flows[0, c]]) for c in range(2)])
-    own_nodes = jnp.concatenate([own_nodes[..., 0::2], own_nodes[..., 1::2]], axis=-1).astype(jnp.bfloat16)
-
-    shifted = from_behind(patches, "gz", 1)
-    earlier = jnp.where(gz_index == 0, prior_patches[None], shifted)[0]
     owner_tile = dest[0, :, 0]
-    wanted = target[0]
-    own_blocks = blocks[0]
-    block_ids = jnp.arange(own_blocks.shape[0], dtype=jnp.int32)
-    slot_ids = jnp.arange(tile_count * CAP, dtype=jnp.int32)
+    block_ids = jnp.arange(blocks.shape[1], dtype=jnp.int32)
     before = (owner_tile[:, None] == owner_tile[None, :]) & (block_ids[None, :] < block_ids[:, None])
     slot_index = owner_tile * CAP + jnp.sum(before.astype(jnp.int32), axis=1)
-    slot_picks = slot_index[:, None] == slot_ids[None, :]
-    requested = jnp.sum(jnp.where(slot_picks, wanted[:, None], 0), axis=0).reshape(tile_count, 1, CAP)
-    request = jnp.pad(requested, ((0, 0), (0, 7), (0, LANES - CAP)))
-    asked, window = ask_and_gather(request, own_nodes)
-    asked_rows = asked[:, 0, :CAP]
-    outgoing = patch_spectra(asked_rows.reshape(-1), earlier, first, second)
-    outgoing = outgoing.reshape(tile_count, CAP * WIRE, LANES)
-    arrived = lax.all_to_all(outgoing, "tile", split_axis=0, concat_axis=0, tiled=True)
-    block_spec = block_spectra(own_blocks, first, second)
+    arrived, block_spec, window = trade(
+        tile_count, patches, prior_patches, blocks, dest[0], owner_tile[None], target, flows, valid, stiffness, first, second
+    )
     corr_maps, peaks = match(slot_index, arrived.reshape(tile_count * CAP, WIRE, LANES), block_spec, third, fourth)
 
     conf_window = gather_conf(tile_count, peaks, node_cols)

time: 224 us -> 193 us (0.86)
  waiting for transfers between devices: 55.2 us -> 0 us
  Pallas kernels: 133 us -> 181 us
  local copies, waits for them, and re-layouts: 18.1 us -> 6.74 us
  starting transfers between devices: 11 us -> 0 us
  other arithmetic: 4.97 us -> 1.65 us
    all_to_all x1 -> x0, waiting for transfers between devices: 55.2 us -> none  [on_device(): lax.all_to_all(outgoing, 'tile', split_axis=0, concat_axis=0, tiled=True)]
    pallas_call x3 -> x1, Pallas kernels: 65.3 us -> 108 us  [trade(): pl.pallas_call(functools.partial(trade_kernel, tile_count), out_shape=(ja...]
    unnamed x27 -> x15, local copies, waits for them, and re-layouts: 14.8 us -> 5.4 us
    all_to_all x1 -> x0, starting transfers between devices: 7.34 us -> none  [on_device(): lax.all_to_all(outgoing, 'tile', split_axis=0, concat_axis=0, tiled=True)]
    pallas_call x1, Pallas kernels: 16.8 us -> 23.3 us  [gather_conf(): pl.pallas_call(functools.partial(conf_kernel, tile_count), out_shape=jax....]
    ppermute x1 -> x0, starting transfers between devices: 3.68 us -> none  [from_behind(): lax.ppermute(value, axis, [(source, source + steps) for source in range(f...]
  transfers between devices with their start and end apart: 2 -> 0, of which waited for: 1 -> 0; matrix products, arithmetic and copies ran while one was open for 3% -> 0% of each run, Pallas kernels for 23% -> 0%
where the time goes in v5:
time: 193 us; the launch traced here: 190 us
  Pallas kernels  181 us (94%)
  local copies, waits for them, and re-layouts  6.74 us (3%)
    pallas_call x1, Pallas kernels, trade(): pl.pallas_call(functools.partial(trade_kernel, tile_count), out_shape=(ja...  108 us
    pallas_call x1, Pallas kernels, relax(): pl.pallas_call(functools.partial(relax_kernel, total), out_shape=jax.Shap...  25.3 us
    pallas_call x1, Pallas kernels, gather_conf(): pl.pallas_call(functools.partial(conf_kernel, tile_count), out_shape=jax....  23.3 us
    pallas_call x1, Pallas kernels, match(): pl.pallas_call(match_kernel, out_shape=(jax.ShapeDtypeStruct((count, PIX)...  16.1 us
    pallas_call x1, Pallas kernels, spread_result(): pl.pallas_call(spread_kernel, out_shape=jax.ShapeDtypeStruct((2, 8, colum...  8.03 us
    unnamed x15, local copies, waits for them, and re-layouts  5.4 us

profile of v5, /device:TPU:33, one launch (start us, length us, event | category | flops | bytes accessed | tf_op | source)
XLA Modules:
  0.0 190.0 jit_solution(17636661600567215906)
XLA Ops:
  0.6 0.9 convert_reduce_fusion
  1.5 0.7 multiply_add_fusion.slot_ref
  2.2 1.3 copy.15.col_ref
  3.5 0.0 copy-start.5
  3.5 0.0 copy-start.6
  3.5 108.2 %shard_map.131 = (bf16[32,416,128]{2,1,0:T(8,128)(2,1)}, bf16[32,160,512]{2,1,0:T(8,128)(2,1)}, bf16[17,8,16,256]{3,2,1,0:T(8,128)(2,1)}) custom-call(bf16[1,16,25600]{2,1,0:T(8,128)(2,1)} %patch_ref.1, bf16[16,25600]{1,0:T(8,128)(2,1)} %prior_ref.1, bf16[1,32,25600]{2,1,0:T(8,128)(2,1)} %block_ref.1, s32[32,1]{1,0:T(8,128)} %copy.15.col_ref, ...), custom_call_target="tpu_custom_call" | custom-call | flops 30000001024 | bytes 32000000 | tf_op jit(solution)/shard_map/pallas_call | solution.py:415
  111.7 0.0 copy-done.5
  111.7 0.0 copy-done.6
  111.7 0.0 copy-start.4
  111.8 2.0 %copy-done.4 = bf16[32,416,128]{2,1,0:T(8,128)(2,1)S(1)} copy-done((bf16[32,416,128]{2,1,0:T(8,128)(2,1)S(1)}, bf16[32,416,128]{2,1,0:T(8,128)(2,1)}, u32[]{:S(2)}) %copy-start.4) | copy-done | bytes 3407896
  113.7 0.0 copy-start
  113.7 16.1 %shard_map.132 = (bf16[32,25600]{1,0:T(8,128)(2,1)}, f32[32,128]{1,0:T(8,128)S(1)}) custom-call(s32[32]{0:T(128)S(1)} %multiply_add_fusion.slot_ref, bf16[64,208,128]{2,1,0:T(8,128)(2,1)S(1)} %bitcast.9, bf16[32,160,512]{2,1,0:T(8,128)(2,1)} %get-tuple-element.8.block_ref, bf16[320,160]{1,0:T(8,128)(2,1)S(1)} %copy-done.6, bf16[512,256]{1,0:T(8,128)(2,1)S(1)} %copy-done.5), custom_call_target="tpu_custom_call" | custom-call | flops 20000000000 | bytes 10000000 | tf_op jit(solution)/shard_map/pallas_call | solution.py:179
  129.8 0.0 copy-start.3
  129.8 0.6 copy-done.3
  130.4 0.1 pad_add_fusion.place_ref
  130.5 23.3 %shard_map.133.conf_ref = f32[17,8,256]{2,1,0:T(8,128)} custom-call(f32[32,128]{1,0:T(8,128)} %copy-done.3), custom_call_target="tpu_custom_call" | custom-call | tf_op jit(solution)/shard_map/pallas_call | solution.py:482
  153.8 0.0 copy-done
  153.8 0.0 copy-start.1
  153.8 0.9 copy-done.1
  154.7 25.3 %shard_map.134.own_ref = f32[2,8,256]{2,1,0:T(8,128)S(1)} custom-call(s32[2]{0:T(128)S(1)} %pad_add_fusion.place_ref, bf16[17,8,16,256]{3,2,1,0:T(8,128)(2,1)S(1)} %copy-done, f32[17,8,256]{2,1,0:T(8,128)S(1)} %copy-done.1), custom_call_target="tpu_custom_call" | custom-call | tf_op jit(solution)/shard_map/pallas_call | solution.py:609
  180.0 0.0 copy-start.2
  180.0 0.6 copy-done.2
  180.6 8.0 %shard_map.135 = f32[2,8,256]{2,1,0:T(8,128)} custom-call(f32[2,8,256]{2,1,0:T(8,128)} %copy-done.2), custom_call_target="tpu_custom_call" | custom-call | tf_op jit(solution)/shard_map/pallas_call | solution.py:527
  188.6 1.3 copy.17
Async XLA Ops:
  3.5 108.2 %copy-start.5 = (bf16[512,256]{1,0:T(8,128)(2,1)S(1)}, bf16[512,256]{1,0:T(8,128)(2,1)}, u32[]{:S(2)}) copy-start(bf16[512,256]{1,0:T(8,128)(2,1)} %constant.37.clone.fourth_ref) | copy-start | bytes 786436
  3.5 108.2 %copy-start.6 = (bf16[320,160]{1,0:T(8,128)(2,1)S(1)}, bf16[320,160]{1,0:T(8,128)(2,1)}, u32[]{:S(2)}) copy-start(bf16[320,160]{1,0:T(8,128)(2,1)} %constant.36.clone.third_ref) | copy-start | bytes 307204
  111.7 2.0 %copy-start.4 = (bf16[32,416,128]{2,1,0:T(8,128)(2,1)S(1)}, bf16[32,416,128]{2,1,0:T(8,128)(2,1)}, u32[]{:S(2)}) copy-start(bf16[32,416,128]{2,1,0:T(8,128)(2,1)} %get-tuple-element.7) | copy-start | bytes 10223620
  113.7 40.1 %copy-start = (bf16[17,8,16,256]{3,2,1,0:T(8,128)(2,1)S(1)}, bf16[17,8,16,256]{3,2,1,0:T(8,128)(2,1)}, u32[]{:S(2)}) copy-start(bf16[17,8,16,256]{3,2,1,0:T(8,128)(2,1)} %get-tuple-element.10.window_ref) | copy-start | bytes 3342340
  129.8 0.6 copy-start.3
  153.8 0.9 copy-start.1
  180.0 0.6 copy-start.2

commit v6 on v5

v6 whole, which is shorter than its diff:
```python
import functools

import jax
import jax.numpy as jnp
import ml_dtypes
import numpy as np
from jax import lax
from jax.experimental import pallas as pl
from jax.experimental.pallas import tpu as pltpu
from jax.sharding import PartitionSpec as P

P_SIZE = 160
PIX = 25600
CAP = 2
ITERS = 64
GROUP = 4
PHASE = ITERS // 2
UNROLL = 8


LANES = 128
HALF = 64
WIRE = 208
BATCH = 16


def tables():
    size = P_SIZE
    line = np.arange(size)
    angles = (np.outer(line, line) % size).astype(np.float32) * np.float32(2.0 * np.pi / size)
    rounded = lambda x: x.astype(ml_dtypes.bfloat16).astype(np.float32)
    cos_t, sin_t = rounded(np.cos(angles)), rounded(np.sin(angles))
    lane = np.arange(2 * LANES)
    column = HALF * (lane // LANES) + lane % HALF
    used = column <= size // 2
    column = np.where(used, column, 0)
    real = lane % LANES < HALF
    c, s = cos_t[:, column] * used, sin_t[:, column] * used
    first = np.zeros((2 * LANES, 4 * LANES), np.float32)
    first[:size, : 2 * LANES] = np.where(real, c, s)
    first[:size, 2 * LANES :] = np.where(real, -s, c)
    second = np.concatenate([cos_t, sin_t], axis=1)
    third = np.concatenate([cos_t, sin_t], axis=0)
    twice = np.where((column == 0) | (column == size // 2), 1.0, 2.0)
    fourth = np.zeros((4 * LANES, 2 * LANES), np.float32)
    fourth[: 2 * LANES, :size] = (np.where(real, c, -s) * twice).T
    fourth[2 * LANES :, :size] = (np.where(real, -s, -c) * twice).T
    return [jnp.asarray(x, jnp.bfloat16) for x in (first, second, third, fourth)]


def to_images(rows_ref, low_buf, high_buf):
    parts = PIX // 640
    chunk = lambda m: rows_ref[:, pl.ds(pl.multiple_of(640 * m, LANES), 640)].astype(jnp.float32)
    fold = lambda x: sum(x[:, LANES * k : LANES * k + LANES] for k in range(5))
    zero = jnp.zeros((BATCH, LANES), jnp.float32)
    sums = lax.fori_loop(0, parts, lambda m, t: t + fold(chunk(m)), zero)
    mean = jnp.sum(sums, axis=1, keepdims=True) * (1.0 / PIX)

    def square(m, t):
        x = chunk(m) - mean
        return t + fold(x * x)

    sums = lax.fori_loop(0, parts, square, zero)
    scale = lax.rsqrt(jnp.sum(sums, axis=1, keepdims=True) * (1.0 / PIX) + 1e-05)
    lane = lax.broadcasted_iota(jnp.int32, (BATCH, LANES), 1)

    def place(m, carry):
        x = (chunk(m) - mean) * scale
        t = [x[:, LANES * k : LANES * k + LANES] for k in range(5)]
        low = [
            t[0],
            pltpu.roll(jnp.where(lane < 32, t[2], t[1]), 96, 1),
            pltpu.roll(jnp.where(lane < 64, t[3], t[2]), 64, 1),
            pltpu.roll(jnp.where(lane < 96, t[4], t[3]), 32, 1),
        ]
        high = [t[1], pltpu.roll(t[2], 96, 1), pltpu.roll(t[3], 64, 1), pltpu.roll(t[4], 32, 1)]
        for k in range(4):
            at = pl.ds(4 * m + k, BATCH, stride=P_SIZE)
            low_buf[at, :] = low[k]
            high_buf[at, :] = high[k]
        return carry

    lax.fori_loop(0, parts, place, 0)


def image_spectrum(n, low_buf, high_buf, first_ref, second_ref):
    at = pl.ds(pl.multiple_of(P_SIZE * n, 8), P_SIZE)
    image = jnp.concatenate([low_buf[at, :], high_buf[at, :]], axis=1).astype(jnp.bfloat16)
    first = jnp.dot(image, first_ref[...], preferred_element_type=jnp.float32).astype(jnp.bfloat16)
    both = jnp.concatenate([first[:, : 2 * LANES], first[:, 2 * LANES :]], axis=0)
    return jnp.dot(second_ref[...], both, preferred_element_type=jnp.float32)


def block_batch(low_buf, high_buf, first_ref, second_ref, out_ref):
    low_half = lax.broadcasted_iota(jnp.int32, (P_SIZE, LANES), 1) < HALF

    def image(n, carry):
        spec = image_spectrum(n, low_buf, high_buf, first_ref, second_ref)
        for h in range(2):
            x = spec[:, LANES * h : LANES * h + LANES]
            swapped = pltpu.roll(x, HALF, 1)
            out_ref[n, :, LANES * h : LANES * h + LANES] = jnp.where(low_half, x, swapped).astype(jnp.bfloat16)
            at = slice(LANES * (2 + h), LANES * (3 + h))
            out_ref[n, :, at] = jnp.where(low_half, swapped, -x).astype(jnp.bfloat16)
        return carry

    lax.fori_loop(0, BATCH, image, 0, unroll=UNROLL)


def patch_batch(low_buf, high_buf, first_ref, second_ref, wire_buf):
    lane = lax.broadcasted_iota(jnp.int32, (8, LANES), 1) % HALF

    def image(n, carry):
        spec = image_spectrum(n, low_buf, high_buf, first_ref, second_ref)
        rest = [spec[8 * i : 8 * i + 8, LANES:] for i in range(20)]
        pieces = [spec[:, :LANES]]
        for i in range(5):
            pieces.append(sum(pltpu.roll(jnp.where(lane < 16, rest[5 * b + i], 0.0), 16 * b, 1) for b in range(4)))
        pieces.append(sum(pltpu.roll(jnp.where(lane == 16, rest[i], 0.0), (i + 112) % LANES, 1) for i in range(20)))
        wire_buf[n] = jnp.concatenate(pieces, axis=0).astype(jnp.bfloat16)
        return carry

    lax.fori_loop(0, BATCH, image, 0, unroll=UNROLL)


def match_one(wire, block_of, third_ref, fourth_ref):
    lane8 = lax.broadcasted_iota(jnp.int32, (8, LANES), 1) % HALF == 16
    last = wire[200:208]
    rest = []
    for i in range(20):
        part = wire[160 + 8 * (i % 5) : 168 + 8 * (i % 5)]
        part = pltpu.roll(part, (LANES - 16 * (i // 5)) % LANES, 1)
        rest.append(jnp.where(lane8, pltpu.roll(last, (16 - i) % LANES, 1), part))
    cross = []
    for h, a in enumerate((wire[:P_SIZE], jnp.concatenate(rest, axis=0))):
        straight, swapped = block_of(h).astype(jnp.float32), block_of(2 + h).astype(jnp.float32)
        cross.append((a * straight + pltpu.roll(a, HALF, 1) * swapped).astype(jnp.bfloat16))
    back = jnp.dot(third_ref[...], jnp.concatenate(cross, axis=1), preferred_element_type=jnp.float32)
    back = back.astype(jnp.bfloat16)
    back = jnp.concatenate([back[:P_SIZE], back[P_SIZE:]], axis=1)
    return jnp.dot(back, fourth_ref[...], preferred_element_type=jnp.float32) * (1.0 / float(P_SIZE) ** 3)


def to_rows(low_buf, high_buf, map_ref, peak_ref):
    lane = lax.broadcasted_iota(jnp.int32, (BATCH, LANES), 1)

    def place(m, top):
        load = lambda buf, k: buf[pl.ds(4 * m + k, BATCH, stride=P_SIZE), :]
        low = [load(low_buf, 0)] + [pltpu.roll(load(low_buf, k), 32 * k, 1) for k in range(1, 4)]
        high = [load(high_buf, 0)] + [pltpu.roll(load(high_buf, k), 32 * k, 1) for k in range(1, 4)]
        tiles = [
            low[0],
            jnp.where(lane < 32, high[0], low[1]),
            jnp.where(lane < 32, low[1], jnp.where(lane < 64, high[1], low[2])),
            jnp.where(lane < 64, low[2], jnp.where(lane < 96, high[2], low[3])),
            jnp.where(lane < 96, low[3], high[3]),
        ]
        rows = jnp.concatenate(tiles, axis=1).astype(jnp.bfloat16)
        map_ref[:, pl.ds(pl.multiple_of(640 * m, LANES), 640)] = rows
        for tile in tiles:
            top = jnp.maximum(top, tile)
        return top

    start = jnp.full((BATCH, LANES), -jnp.inf, jnp.float32)
    top = lax.fori_loop(0, P_SIZE // 4, place, start, unroll=2)
    top = jnp.max(top, axis=1, keepdims=True).astype(jnp.bfloat16).astype(jnp.float32)
    peak_ref[...] = jnp.broadcast_to(top, (BATCH, LANES))


MESH = pl.DeviceIdType.MESH
GZ = 8
REACH = 4


def group_barrier(peers):
    barrier = pltpu.get_barrier_semaphore()
    for peer in peers:
        pl.semaphore_signal(barrier, inc=1, device_id=peer, device_id_type=MESH)
    pl.semaphore_wait(barrier, len(peers))


def gz_peers():
    gz, tile = lax.axis_index("gz"), lax.axis_index("tile")
    return [(lax.rem(gz + d, GZ), tile) for d in range(1, GZ)]


def tile_peers(tile_count):
    gz, tile = lax.axis_index("gz"), lax.axis_index("tile")
    offsets = [e for k in range(1, REACH + 1) for e in (k, -k)]
    return offsets, [(gz, lax.rem(tile + e + tile_count, tile_count)) for e in offsets]


def exchange_gz(source_of, held, send, recv):
    gz = lax.axis_index("gz")
    copies = []
    for d, peer in enumerate(gz_peers()):
        copies.append(
            pltpu.make_async_remote_copy(
                src_ref=source_of(peer[0]), dst_ref=held.at[gz], send_sem=send.at[d], recv_sem=recv.at[d],
                device_id=peer, device_id_type=MESH,
            )
        )
    for copy in copies:
        copy.start()
    return copies


def exchange_tiles(tile_count, source, window, send, recv):
    offsets, peers = tile_peers(tile_count)
    copies = []
    for n, (e, peer) in enumerate(zip(offsets, peers)):
        copies.append(
            pltpu.make_async_remote_copy(
                src_ref=source, dst_ref=window.at[REACH - e], send_sem=send.at[n], recv_sem=recv.at[n],
                device_id=peer, device_id_type=MESH,
            )
        )
    for copy in copies:
        copy.start()
    return copies


def request_rows(owner_row, wanted_row, tile_count):
    count = owner_row.shape[1]
    grid = lambda axis: lax.broadcasted_iota(jnp.int32, (count, count), axis)
    owner_col = jnp.sum(jnp.where(grid(0) == grid(1), owner_row, 0), axis=1, keepdims=True)
    same = owner_col == owner_row
    rank = jnp.sum(jnp.where((grid(0) < grid(1)) & same, 1, 0), axis=0, keepdims=True)
    rank_col = jnp.sum(jnp.where((grid(1) < grid(0)) & same, 1, 0), axis=1, keepdims=True)
    hit = owner_row == lax.broadcasted_iota(jnp.int32, (tile_count, count), 0)
    lane = lax.broadcasted_iota(jnp.int32, (tile_count, LANES), 1)
    rows = jnp.zeros((tile_count, LANES), jnp.int32)
    for c in range(CAP):
        asked = jnp.sum(jnp.where(hit & (rank == c), wanted_row, 0), axis=1, keepdims=True)
        rows = jnp.where(lane == c, asked, rows)
    used = owner_col * CAP + rank_col == lax.broadcasted_iota(jnp.int32, (count, LANES), 1)
    block = jnp.sum(jnp.where(used, lax.broadcasted_iota(jnp.int32, (count, LANES), 0), 0), axis=0, keepdims=True)
    return rows, owner_row * CAP + rank, block


FRONT = 32
SPAN = 8 * (2 * REACH + 1)


def whole_kernel(
    tile_count, patch_ref, prior_ref, block_ref, row_ref, want_ref, flow_ref, valid_ref, stiff_ref, first_ref,
    second_ref, third_ref, fourth_ref, map_ref, mesh_ref, rows_buf, block_buf, low_buf, high_buf, wire_buf, send_buf,
    arrived_buf, spec_buf, field_buf, map_buf, peak_buf, own_buf, held, window_buf, ask_buf, heard_buf, list_buf,
    told_buf, index_buf, told_smem, index_smem, conf_own, conf_held, conf_pack, conf_window, s_buf, w_buf, f_buf, u_buf,
    mid_buf, spread_own, spread_held, local, send_r, recv_r, send_a, recv_a, send_b, recv_b, send_f, recv_f, send_p,
    recv_p, send_c, recv_c, send_d, recv_d, send_m, recv_m, send_s, recv_s,
):
    gz, tile = lax.axis_index("gz"), lax.axis_index("tile")
    component, part = lax.rem(gz, 2), gz // 2
    mid_buf[...] = jnp.zeros_like(mid_buf)
    after, before = lax.rem(gz + 1, GZ), lax.rem(gz + GZ - 1, GZ)
    barrier = pltpu.get_barrier_semaphore()

    def greet(peer):
        pl.semaphore_signal(barrier, inc=1, device_id=peer, device_id_type=MESH)

    def greet_tiles(d, carry):
        peer = lax.rem(tile + d, tile_count)
        greet((after, peer))
        greet((before, peer))

        @pl.when(d > 0)
        def _():
            greet((gz, peer))

        return carry

    lax.fori_loop(0, tile_count, greet_tiles, 0)
    for d in range(2, GZ - 1):
        greet((lax.rem(gz + d, GZ), tile))
    for d in (2, 4, 6):
        for e in range(1, REACH + 1):
            for sign in (e, tile_count - e):
                greet((lax.rem(gz + d, GZ), lax.rem(tile + sign, tile_count)))

    from_prior = pltpu.make_async_copy(prior_ref, rows_buf, local.at[0])
    from_patches = pltpu.make_async_copy(patch_ref.at[0], rows_buf, local.at[0])
    load_blocks = pltpu.make_async_copy(block_ref.at[0], block_buf, local.at[1])

    @pl.when(gz == GZ - 1)
    def _():
        from_prior.start()

    @pl.when(gz != GZ - 1)
    def _():
        from_patches.start()

    load_blocks.start()

    rows, slot_row, block_row = request_rows(row_ref[...], want_ref[...], tile_count)
    count = slot_row.shape[1]
    index_buf[0:1, 0:count] = slot_row
    index_buf[1:2, :] = block_row
    index = pltpu.make_async_copy(index_buf, index_smem, local.at[6])
    index.start()
    for j in range(8):
        ask_buf[pl.ds(j, tile_count, stride=8), :] = rows
    columns = stiff_ref.shape[2]
    lane = lax.broadcasted_iota(jnp.int32, (columns, columns), 1)
    order = 2 * lax.rem(lane, columns // 2) + lane // (columns // 2)
    pick = jnp.where(lax.broadcasted_iota(jnp.int32, (columns, columns), 0) == order, 1.0, 0.0).astype(jnp.bfloat16)
    spring = stiff_ref[0] * valid_ref[0].astype(jnp.float32)
    for c in range(2):
        nodes = jnp.concatenate([spring, flow_ref[0, c]], axis=0).astype(jnp.bfloat16)
        own_buf[c] = jnp.dot(nodes, pick, preferred_element_type=jnp.float32).astype(jnp.bfloat16)

    pl.semaphore_wait(barrier, 3 * tile_count - 1 + GZ - 3 + 6 * REACH)

    springs = exchange_gz(lambda peer: own_buf.at[lax.rem(peer, 2)], held, send_a, recv_a)
    mine = pltpu.make_async_copy(own_buf.at[lax.rem(gz, 2)], held.at[gz], local.at[2])
    mine.start()

    def request(d):
        peer = lax.rem(tile + d, tile_count)
        part = lambda t: pl.ds(pl.multiple_of(8 * t, 8), 8)
        return pltpu.make_async_remote_copy(
            src_ref=ask_buf.at[part(peer)], dst_ref=heard_buf.at[part(tile)], send_sem=send_r.at[d],
            recv_sem=recv_r.at[d], device_id=(gz, peer), device_id_type=MESH,
        )

    def each(first, last, act):
        def body(d, carry):
            act(d)
            return carry

        lax.fori_loop(first, last, body, 0)

    each(1, tile_count, lambda d: request(d).start())
    own_part = pl.ds(pl.multiple_of(8 * tile, 8), 8)
    heard_buf[own_part, :] = ask_buf[own_part, :]

    @pl.when(gz == GZ - 1)
    def _():
        from_prior.wait()

    @pl.when(gz != GZ - 1)
    def _():
        from_patches.wait()

    to_images(rows_buf, low_buf, high_buf)

    mine.wait()
    for copy in springs:
        copy.wait()
    springs = exchange_tiles(tile_count, held, window_buf, send_b, recv_b)
    mine = pltpu.make_async_copy(held, window_buf.at[REACH], local.at[2])
    mine.start()
    each(1, tile_count, lambda d: request(d).wait())
    list_buf[...] = heard_buf[pl.ds(0, tile_count, stride=8), :]
    forward = pltpu.make_async_remote_copy(
        src_ref=list_buf, dst_ref=told_buf, send_sem=send_f.at[0], recv_sem=recv_f.at[0], device_id=(before, tile),
        device_id_type=MESH,
    )
    forward.start()
    patch_batch(low_buf, high_buf, first_ref, second_ref, wire_buf)
    forward.wait()
    told = pltpu.make_async_copy(told_buf, told_smem, local.at[3])
    told.start()
    told.wait()

    def parcel(d):
        peer = lax.rem(tile + d, tile_count)
        return pltpu.make_async_remote_copy(
            src_ref=send_buf.at[peer], dst_ref=arrived_buf.at[tile], send_sem=send_p.at[d], recv_sem=recv_p.at[d],
            device_id=(after, peer), device_id_type=MESH,
        )

    halfway = tile_count // 2

    def post(k):
        for d in (k, k + halfway):
            peer = lax.rem(tile + d, tile_count)
            for c in range(CAP):
                send_buf[peer, WIRE * c : WIRE * c + WIRE, :] = wire_buf[told_smem[peer, c]]
            parcel(d).start()

    each(0, halfway, post)

    load_blocks.wait()
    for half in range(2):
        batch = pl.ds(BATCH * half, BATCH)
        to_images(block_buf.at[batch], low_buf, high_buf)
        block_batch(low_buf, high_buf, first_ref, second_ref, spec_buf.at[batch])
    index.wait()
    mine.wait()
    for copy in springs:
        copy.wait()

    def match(k):
        for d in (k, k + halfway):
            parcel(d).wait_recv()
        for d in (k, k + halfway):
            source = lax.rem(tile - d + tile_count, tile_count)
            for c in range(CAP):
                wire = arrived_buf[source, WIRE * c : WIRE * c + WIRE, :].astype(jnp.float32)
                block = index_smem[1, CAP * source + c]
                quarter = lambda q: spec_buf[block, :, LANES * q : LANES * q + LANES]
                field_buf[CAP * source + c] = match_one(wire, quarter, third_ref, fourth_ref)

    each(0, halfway, match)
    stores = []
    for half in range(2):
        batch = pl.ds(BATCH * half, BATCH)

        def collect(n):
            field = field_buf[index_smem[0, BATCH * half + n]]
            at = pl.ds(pl.multiple_of(P_SIZE * n, 8), P_SIZE)
            low_buf[at, :] = field[:, :LANES]
            high_buf[at, :] = field[:, LANES:]

        each(0, BATCH, collect)
        to_rows(low_buf, high_buf, map_buf.at[batch], peak_buf.at[batch])
        stores.append(pltpu.make_async_copy(map_buf.at[batch], map_ref.at[batch], local.at[4 + half]))
        stores[-1].start()

    peak = jnp.concatenate([peak_buf[...]] * (columns // LANES), axis=1)
    block = lax.rem(lax.broadcasted_iota(jnp.int32, (count, columns), 1), columns // 2) // (columns // 2 // count)
    own = block == lax.broadcasted_iota(jnp.int32, (count, columns), 0)
    confidence = jnp.sum(jnp.where(own, peak / (1.0 + peak), 0.0), axis=0, keepdims=True)
    conf_own[...] = jnp.broadcast_to(confidence, conf_own.shape)
    copies = exchange_gz(lambda peer: conf_own, conf_held, send_c, recv_c)
    conf_held[gz] = conf_own[...]
    for buf in (w_buf, f_buf, u_buf):
        buf[...] = jnp.zeros_like(buf)
    for copy in copies:
        copy.wait()
    for s in range(GZ):
        conf_pack[s : s + 1, :] = conf_held[s, 0:1, :]
    copies = exchange_tiles(tile_count, conf_pack, conf_window, send_d, recv_d)
    conf_window[REACH] = conf_pack[...]
    for copy in copies:
        copy.wait()

    first_slot = jnp.maximum(REACH - tile, 0)
    last_slot = jnp.minimum(REACH + tile_count - tile, 2 * REACH + 1)
    lane = lax.broadcasted_iota(jnp.int32, (1, 8, LANES), 2)
    first_lane, last_lane = lane == 0, lane == LANES - 1
    section = lax.broadcasted_iota(jnp.int32, (8, columns), 0)

    def picked(j):
        return jnp.concatenate([s_buf[h, pl.ds(j, 8, stride=16), :] for h in range(2)], axis=1)

    def prepare(k, carry):
        conf = jnp.where(section == 0, 0.0, 0.15 * conf_window[k])
        nodes = window_buf[k].astype(jnp.float32).reshape(LANES, columns)
        s_buf[0], s_buf[1] = nodes[:, :LANES], nodes[:, LANES:]
        for j in range(8):
            i = FRONT + 8 * k + j
            w = picked(j) * conf
            wf = w * picked(8 + j)
            w_buf[i] = w
            f_buf[i] = wf
            u_buf[0, i] = wf - pltpu.roll(wf, 7, 0)
        return carry

    lax.fori_loop(first_slot, last_slot, prepare, 0)

    def step(source, target, s):
        low = jnp.maximum((2 * part + s) // 8, first_slot)
        high = jnp.minimum((2 * part + 2 * PHASE + 2 - s + 7) // 8, last_slot)
        groups = (high - low + GROUP - 1) // GROUP
        low = jnp.where(tile < REACH, low, high - groups * GROUP)

        def group(g, carry):
            i = FRONT + 8 * low + 8 * GROUP * g
            rows = 8 * GROUP
            even, odd = [source[pl.ds(i - 1, rows + 2), :, LANES * h : LANES * h + LANES] for h in range(2)]
            to_left = jnp.where(first_lane, 0.0, pltpu.roll(odd[1:-1], 1, 2))
            to_right = jnp.where(last_lane, 0.0, pltpu.roll(even[1:-1], LANES - 1, 2))
            for h, (x, beside, other) in enumerate(((even, odd[1:-1], to_left), (odd, even[1:-1], to_right))):
                at = (pl.ds(i, rows), slice(None), slice(LANES * h, LANES * h + LANES))
                mid = x[1:-1]
                around = (x[:-2] + x[2:]) + (beside + other)
                force = w_buf[at] * (pltpu.roll(mid, 1, 1) - mid) + f_buf[at]
                target[at] = (0.4 * mid + 0.15 * around) + (force - pltpu.roll(force, 7, 1))
            return carry

        lax.fori_loop(0, groups, group, 0)

    ping, pong = u_buf.at[0], u_buf.at[1]

    def pair(k, carry):
        step(ping, pong, 2 * k + 2)
        step(pong, ping, 2 * k + 3)
        return carry

    def rest_of_phase():
        lax.fori_loop(0, (PHASE - 2) // 2, pair, 0)
        step(ping, pong, PHASE)

    base = FRONT + 8 * REACH + 2 * part
    rest_of_phase()

    place = 4 * tile + part
    places = 4 * tile_count

    def handover(n):
        e = jnp.where(n < 4 * REACH, n + 1, 4 * REACH - 1 - n)
        peer = lax.rem(place + e + places, places)
        row = FRONT + 8 * REACH + 2 * lax.rem(part + e + 4 * REACH, 4) - 2 * e
        copy = pltpu.make_async_remote_copy(
            src_ref=pong.at[pl.ds(base, 2)], dst_ref=mid_buf.at[pl.ds(row, 2)], send_sem=send_m.at[n],
            recv_sem=recv_m.at[n], device_id=(2 * lax.rem(peer, 4) + component, peer // 4), device_id_type=MESH,
        )
        sends = (place + e >= 0) & (place + e < places)
        receives = (place - e >= 0) & (place - e < places)
        return copy, sends, receives

    def hand_out(n):
        copy, sends, _ = handover(n)

        @pl.when(sends)
        def _():
            copy.start()

    def take_in(n):
        copy, sends, receives = handover(n)

        @pl.when(sends)
        def _():
            copy.wait_send()

        @pl.when(receives)
        def _():
            copy.wait_recv()

    each(0, 8 * REACH, hand_out)
    mid_buf[pl.ds(base, 2)] = pong[pl.ds(base, 2)]
    each(0, 8 * REACH, take_in)
    step(mid_buf, ping, 1)
    rest_of_phase()

    for s in range(GZ):
        for r in range(2):
            spread_own[s, r : r + 1, :] = pong[base + r, s : s + 1, :]
    copies = exchange_gz(lambda peer: spread_own.at[peer], spread_held, send_s, recv_s)
    spread_held[gz] = spread_own[gz]
    order = lax.broadcasted_iota(jnp.int32, (columns, columns), 1)
    order = order // 2 + lax.rem(order, 2) * (columns // 2)
    spot = lax.broadcasted_iota(jnp.int32, (columns, columns), 0) == order
    pick = jnp.where(spot, 1.0, 0.0).astype(jnp.bfloat16)
    for copy in copies:
        copy.wait()
    rest = jnp.concatenate([spread_held[2 * h + c, 0:2, :] for c in range(2) for h in range(4)], axis=0)
    total = jnp.zeros_like(rest)
    for _ in range(3):
        piece = rest.astype(jnp.bfloat16)
        rest = rest - piece.astype(jnp.float32)
        total = total + jnp.dot(piece, pick, preferred_element_type=jnp.float32)
    mesh_ref[0] = total[:8]
    mesh_ref[1] = total[8:]
    for copy in stores:
        copy.wait()
    each(0, tile_count, lambda d: parcel(d).wait_send())


def whole(tile_count, patches, prior, blocks, row, want, flows, valid, stiffness, *fixed):
    count = blocks.shape[1]
    columns = flows.shape[3]
    rows = SPAN + 2 * FRONT
    dma = lambda number: pltpu.SemaphoreType.DMA((number,))
    vmem, anywhere = pl.BlockSpec(memory_space=pltpu.VMEM), pl.BlockSpec(memory_space=pl.ANY)
    f32, bf16, i32 = jnp.float32, jnp.bfloat16, jnp.int32
    images = pltpu.VMEM((BATCH * P_SIZE, LANES), f32)
    parcels = pltpu.VMEM((tile_count, CAP * WIRE, LANES), bf16)
    near = pltpu.VMEM((GZ, 8, columns), f32)
    return pl.pallas_call(
        functools.partial(whole_kernel, tile_count),
        out_shape=(
            jax.ShapeDtypeStruct((count, PIX), bf16),
            jax.ShapeDtypeStruct((2, 8, columns), f32),
        ),
        in_specs=[anywhere] * 3 + [vmem] * 9,
        out_specs=(anywhere, vmem),
        scratch_shapes=[
            pltpu.VMEM((BATCH, PIX), bf16),
            pltpu.VMEM((count, PIX), bf16),
            images,
            images,
            pltpu.VMEM((BATCH, WIRE, LANES), bf16),
            parcels,
            parcels,
            pltpu.VMEM((count, P_SIZE, 4 * LANES), bf16),
            pltpu.VMEM((CAP * tile_count, P_SIZE, 2 * LANES), f32),
            pltpu.VMEM((count, PIX), bf16),
            pltpu.VMEM((count, LANES), f32),
            pltpu.VMEM((2, 16, columns), bf16),
            pltpu.VMEM((GZ, 16, columns), bf16),
            pltpu.VMEM((2 * REACH + 1, GZ, 16, columns), bf16),
            pltpu.VMEM((8 * tile_count, LANES), i32),
            pltpu.VMEM((8 * tile_count, LANES), i32),
            pltpu.VMEM((tile_count, LANES), i32),
            pltpu.VMEM((tile_count, LANES), i32),
            pltpu.VMEM((8, LANES), i32),
            pltpu.SMEM((tile_count, LANES), i32),
            pltpu.SMEM((8, LANES), i32),
            pltpu.VMEM((8, columns), f32),
            near,
            pltpu.VMEM((GZ, columns), f32),
            pltpu.VMEM((2 * REACH + 1, GZ, columns), f32),
            pltpu.VMEM((2, LANES, LANES), f32),
            pltpu.VMEM((rows, 8, columns), f32),
            pltpu.VMEM((rows, 8, columns), f32),
            pltpu.VMEM((2, rows, 8, columns), f32),
            pltpu.VMEM((rows, 8, columns), f32),
            near,
            near,
            dma(7),
        ]
        + [dma(tile_count)] * 2
        + [dma(GZ - 1)] * 2
        + [dma(2 * REACH)] * 2
        + [dma(1)] * 2
        + [dma(tile_count)] * 2
        + [dma(GZ - 1)] * 2
        + [dma(2 * REACH)] * 2
        + [dma(8 * REACH)] * 2
        + [dma(GZ - 1)] * 2,
        compiler_params=pltpu.CompilerParams(
            collective_id=1, has_side_effects=True, vmem_limit_bytes=60 * 1024 * 1024
        ),
        cost_estimate=pl.CostEstimate(flops=30_000_000_000, bytes_accessed=32_000_000, transcendentals=0),
    )(patches, prior, blocks, row, want, flows, valid, stiffness, *fixed)


def on_device(patches, prior_patches, blocks, dest, target, flows, valid, stiffness):
    corr_maps, mesh_nodes = whole(
        lax.axis_size("tile"), patches, prior_patches, blocks, dest[:, :, 0], target, flows, valid, stiffness, *tables()
    )
    return (corr_maps[None], mesh_nodes[None])


def solution(mesh):
    return jax.shard_map(
        on_device,
        mesh=mesh,
        in_specs=(
            P("gz", "tile", None),
            P("tile", None),
            P("gz", "tile", None),
            P("gz", "tile", None),
            P("gz", "tile"),
            P("gz", None, "tile", None),
            P("gz", "tile", None),
            P("gz", "tile", None),
        ),
        out_specs=(P("gz", "tile", None), P("gz", None, "tile", None)),
        check_vma=False,
    )
```

time: 193 us -> 154 us (0.80); the launches traced: 190 us -> 154 us
  Pallas kernels: 181 us -> 150 us
  local copies, waits for them, and re-layouts: 6.74 us -> 3.31 us
    pallas_call x5 -> x1, Pallas kernels: 181 us -> 150 us  [whole(): pl.pallas_call(functools.partial(whole_kernel, tile_count), out_shape=(ja...]
    unnamed x15 -> x4, local copies, waits for them, and re-layouts: 5.4 us -> 3.31 us
where the time goes in v6:
time: 154 us
  Pallas kernels  150 us (97%)
  local copies, waits for them, and re-layouts  3.31 us (2%)
    pallas_call x1, Pallas kernels, whole(): pl.pallas_call(functools.partial(whole_kernel, tile_count), out_shape=(ja...  150 us
    unnamed x4, local copies, waits for them, and re-layouts  3.31 us

profile of v6, /device:TPU:33, one launch (start us, length us, event | category | flops | bytes accessed | tf_op | source)
XLA Modules:
  0.0 153.9 jit_solution(17279165750135697097)
XLA Ops:
  0.6 149.9 %shard_map.131 = (bf16[32,25600]{1,0:T(8,128)(2,1)}, f32[2,8,256]{2,1,0:T(8,128)}) custom-call(bf16[1,16,25600]{2,1,0:T(8,128)(2,1)} %patch_ref.1, bf16[16,25600]{1,0:T(8,128)(2,1)} %prior_ref.1, bf16[1,32,25600]{2,1,0:T(8,128)(2,1)} %block_ref.1, s32[1,32]{1,0:T(1,128)} %bitcast.5, s32[1,32]{1,0:T(1,128)} %want_ref.1, f32[1,2,8,256]{3,2,1,0:T(8,128)} %flow_ref.1, ...), custom_call_target="tpu_custom_call" | custom-call | flops 30000001024 | bytes 32000000 | tf_op jit(solution)/shard_map/pallas_call | solution.py:572
  150.6 0.0 copy-start
  150.6 2.7 %copy.16 = bf16[1,32,25600]{2,1,0:T(8,128)(2,1)} copy(bf16[1,32,25600]{2,1,0:T(8,128)(2,1)} %bitcast.3) | data formatting | bytes 3276800
  153.3 0.0 copy-done
  153.3 0.6 copy.17
Async XLA Ops:
  150.6 2.7 %copy-start = (f32[2,8,256]{2,1,0:T(8,128)S(1)}, f32[2,8,256]{2,1,0:T(8,128)}, u32[]{:S(2)}) copy-start(f32[2,8,256]{2,1,0:T(8,128)} %get-tuple-element.5) | copy-start | bytes 49156

commit v7 on v6

--- a/solution.py
+++ b/solution.py
@@ -13,7 +13,6 @@
 PIX = 25600
 CAP = 2
 ITERS = 64
-GROUP = 4
 PHASE = ITERS // 2
 UNROLL = 8
 
@@ -141,10 +140,10 @@
     return jnp.dot(back, fourth_ref[...], preferred_element_type=jnp.float32) * (1.0 / float(P_SIZE) ** 3)
 
 
-def to_rows(low_buf, high_buf, map_ref, peak_ref):
+def to_rows(low_buf, high_buf, map_ref):
     lane = lax.broadcasted_iota(jnp.int32, (BATCH, LANES), 1)
 
-    def place(m, top):
+    def place(m, carry):
         load = lambda buf, k: buf[pl.ds(4 * m + k, BATCH, stride=P_SIZE), :]
         low = [load(low_buf, 0)] + [pltpu.roll(load(low_buf, k), 32 * k, 1) for k in range(1, 4)]
         high = [load(high_buf, 0)] + [pltpu.roll(load(high_buf, k), 32 * k, 1) for k in range(1, 4)]
@@ -157,14 +156,9 @@
         ]
         rows = jnp.concatenate(tiles, axis=1).astype(jnp.bfloat16)
         map_ref[:, pl.ds(pl.multiple_of(640 * m, LANES), 640)] = rows
-        for tile in tiles:
-            top = jnp.maximum(top, tile)
-        return top
-
-    start = jnp.full((BATCH, LANES), -jnp.inf, jnp.float32)
-    top = lax.fori_loop(0, P_SIZE // 4, place, start, unroll=2)
-    top = jnp.max(top, axis=1, keepdims=True).astype(jnp.bfloat16).astype(jnp.float32)
-    peak_ref[...] = jnp.broadcast_to(top, (BATCH, LANES))
+        return carry
+
+    lax.fori_loop(0, P_SIZE // 4, place, 0, unroll=2)
 
 
 MESH = pl.DeviceIdType.MESH
@@ -245,9 +239,9 @@
 def whole_kernel(
     tile_count, patch_ref, prior_ref, block_ref, row_ref, want_ref, flow_ref, valid_ref, stiff_ref, first_ref,
     second_ref, third_ref, fourth_ref, map_ref, mesh_ref, rows_buf, block_buf, low_buf, high_buf, wire_buf, send_buf,
-    arrived_buf, spec_buf, field_buf, map_buf, peak_buf, own_buf, held, window_buf, ask_buf, heard_buf, list_buf,
-    told_buf, index_buf, told_smem, index_smem, conf_own, conf_held, conf_pack, conf_window, s_buf, w_buf, f_buf, u_buf,
-    mid_buf, spread_own, spread_held, local, send_r, recv_r, send_a, recv_a, send_b, recv_b, send_f, recv_f, send_p,
+    arrived_buf, spec_buf, field_buf, map_buf, slot_peak, peak_buf, own_buf, held, window_buf, ask_buf, heard_buf, list_buf,
+    index_buf, told_smem, index_smem, conf_own, conf_held, conf_pack, conf_window, s_buf, w_buf, f_buf, u_buf,
+    mid_buf, spread_own, spread_held, local, send_r, recv_r, send_a, recv_a, send_b, recv_b, send_p,
     recv_p, send_c, recv_c, send_d, recv_d, send_m, recv_m, send_s, recv_s,
 ):
     gz, tile = lax.axis_index("gz"), lax.axis_index("tile")
@@ -264,16 +258,12 @@
         greet((after, peer))
         greet((before, peer))
 
-        @pl.when(d > 0)
-        def _():
-            greet((gz, peer))
-
         return carry
 
     lax.fori_loop(0, tile_count, greet_tiles, 0)
     for d in range(2, GZ - 1):
         greet((lax.rem(gz + d, GZ), tile))
-    for d in (2, 4, 6):
+    for d in (0, 2, 4, 6):
         for e in range(1, REACH + 1):
             for sign in (e, tile_count - e):
                 greet((lax.rem(gz + d, GZ), lax.rem(tile + sign, tile_count)))
@@ -309,7 +299,17 @@
         nodes = jnp.concatenate([spring, flow_ref[0, c]], axis=0).astype(jnp.bfloat16)
         own_buf[c] = jnp.dot(nodes, pick, preferred_element_type=jnp.float32).astype(jnp.bfloat16)
 
-    pl.semaphore_wait(barrier, 3 * tile_count - 1 + GZ - 3 + 6 * REACH)
+    @pl.when(gz == GZ - 1)
+    def _():
+        from_prior.wait()
+
+    @pl.when(gz != GZ - 1)
+    def _():
+        from_patches.wait()
+
+    to_images(rows_buf, low_buf, high_buf)
+
+    pl.semaphore_wait(barrier, 2 * tile_count + GZ - 3 + 8 * REACH)
 
     springs = exchange_gz(lambda peer: own_buf.at[lax.rem(peer, 2)], held, send_a, recv_a)
     mine = pltpu.make_async_copy(own_buf.at[lax.rem(gz, 2)], held.at[gz], local.at[2])
@@ -320,7 +320,7 @@
         part = lambda t: pl.ds(pl.multiple_of(8 * t, 8), 8)
         return pltpu.make_async_remote_copy(
             src_ref=ask_buf.at[part(peer)], dst_ref=heard_buf.at[part(tile)], send_sem=send_r.at[d],
-            recv_sem=recv_r.at[d], device_id=(gz, peer), device_id_type=MESH,
+            recv_sem=recv_r.at[d], device_id=(before, peer), device_id_type=MESH,
         )
 
     def each(first, last, act):
@@ -330,19 +330,7 @@
 
         lax.fori_loop(first, last, body, 0)
 
-    each(1, tile_count, lambda d: request(d).start())
-    own_part = pl.ds(pl.multiple_of(8 * tile, 8), 8)
-    heard_buf[own_part, :] = ask_buf[own_part, :]
-
-    @pl.when(gz == GZ - 1)
-    def _():
-        from_prior.wait()
-
-    @pl.when(gz != GZ - 1)
-    def _():
-        from_patches.wait()
-
-    to_images(rows_buf, low_buf, high_buf)
+    each(0, tile_count, lambda d: request(d).start())
 
     mine.wait()
     for copy in springs:
@@ -350,17 +338,11 @@
     springs = exchange_tiles(tile_count, held, window_buf, send_b, recv_b)
     mine = pltpu.make_async_copy(held, window_buf.at[REACH], local.at[2])
     mine.start()
-    each(1, tile_count, lambda d: request(d).wait())
+    each(0, tile_count, lambda d: request(d).wait())
     list_buf[...] = heard_buf[pl.ds(0, tile_count, stride=8), :]
-    forward = pltpu.make_async_remote_copy(
-        src_ref=list_buf, dst_ref=told_buf, send_sem=send_f.at[0], recv_sem=recv_f.at[0], device_id=(before, tile),
-        device_id_type=MESH,
-    )
-    forward.start()
+    told = pltpu.make_async_copy(list_buf, told_smem, local.at[3])
+    told.start()
     patch_batch(low_buf, high_buf, first_ref, second_ref, wire_buf)
-    forward.wait()
-    told = pltpu.make_async_copy(told_buf, told_smem, local.at[3])
-    told.start()
     told.wait()
 
     def parcel(d):
@@ -380,6 +362,8 @@
             parcel(d).start()
 
     each(0, halfway, post)
+    for buf in (w_buf, f_buf, u_buf):
+        buf[...] = jnp.zeros_like(buf)
 
     load_blocks.wait()
     for half in range(2):
@@ -391,6 +375,8 @@
     for copy in springs:
         copy.wait()
 
+    inner = lax.broadcasted_iota(jnp.int32, (P_SIZE, LANES), 1) < P_SIZE - LANES
+
     def match(k):
         for d in (k, k + halfway):
             parcel(d).wait_recv()
@@ -400,11 +386,15 @@
                 wire = arrived_buf[source, WIRE * c : WIRE * c + WIRE, :].astype(jnp.float32)
                 block = index_smem[1, CAP * source + c]
                 quarter = lambda q: spec_buf[block, :, LANES * q : LANES * q + LANES]
-                field_buf[CAP * source + c] = match_one(wire, quarter, third_ref, fourth_ref)
+                field = match_one(wire, quarter, third_ref, fourth_ref)
+                field_buf[CAP * source + c] = field
+                top = jnp.maximum(field[:, :LANES], jnp.where(inner, field[:, LANES:], field[:, :LANES]))
+                top = jnp.max(jnp.max(top, axis=0, keepdims=True), axis=1, keepdims=True)
+                slot_peak[pl.ds(CAP * source + c, 1), :] = jnp.broadcast_to(top, (1, LANES))
 
     each(0, halfway, match)
-    stores = []
-    for half in range(2):
+
+    def store_maps(half):
         batch = pl.ds(BATCH * half, BATCH)
 
         def collect(n):
@@ -414,25 +404,29 @@
             high_buf[at, :] = field[:, LANES:]
 
         each(0, BATCH, collect)
-        to_rows(low_buf, high_buf, map_buf.at[batch], peak_buf.at[batch])
-        stores.append(pltpu.make_async_copy(map_buf.at[batch], map_ref.at[batch], local.at[4 + half]))
-        stores[-1].start()
-
-    peak = jnp.concatenate([peak_buf[...]] * (columns // LANES), axis=1)
+        to_rows(low_buf, high_buf, map_buf.at[batch])
+        store = pltpu.make_async_copy(map_buf.at[batch], map_ref.at[batch], local.at[4 + half])
+        store.start()
+        return store
+
+    for n in range(count):
+        peak_buf[n : n + 1, :] = slot_peak[pl.ds(index_smem[0, n], 1), :]
+    peak = peak_buf[...].astype(jnp.bfloat16).astype(jnp.float32)
+    peak = jnp.concatenate([peak] * (columns // LANES), axis=1)
     block = lax.rem(lax.broadcasted_iota(jnp.int32, (count, columns), 1), columns // 2) // (columns // 2 // count)
     own = block == lax.broadcasted_iota(jnp.int32, (count, columns), 0)
     confidence = jnp.sum(jnp.where(own, peak / (1.0 + peak), 0.0), axis=0, keepdims=True)
     conf_own[...] = jnp.broadcast_to(confidence, conf_own.shape)
     copies = exchange_gz(lambda peer: conf_own, conf_held, send_c, recv_c)
     conf_held[gz] = conf_own[...]
-    for buf in (w_buf, f_buf, u_buf):
-        buf[...] = jnp.zeros_like(buf)
+    stores = [store_maps(0)]
     for copy in copies:
         copy.wait()
     for s in range(GZ):
         conf_pack[s : s + 1, :] = conf_held[s, 0:1, :]
     copies = exchange_tiles(tile_count, conf_pack, conf_window, send_d, recv_d)
     conf_window[REACH] = conf_pack[...]
+    stores.append(store_maps(1))
     for copy in copies:
         copy.wait()
 
@@ -463,12 +457,10 @@
     def step(source, target, s):
         low = jnp.maximum((2 * part + s) // 8, first_slot)
         high = jnp.minimum((2 * part + 2 * PHASE + 2 - s + 7) // 8, last_slot)
-        groups = (high - low + GROUP - 1) // GROUP
-        low = jnp.where(tile < REACH, low, high - groups * GROUP)
-
-        def group(g, carry):
-            i = FRONT + 8 * low + 8 * GROUP * g
-            rows = 8 * GROUP
+        i = FRONT + 8 * low
+
+        def advance(slots):
+            rows = 8 * slots
             even, odd = [source[pl.ds(i - 1, rows + 2), :, LANES * h : LANES * h + LANES] for h in range(2)]
             to_left = jnp.where(first_lane, 0.0, pltpu.roll(odd[1:-1], 1, 2))
             to_right = jnp.where(last_lane, 0.0, pltpu.roll(even[1:-1], LANES - 1, 2))
@@ -478,20 +470,21 @@
                 around = (x[:-2] + x[2:]) + (beside + other)
                 force = w_buf[at] * (pltpu.roll(mid, 1, 1) - mid) + f_buf[at]
                 target[at] = (0.4 * mid + 0.15 * around) + (force - pltpu.roll(force, 7, 1))
-            return carry
-
-        lax.fori_loop(0, groups, group, 0)
+
+        for slots in range(1, 2 * REACH + 2):
+
+            @pl.when(high - low == slots)
+            def _():
+                advance(slots)
 
     ping, pong = u_buf.at[0], u_buf.at[1]
 
-    def pair(k, carry):
-        step(ping, pong, 2 * k + 2)
-        step(pong, ping, 2 * k + 3)
+    def run_step(s, carry):
+        step(u_buf.at[lax.rem(s, 2)], u_buf.at[1 - lax.rem(s, 2)], s)
         return carry
 
     def rest_of_phase():
-        lax.fori_loop(0, (PHASE - 2) // 2, pair, 0)
-        step(ping, pong, PHASE)
+        lax.fori_loop(2, PHASE + 1, run_step, 0)
 
     base = FRONT + 8 * REACH + 2 * part
     rest_of_phase()
@@ -588,13 +581,13 @@
             pltpu.VMEM((count, P_SIZE, 4 * LANES), bf16),
             pltpu.VMEM((CAP * tile_count, P_SIZE, 2 * LANES), f32),
             pltpu.VMEM((count, PIX), bf16),
+            pltpu.VMEM((CAP * tile_count, LANES), f32),
             pltpu.VMEM((count, LANES), f32),
             pltpu.VMEM((2, 16, columns), bf16),
             pltpu.VMEM((GZ, 16, columns), bf16),
             pltpu.VMEM((2 * REACH + 1, GZ, 16, columns), bf16),
             pltpu.VMEM((8 * tile_count, LANES), i32),
             pltpu.VMEM((8 * tile_count, LANES), i32),
-            pltpu.VMEM((tile_count, LANES), i32),
             pltpu.VMEM((tile_count, LANES), i32),
             pltpu.VMEM((8, LANES), i32),
             pltpu.SMEM((tile_count, LANES), i32),
@@ -615,7 +608,6 @@
         + [dma(tile_count)] * 2
         + [dma(GZ - 1)] * 2
         + [dma(2 * REACH)] * 2
-        + [dma(1)] * 2
         + [dma(tile_count)] * 2
         + [dma(GZ - 1)] * 2
         + [dma(2 * REACH)] * 2

time: 154 us -> 147 us (0.955)
  Pallas kernels: 150 us -> 143 us
    pallas_call x1, Pallas kernels: 150 us -> 143 us  [whole(): pl.pallas_call(functools.partial(whole_kernel, tile_count), out_shape=(ja...]
where the time goes in v7:
time: 147 us
  Pallas kernels  143 us (97%)
  local copies, waits for them, and re-layouts  3.31 us (2%)
    pallas_call x1, Pallas kernels, whole(): pl.pallas_call(functools.partial(whole_kernel, tile_count), out_shape=(ja...  143 us
    unnamed x4, local copies, waits for them, and re-layouts  3.31 us

profile of v7, /device:TPU:33, one launch (start us, length us, event | category | flops | bytes accessed | tf_op | source)
XLA Modules:
  0.0 147.0 jit_solution(4011108809645937304)
XLA Ops:
  0.6 143.0 %shard_map.131 = (bf16[32,25600]{1,0:T(8,128)(2,1)}, f32[2,8,256]{2,1,0:T(8,128)}) custom-call(bf16[1,16,25600]{2,1,0:T(8,128)(2,1)} %patch_ref.1, bf16[16,25600]{1,0:T(8,128)(2,1)} %prior_ref.1, bf16[1,32,25600]{2,1,0:T(8,128)(2,1)} %block_ref.1, s32[1,32]{1,0:T(1,128)} %bitcast.5, s32[1,32]{1,0:T(1,128)} %want_ref.1, f32[1,2,8,256]{3,2,1,0:T(8,128)} %flow_ref.1, ...), custom_call_target="tpu_custom_call" | custom-call | flops 30000001024 | bytes 32000000 | tf_op jit(solution)/shard_map/pallas_call | solution.py:565
  143.7 0.0 copy-start
  143.7 2.7 %copy.16 = bf16[1,32,25600]{2,1,0:T(8,128)(2,1)} copy(bf16[1,32,25600]{2,1,0:T(8,128)(2,1)} %bitcast.3) | data formatting | bytes 3276800
  146.4 0.0 copy-done
  146.4 0.6 copy.17
Async XLA Ops:
  143.7 2.7 %copy-start = (f32[2,8,256]{2,1,0:T(8,128)S(1)}, f32[2,8,256]{2,1,0:T(8,128)}, u32[]{:S(2)}) copy-start(f32[2,8,256]{2,1,0:T(8,128)} %get-tuple-element.5) | copy-start | bytes 49156

commit v8 on v7

--- a/solution.py
+++ b/solution.py
@@ -214,22 +214,23 @@
     return copies
 
 
-def request_rows(owner_row, wanted_row, tile_count):
+def request_rows(owner_row, wanted_row):
     count = owner_row.shape[1]
     grid = lambda axis: lax.broadcasted_iota(jnp.int32, (count, count), axis)
-    owner_col = jnp.sum(jnp.where(grid(0) == grid(1), owner_row, 0), axis=1, keepdims=True)
+    column = lambda row: jnp.sum(jnp.where(grid(0) == grid(1), row, 0), axis=1, keepdims=True)
+    owner_col = column(owner_row)
     same = owner_col == owner_row
     rank = jnp.sum(jnp.where((grid(0) < grid(1)) & same, 1, 0), axis=0, keepdims=True)
     rank_col = jnp.sum(jnp.where((grid(1) < grid(0)) & same, 1, 0), axis=1, keepdims=True)
-    hit = owner_row == lax.broadcasted_iota(jnp.int32, (tile_count, count), 0)
-    lane = lax.broadcasted_iota(jnp.int32, (tile_count, LANES), 1)
-    rows = jnp.zeros((tile_count, LANES), jnp.int32)
-    for c in range(CAP):
-        asked = jnp.sum(jnp.where(hit & (rank == c), wanted_row, 0), axis=1, keepdims=True)
-        rows = jnp.where(lane == c, asked, rows)
     used = owner_col * CAP + rank_col == lax.broadcasted_iota(jnp.int32, (count, LANES), 1)
-    block = jnp.sum(jnp.where(used, lax.broadcasted_iota(jnp.int32, (count, LANES), 0), 0), axis=0, keepdims=True)
-    return rows, owner_row * CAP + rank, block
+    total = lambda values: jnp.sum(jnp.where(used, values, 0), axis=0, keepdims=True)
+    block = total(lax.broadcasted_iota(jnp.int32, (count, LANES), 0))
+    return owner_row * CAP + rank, block, total(column(wanted_row))
+
+
+SIDE = 4
+STEPS = 2
+KINDS = ((0, 0), (-1, 0), (1, 0), (-2, 0), (2, 0), (-2, 1), (2, -1), (-2, 2), (2, -2))
 
 
 FRONT = 32
@@ -239,28 +240,35 @@
 def whole_kernel(
     tile_count, patch_ref, prior_ref, block_ref, row_ref, want_ref, flow_ref, valid_ref, stiff_ref, first_ref,
     second_ref, third_ref, fourth_ref, map_ref, mesh_ref, rows_buf, block_buf, low_buf, high_buf, wire_buf, send_buf,
-    arrived_buf, spec_buf, field_buf, map_buf, slot_peak, peak_buf, own_buf, held, window_buf, ask_buf, heard_buf, list_buf,
-    index_buf, told_smem, index_smem, conf_own, conf_held, conf_pack, conf_window, s_buf, w_buf, f_buf, u_buf,
-    mid_buf, spread_own, spread_held, local, send_r, recv_r, send_a, recv_a, send_b, recv_b, send_p,
+    arrived_buf, spec_buf, field_buf, map_buf, slot_peak, peak_buf, own_buf, held, window_buf, near_up, far_up, near_down, far_down, ask_buf, heard_buf,
+    list_buf, index_buf, told_smem, index_smem, conf_own, conf_held, conf_pack, conf_window, s_buf, w_buf, f_buf, u_buf,
+    mid_buf, mid_wire, mid_own, spread_own, spread_held, local, send_r, recv_r, send_a, recv_a, send_b, recv_b, send_h, recv_h, send_p,
     recv_p, send_c, recv_c, send_d, recv_d, send_m, recv_m, send_s, recv_s,
 ):
     gz, tile = lax.axis_index("gz"), lax.axis_index("tile")
     component, part = lax.rem(gz, 2), gz // 2
-    mid_buf[...] = jnp.zeros_like(mid_buf)
+    mid_wire[...] = jnp.zeros_like(mid_wire)
     after, before = lax.rem(gz + 1, GZ), lax.rem(gz + GZ - 1, GZ)
     barrier = pltpu.get_barrier_semaphore()
 
     def greet(peer):
         pl.semaphore_signal(barrier, inc=1, device_id=peer, device_id_type=MESH)
 
-    def greet_tiles(d, carry):
-        peer = lax.rem(tile + d, tile_count)
+    plane, spot_in_plane = tile // SIDE, lax.rem(tile, SIDE)
+    planes = tile_count // SIDE
+
+    def tile_at(offset, y):
+        return lax.rem(plane + offset + planes, planes) * SIDE + y
+
+    def greet_planes(n, carry):
+        peer = tile_at(n // SIDE - STEPS, lax.rem(n, SIDE))
         greet((after, peer))
         greet((before, peer))
-
         return carry
 
-    lax.fori_loop(0, tile_count, greet_tiles, 0)
+    asks = SIDE * (2 * STEPS + 1)
+    heard_buf[8 * asks :, :] = jnp.zeros((heard_buf.shape[0] - 8 * asks, LANES), jnp.int32)
+    lax.fori_loop(0, asks, greet_planes, 0)
     for d in range(2, GZ - 1):
         greet((lax.rem(gz + d, GZ), tile))
     for d in (0, 2, 4, 6):
@@ -282,14 +290,13 @@
 
     load_blocks.start()
 
-    rows, slot_row, block_row = request_rows(row_ref[...], want_ref[...], tile_count)
+    slot_row, block_row, asked_row = request_rows(row_ref[...], want_ref[...])
     count = slot_row.shape[1]
     index_buf[0:1, 0:count] = slot_row
     index_buf[1:2, :] = block_row
     index = pltpu.make_async_copy(index_buf, index_smem, local.at[6])
     index.start()
-    for j in range(8):
-        ask_buf[pl.ds(j, tile_count, stride=8), :] = rows
+    ask_buf[...] = jnp.broadcast_to(asked_row, ask_buf.shape)
     columns = stiff_ref.shape[2]
     lane = lax.broadcasted_iota(jnp.int32, (columns, columns), 1)
     order = 2 * lax.rem(lane, columns // 2) + lane // (columns // 2)
@@ -309,18 +316,17 @@
 
     to_images(rows_buf, low_buf, high_buf)
 
-    pl.semaphore_wait(barrier, 2 * tile_count + GZ - 3 + 8 * REACH)
+    pl.semaphore_wait(barrier, 2 * asks + GZ - 3 + 8 * REACH)
 
     springs = exchange_gz(lambda peer: own_buf.at[lax.rem(peer, 2)], held, send_a, recv_a)
     mine = pltpu.make_async_copy(own_buf.at[lax.rem(gz, 2)], held.at[gz], local.at[2])
     mine.start()
 
-    def request(d):
-        peer = lax.rem(tile + d, tile_count)
-        part = lambda t: pl.ds(pl.multiple_of(8 * t, 8), 8)
+    def request(n, landing):
+        peer = tile_at(n // SIDE - STEPS, lax.rem(n, SIDE))
         return pltpu.make_async_remote_copy(
-            src_ref=ask_buf.at[part(peer)], dst_ref=heard_buf.at[part(tile)], send_sem=send_r.at[d],
-            recv_sem=recv_r.at[d], device_id=(before, peer), device_id_type=MESH,
+            src_ref=ask_buf, dst_ref=heard_buf.at[pl.ds(pl.multiple_of(8 * landing, 8), 8)], send_sem=send_r.at[n],
+            recv_sem=recv_r.at[landing], device_id=(before, peer), device_id_type=MESH,
         )
 
     def each(first, last, act):
@@ -330,7 +336,7 @@
 
         lax.fori_loop(first, last, body, 0)
 
-    each(0, tile_count, lambda d: request(d).start())
+    each(0, asks, lambda n: request(n, n // SIDE * SIDE + spot_in_plane).start())
 
     mine.wait()
     for copy in springs:
@@ -338,61 +344,119 @@
     springs = exchange_tiles(tile_count, held, window_buf, send_b, recv_b)
     mine = pltpu.make_async_copy(held, window_buf.at[REACH], local.at[2])
     mine.start()
-    each(0, tile_count, lambda d: request(d).wait())
-    list_buf[...] = heard_buf[pl.ds(0, tile_count, stride=8), :]
+    each(0, asks, lambda n: request(n, n).wait())
+    list_buf[...] = heard_buf[pl.ds(0, list_buf.shape[0], stride=8), :]
     told = pltpu.make_async_copy(list_buf, told_smem, local.at[3])
     told.start()
     patch_batch(low_buf, high_buf, first_ref, second_ref, wire_buf)
     told.wait()
 
-    def parcel(d):
-        peer = lax.rem(tile + d, tile_count)
+    def hop(up, far, chunk):
+        near, end = (near_up, far_up) if up else (near_down, far_down)
+        batch = pl.ds(BATCH // 2 * chunk, BATCH // 2)
+        number = 4 * int(up) + 2 * int(far) + chunk
         return pltpu.make_async_remote_copy(
-            src_ref=send_buf.at[peer], dst_ref=arrived_buf.at[tile], send_sem=send_p.at[d], recv_sem=recv_p.at[d],
-            device_id=(after, peer), device_id_type=MESH,
+            src_ref=(near if far else wire_buf).at[batch], dst_ref=(end if far else near).at[batch],
+            send_sem=send_h.at[number], recv_sem=recv_h.at[number],
+            device_id=(gz, tile_at(1 if up else -1, spot_in_plane)), device_id_type=MESH,
         )
 
-    halfway = tile_count // 2
-
-    def post(k):
-        for d in (k, k + halfway):
-            peer = lax.rem(tile + d, tile_count)
-            for c in range(CAP):
-                send_buf[peer, WIRE * c : WIRE * c + WIRE, :] = wire_buf[told_smem[peer, c]]
-            parcel(d).start()
-
-    each(0, halfway, post)
-    for buf in (w_buf, f_buf, u_buf):
+    def parcel(kind, y_to, source, landing):
+        if isinstance(kind, int) and kind >= 7:
+            half = pl.ds(WIRE * (kind - 7), WIRE)
+            outgoing, incoming = send_buf.at[28 + y_to, half], arrived_buf.at[source, half]
+        else:
+            outgoing, incoming = send_buf.at[SIDE * kind + y_to], arrived_buf.at[source]
+        reach = KINDS[kind][1] if isinstance(kind, int) else 0
+        return pltpu.make_async_remote_copy(
+            src_ref=outgoing, dst_ref=incoming, send_sem=send_p.at[SIDE * kind + y_to],
+            recv_sem=recv_p.at[SIDE * kind + landing], device_id=(after, tile_at(reach, y_to)), device_id_type=MESH,
+        )
+
+    def post(kind, held_patches):
+        offset, reach = KINDS[kind]
+        source = tile_at(offset, spot_in_plane)
+
+        def one(y):
+            listed = (STEPS - reach) * SIDE + y
+            for c in range(CAP) if kind < 7 else (kind - 7,):
+                entry, half = (SIDE * kind + y, c) if kind < 7 else (28 + y, c)
+                patch = held_patches[told_smem[listed, CAP * source + c]]
+                send_buf[entry, WIRE * half : WIRE * half + WIRE, :] = patch
+            parcel(kind, y, source, spot_in_plane).start()
+
+        each(0, SIDE, one)
+
+    for chunk in range(2):
+        for up in (True, False):
+            hop(up, False, chunk).start()
+    post(0, wire_buf)
+    for buf in (w_buf, f_buf, u_buf, mid_buf):
         buf[...] = jnp.zeros_like(buf)
 
     load_blocks.wait()
     for half in range(2):
         batch = pl.ds(BATCH * half, BATCH)
         to_images(block_buf.at[batch], low_buf, high_buf)
+        if half == 0:
+            for up in (True, False):
+                hop(up, False, 0).wait_recv()
+                hop(up, True, 0).start()
         block_batch(low_buf, high_buf, first_ref, second_ref, spec_buf.at[batch])
+    for up in (True, False):
+        hop(up, False, 1).wait_recv()
+        hop(up, True, 1).start()
+    post(1, near_up)
+    post(2, near_down)
     index.wait()
     mine.wait()
     for copy in springs:
         copy.wait()
-
     inner = lax.broadcasted_iota(jnp.int32, (P_SIZE, LANES), 1) < P_SIZE - LANES
 
-    def match(k):
-        for d in (k, k + halfway):
-            parcel(d).wait_recv()
-        for d in (k, k + halfway):
-            source = lax.rem(tile - d + tile_count, tile_count)
+    def match_slot(source, c):
+        wire = arrived_buf[source, WIRE * c : WIRE * c + WIRE, :].astype(jnp.float32)
+        block = index_smem[1, CAP * source + c]
+        quarter = lambda q: spec_buf[block, :, LANES * q : LANES * q + LANES]
+        field = match_one(wire, quarter, third_ref, fourth_ref)
+        field_buf[CAP * source + c] = field
+        top = jnp.maximum(field[:, :LANES], jnp.where(inner, field[:, LANES:], field[:, :LANES]))
+        top = jnp.max(jnp.max(top, axis=0, keepdims=True), axis=1, keepdims=True)
+        slot_peak[pl.ds(CAP * source + c, 1), :] = jnp.broadcast_to(top, (1, LANES))
+
+    def match(n):
+        kind = n // 2
+        away = (kind + 1) // 2
+        offset = jnp.where(lax.rem(kind, 2) == 1, -away, away)
+        pairs = []
+        for y in (2 * lax.rem(n, 2), 2 * lax.rem(n, 2) + 1):
+            source = tile_at(offset, y)
+            parcel(kind, y, source, y).wait_recv()
+            pairs.append(source)
+        for source in pairs:
             for c in range(CAP):
-                wire = arrived_buf[source, WIRE * c : WIRE * c + WIRE, :].astype(jnp.float32)
-                block = index_smem[1, CAP * source + c]
-                quarter = lambda q: spec_buf[block, :, LANES * q : LANES * q + LANES]
-                field = match_one(wire, quarter, third_ref, fourth_ref)
-                field_buf[CAP * source + c] = field
-                top = jnp.maximum(field[:, :LANES], jnp.where(inner, field[:, LANES:], field[:, :LANES]))
-                top = jnp.max(jnp.max(top, axis=0, keepdims=True), axis=1, keepdims=True)
-                slot_peak[pl.ds(CAP * source + c, 1), :] = jnp.broadcast_to(top, (1, LANES))
-
-    each(0, halfway, match)
+                match_slot(source, c)
+
+    each(0, 2, match)
+    for chunk in range(2):
+        for up in (True, False):
+            hop(up, True, chunk).wait_recv()
+    for kind, held_patches in ((7, far_up), (8, far_down), (5, far_up), (6, far_down), (3, far_up), (4, far_down)):
+        post(kind, held_patches)
+    each(2, 14, match)
+
+    def match_halfway(n):
+        pairs = []
+        for y in (2 * n, 2 * n + 1):
+            source = tile_at(planes // 2, y)
+            for kind in (7, 8):
+                parcel(kind, y, source, y).wait_recv()
+            pairs.append(source)
+        for source in pairs:
+            for c in range(CAP):
+                match_slot(source, c)
+
+    each(0, SIDE // 2, match_halfway)
 
     def store_maps(half):
         batch = pl.ds(BATCH * half, BATCH)
@@ -497,7 +561,7 @@
         peer = lax.rem(place + e + places, places)
         row = FRONT + 8 * REACH + 2 * lax.rem(part + e + 4 * REACH, 4) - 2 * e
         copy = pltpu.make_async_remote_copy(
-            src_ref=pong.at[pl.ds(base, 2)], dst_ref=mid_buf.at[pl.ds(row, 2)], send_sem=send_m.at[n],
+            src_ref=mid_own, dst_ref=mid_wire.at[row // 2], send_sem=send_m.at[n],
             recv_sem=recv_m.at[n], device_id=(2 * lax.rem(peer, 4) + component, peer // 4), device_id_type=MESH,
         )
         sends = (place + e >= 0) & (place + e < places)
@@ -522,9 +586,15 @@
         def _():
             copy.wait_recv()
 
+    mid_own[...] = pong[pl.ds(base, 2)].reshape(mid_own.shape).astype(jnp.bfloat16)
     each(0, 8 * REACH, hand_out)
+    each(0, 8 * REACH, take_in)
+
+    def widen(p):
+        mid_buf[pl.ds(2 * p, 2)] = mid_wire[p].astype(jnp.float32).reshape(2, 8, columns)
+
+    each(FRONT // 2, (FRONT + SPAN) // 2, widen)
     mid_buf[pl.ds(base, 2)] = pong[pl.ds(base, 2)]
-    each(0, 8 * REACH, take_in)
     step(mid_buf, ping, 1)
     rest_of_phase()
 
@@ -549,7 +619,13 @@
     mesh_ref[1] = total[8:]
     for copy in stores:
         copy.wait()
-    each(0, tile_count, lambda d: parcel(d).wait_send())
+    each(0, 7 * SIDE, lambda n: parcel(n // SIDE, lax.rem(n, SIDE), tile, 0).wait_send())
+    for kind in (7, 8):
+        each(0, SIDE, lambda y: parcel(kind, y, tile, 0).wait_send())
+    for up in (True, False):
+        for far in (False, True):
+            for chunk in range(2):
+                hop(up, far, chunk).wait_send()
 
 
 def whole(tile_count, patches, prior, blocks, row, want, flows, valid, stiffness, *fixed):
@@ -562,6 +638,8 @@
     images = pltpu.VMEM((BATCH * P_SIZE, LANES), f32)
     parcels = pltpu.VMEM((tile_count, CAP * WIRE, LANES), bf16)
     near = pltpu.VMEM((GZ, 8, columns), f32)
+    patches_held = pltpu.VMEM((BATCH, WIRE, LANES), bf16)
+    listed = 24
     return pl.pallas_call(
         functools.partial(whole_kernel, tile_count),
         out_shape=(
@@ -586,11 +664,15 @@
             pltpu.VMEM((2, 16, columns), bf16),
             pltpu.VMEM((GZ, 16, columns), bf16),
             pltpu.VMEM((2 * REACH + 1, GZ, 16, columns), bf16),
-            pltpu.VMEM((8 * tile_count, LANES), i32),
-            pltpu.VMEM((8 * tile_count, LANES), i32),
-            pltpu.VMEM((tile_count, LANES), i32),
+            patches_held,
+            patches_held,
+            patches_held,
+            patches_held,
             pltpu.VMEM((8, LANES), i32),
-            pltpu.SMEM((tile_count, LANES), i32),
+            pltpu.VMEM((8 * listed, LANES), i32),
+            pltpu.VMEM((listed, LANES), i32),
+            pltpu.VMEM((8, LANES), i32),
+            pltpu.SMEM((listed, LANES), i32),
             pltpu.SMEM((8, LANES), i32),
             pltpu.VMEM((8, columns), f32),
             near,
@@ -601,14 +683,17 @@
             pltpu.VMEM((rows, 8, columns), f32),
             pltpu.VMEM((2, rows, 8, columns), f32),
             pltpu.VMEM((rows, 8, columns), f32),
+            pltpu.VMEM((rows // 2, 16, columns), bf16),
+            pltpu.VMEM((16, columns), bf16),
             near,
             near,
             dma(7),
         ]
-        + [dma(tile_count)] * 2
+        + [dma(SIDE * (2 * STEPS + 1))] * 2
         + [dma(GZ - 1)] * 2
         + [dma(2 * REACH)] * 2
-        + [dma(tile_count)] * 2
+        + [dma(8)] * 2
+        + [dma(SIDE * len(KINDS))] * 2
         + [dma(GZ - 1)] * 2
         + [dma(2 * REACH)] * 2
         + [dma(8 * REACH)] * 2

time: 147 us -> 143 us (0.973)
  Pallas kernels: 143 us -> 139 us
    pallas_call x1, Pallas kernels: 143 us -> 139 us  [whole(): pl.pallas_call(functools.partial(whole_kernel, tile_count), out_shape=(ja...]
where the time goes in v8:
time: 143 us
  Pallas kernels  139 us (97%)
  local copies, waits for them, and re-layouts  3.31 us (2%)
    pallas_call x1, Pallas kernels, whole(): pl.pallas_call(functools.partial(whole_kernel, tile_count), out_shape=(ja...  139 us
    unnamed x4, local copies, waits for them, and re-layouts  3.31 us

profile of v8, /device:TPU:33, one launch (start us, length us, event | category | flops | bytes accessed | tf_op | source)
XLA Modules:
  0.0 143.3 jit_solution(2790249776018985261)
XLA Ops:
  0.6 139.4 %shard_map.131 = (bf16[32,25600]{1,0:T(8,128)(2,1)}, f32[2,8,256]{2,1,0:T(8,128)}) custom-call(bf16[1,16,25600]{2,1,0:T(8,128)(2,1)} %patch_ref.1, bf16[16,25600]{1,0:T(8,128)(2,1)} %prior_ref.1, bf16[1,32,25600]{2,1,0:T(8,128)(2,1)} %block_ref.1, s32[1,32]{1,0:T(1,128)} %bitcast.5, s32[1,32]{1,0:T(1,128)} %want_ref.1, f32[1,2,8,256]{3,2,1,0:T(8,128)} %flow_ref.1, ...), custom_call_target="tpu_custom_call" | custom-call | flops 30000001024 | bytes 32000000 | tf_op jit(solution)/shard_map/pallas_call | solution.py:643
  140.0 0.0 copy-start
  140.0 2.7 %copy.16 = bf16[1,32,25600]{2,1,0:T(8,128)(2,1)} copy(bf16[1,32,25600]{2,1,0:T(8,128)(2,1)} %bitcast.3) | data formatting | bytes 3276800
  142.7 0.0 copy-done
  142.7 0.6 copy.17
Async XLA Ops:
  140.0 2.7 %copy-start = (f32[2,8,256]{2,1,0:T(8,128)S(1)}, f32[2,8,256]{2,1,0:T(8,128)}, u32[]{:S(2)}) copy-start(f32[2,8,256]{2,1,0:T(8,128)} %get-tuple-element.5) | copy-start | bytes 49156

commit v9 on v8

--- a/solution.py
+++ b/solution.py
@@ -229,8 +229,8 @@
 
 
 SIDE = 4
-STEPS = 2
-KINDS = ((0, 0), (-1, 0), (1, 0), (-2, 0), (2, 0), (-2, 1), (2, -1), (-2, 2), (2, -2))
+STEPS = 3
+KINDS = ((0, 0), (-1, 0), (1, 0), (-1, 1), (1, -1), (-1, 2), (1, -2), (-1, 3), (1, -3))
 
 
 FRONT = 32
@@ -240,7 +240,7 @@
 def whole_kernel(
     tile_count, patch_ref, prior_ref, block_ref, row_ref, want_ref, flow_ref, valid_ref, stiff_ref, first_ref,
     second_ref, third_ref, fourth_ref, map_ref, mesh_ref, rows_buf, block_buf, low_buf, high_buf, wire_buf, send_buf,
-    arrived_buf, spec_buf, field_buf, map_buf, slot_peak, peak_buf, own_buf, held, window_buf, near_up, far_up, near_down, far_down, ask_buf, heard_buf,
+    arrived_buf, spec_buf, field_buf, map_buf, slot_peak, peak_buf, own_buf, held, window_buf, near_up, near_down, ask_buf, heard_buf,
     list_buf, index_buf, told_smem, index_smem, conf_own, conf_held, conf_pack, conf_window, s_buf, w_buf, f_buf, u_buf,
     mid_buf, mid_wire, mid_own, spread_own, spread_held, local, send_r, recv_r, send_a, recv_a, send_b, recv_b, send_h, recv_h, send_p,
     recv_p, send_c, recv_c, send_d, recv_d, send_m, recv_m, send_s, recv_s,
@@ -351,14 +351,10 @@
     patch_batch(low_buf, high_buf, first_ref, second_ref, wire_buf)
     told.wait()
 
-    def hop(up, far, chunk):
-        near, end = (near_up, far_up) if up else (near_down, far_down)
-        batch = pl.ds(BATCH // 2 * chunk, BATCH // 2)
-        number = 4 * int(up) + 2 * int(far) + chunk
+    def hop(up):
         return pltpu.make_async_remote_copy(
-            src_ref=(near if far else wire_buf).at[batch], dst_ref=(end if far else near).at[batch],
-            send_sem=send_h.at[number], recv_sem=recv_h.at[number],
-            device_id=(gz, tile_at(1 if up else -1, spot_in_plane)), device_id_type=MESH,
+            src_ref=wire_buf, dst_ref=near_up if up else near_down, send_sem=send_h.at[int(up)],
+            recv_sem=recv_h.at[int(up)], device_id=(gz, tile_at(1 if up else -1, spot_in_plane)), device_id_type=MESH,
         )
 
     def parcel(kind, y_to, source, landing):
@@ -387,9 +383,8 @@
 
         each(0, SIDE, one)
 
-    for chunk in range(2):
-        for up in (True, False):
-            hop(up, False, chunk).start()
+    for up in (True, False):
+        hop(up).start()
     post(0, wire_buf)
     for buf in (w_buf, f_buf, u_buf, mid_buf):
         buf[...] = jnp.zeros_like(buf)
@@ -398,16 +393,11 @@
     for half in range(2):
         batch = pl.ds(BATCH * half, BATCH)
         to_images(block_buf.at[batch], low_buf, high_buf)
-        if half == 0:
-            for up in (True, False):
-                hop(up, False, 0).wait_recv()
-                hop(up, True, 0).start()
         block_batch(low_buf, high_buf, first_ref, second_ref, spec_buf.at[batch])
     for up in (True, False):
-        hop(up, False, 1).wait_recv()
-        hop(up, True, 1).start()
-    post(1, near_up)
-    post(2, near_down)
+        hop(up).wait_recv()
+    for kind in (1, 2, 3, 4, 5, 6, 7, 8):
+        post(kind, near_up if kind % 2 else near_down)
     index.wait()
     mine.wait()
     for copy in springs:
@@ -437,13 +427,7 @@
             for c in range(CAP):
                 match_slot(source, c)
 
-    each(0, 2, match)
-    for chunk in range(2):
-        for up in (True, False):
-            hop(up, True, chunk).wait_recv()
-    for kind, held_patches in ((7, far_up), (8, far_down), (5, far_up), (6, far_down), (3, far_up), (4, far_down)):
-        post(kind, held_patches)
-    each(2, 14, match)
+    each(0, 14, match)
 
     def match_halfway(n):
         pairs = []
@@ -623,9 +607,7 @@
     for kind in (7, 8):
         each(0, SIDE, lambda y: parcel(kind, y, tile, 0).wait_send())
     for up in (True, False):
-        for far in (False, True):
-            for chunk in range(2):
-                hop(up, far, chunk).wait_send()
+        hop(up).wait_send()
 
 
 def whole(tile_count, patches, prior, blocks, row, want, flows, valid, stiffness, *fixed):
@@ -639,7 +621,7 @@
     parcels = pltpu.VMEM((tile_count, CAP * WIRE, LANES), bf16)
     near = pltpu.VMEM((GZ, 8, columns), f32)
     patches_held = pltpu.VMEM((BATCH, WIRE, LANES), bf16)
-    listed = 24
+    listed = 32
     return pl.pallas_call(
         functools.partial(whole_kernel, tile_count),
         out_shape=(
@@ -666,8 +648,6 @@
             pltpu.VMEM((2 * REACH + 1, GZ, 16, columns), bf16),
             patches_held,
             patches_held,
-            patches_held,
-            patches_held,
             pltpu.VMEM((8, LANES), i32),
             pltpu.VMEM((8 * listed, LANES), i32),
             pltpu.VMEM((listed, LANES), i32),
@@ -692,7 +672,7 @@
         + [dma(SIDE * (2 * STEPS + 1))] * 2
         + [dma(GZ - 1)] * 2
         + [dma(2 * REACH)] * 2
-        + [dma(8)] * 2
+        + [dma(2)] * 2
         + [dma(SIDE * len(KINDS))] * 2
         + [dma(GZ - 1)] * 2
         + [dma(2 * REACH)] * 2

time: 143 us -> 139 us (0.972)
  Pallas kernels: 139 us -> 135 us
    pallas_call x1, Pallas kernels: 139 us -> 135 us  [whole(): pl.pallas_call(functools.partial(whole_kernel, tile_count), out_shape=(ja...]
where the time goes in v9:
time: 139 us
  Pallas kernels  135 us (97%)
  local copies, waits for them, and re-layouts  3.31 us (2%)
    pallas_call x1, Pallas kernels, whole(): pl.pallas_call(functools.partial(whole_kernel, tile_count), out_shape=(ja...  135 us
    unnamed x4, local copies, waits for them, and re-layouts  3.31 us

profile of v9, /device:TPU:33, one launch (start us, length us, event | category | flops | bytes accessed | tf_op | source)
XLA Modules:
  0.0 139.3 jit_solution(12296986261601975654)
XLA Ops:
  0.6 135.3 %shard_map.131 = (bf16[32,25600]{1,0:T(8,128)(2,1)}, f32[2,8,256]{2,1,0:T(8,128)}) custom-call(bf16[1,16,25600]{2,1,0:T(8,128)(2,1)} %patch_ref.1, bf16[16,25600]{1,0:T(8,128)(2,1)} %prior_ref.1, bf16[1,32,25600]{2,1,0:T(8,128)(2,1)} %block_ref.1, s32[1,32]{1,0:T(1,128)} %bitcast.5, s32[1,32]{1,0:T(1,128)} %want_ref.1, f32[1,2,8,256]{3,2,1,0:T(8,128)} %flow_ref.1, ...), custom_call_target="tpu_custom_call" | custom-call | flops 30000001024 | bytes 32000000 | tf_op jit(solution)/shard_map/pallas_call | solution.py:625
  136.0 0.0 copy-start
  136.0 2.7 %copy.16 = bf16[1,32,25600]{2,1,0:T(8,128)(2,1)} copy(bf16[1,32,25600]{2,1,0:T(8,128)(2,1)} %bitcast.3) | data formatting | bytes 3276800
  138.7 0.0 copy-done
  138.7 0.6 copy.17
Async XLA Ops:
  136.0 2.7 %copy-start = (f32[2,8,256]{2,1,0:T(8,128)S(1)}, f32[2,8,256]{2,1,0:T(8,128)}, u32[]{:S(2)}) copy-start(f32[2,8,256]{2,1,0:T(8,128)} %get-tuple-element.5) | copy-start | bytes 49156
